TPU v7x, 256 devices: a whole 4x4x8 slice. The times are simulated.
256 devices in a mesh: grp: 16 (over z, core), dev: 16 (over x, y).
Axes of the slice: x: 4, y: 4, z: 8, core: 2. Of those that a mesh axis runs over, the one named last changes fastest.
Arguments:
- fields: float32 [6, 64, 32, 32, 128], P(None, None, 'grp', 'dev'), may hold values from 0.14 to 7
- speeds: float32 [3, 2, 32, 32, 128], P(None, None, 'grp', 'dev'), may hold values from -1.5 to 1.5, as said below
- sharpen: float32 [64, 64], replicated, may hold values from -0.75 to 0.75
- mat_count: int32 [32, 32, 128], P('grp', 'dev'), may hold values from 1 to 6, as said below
Outputs:
- remapped: float32 [6, 64, 32, 32, 128], P(None, None, 'grp', 'dev')
Inputs may be any that keep to these rules, and one draw needn't show every extreme that they name: `speeds`: the upper-face speed of an element along a direction equals the lower-face speed of the next element along it, periodically. `mat_count`: an element with 2 or more materials is mixed.
All inputs are finite; a program needn't handle non-finite values.
Results may differ from a plain program's by a relative error of at most 0.0001.
Values sent between devices are 32-bit elements; how exact they have to be, the bound alone decides.
No kernel may reach another device: no remote copies, remote signals or barrier semaphores. Data moves between devices by JAX's collectives and lax.ppermute only.
A program may use at most 64 MiB of HBM per device.

v0:
```python
import functools

import jax
import jax.numpy as jnp
import numpy as np
from jax import lax
from jax.experimental import pallas as pl
from jax.experimental.pallas import tpu as pltpu
from jax.sharding import PartitionSpec as P

DT = 0.08
LIFT = 6.0
NODE = (3, 4, 4, 4, 8, 128)
ROW = (6, 32, 8, 128)
FACE = 24
EXT = 3
STEP = {"dev": 1, "grp": 2}
LIMIT = 48 * 1024 * 1024


def gll_derivative():
    points = np.array([-1.0, -1.0 / np.sqrt(5.0), 1.0 / np.sqrt(5.0), 1.0])
    products = np.array(
        [
            np.prod([points[first] - points[second] for second in range(4) if second != first])
            for first in range(4)
        ]
    )
    matrix = np.zeros((4, 4))
    for first in range(4):
        for second in range(4):
            if first != second:
                matrix[first, second] = (
                    products[first] / products[second] / (points[first] - points[second])
                )
        matrix[first, first] = sum(
            (1.0 / (points[first] - points[other]) for other in range(4) if other != first)
        )
    return matrix


D = gll_derivative()
EVEN = [float(D[r, 0] + D[r, 3]) / 2 for r in (0, 1)]
ODD = [(float(D[r, 0] - D[r, 3]) / 2, float(D[r, 1] - D[r, 2]) / 2) for r in (0, 1)]


def roll(x, shift, axis):
    size = x.shape[axis]
    return pltpu.roll(x, shift % size, axis)


def sublane(shape):
    return lax.broadcasted_iota(jnp.int32, shape, len(shape) - 2)


def bit(shape, step):
    return (sublane(shape) & step) != 0


def even_device(axis):
    return lax.rem(lax.axis_index(axis), 2) == 0


def coefficients(speeds_ref):
    out = []
    low_half = sublane((8, 128)) < 4
    for d in range(3):
        v = speeds_ref[pl.ds(8 * d, 8), :]
        w = roll(v, 4, 0)
        a = jnp.where(low_half, v, w)
        b = jnp.where(low_half, w, v)
        c = 0.5 * (a + b)
        out.append(
            (
                -DT * c,
                (-DT * LIFT) * (c - jnp.minimum(a, 0.0)),
                (DT * LIFT) * jnp.maximum(a, 0.0),
                (-DT * LIFT) * (jnp.maximum(b, 0.0) - c),
                (-DT * LIFT) * jnp.minimum(b, 0.0),
            )
        )
    return out


def line(q, c):
    t = c * ((q[0] + q[3]) - (q[1] + q[2]))
    o0 = c * (q[0] - q[3])
    o1 = c * (q[1] - q[2])
    e = [EVEN[r] * t for r in (0, 1)]
    o = [ODD[r][0] * o0 + ODD[r][1] * o1 for r in (0, 1)]
    return [e[0] + o[0], e[1] + o[1], o[1] - e[1], o[0] - e[0]]


def with_faces(q, coef, dn, up):
    c, low, low_in, high, high_in = coef
    r = line(q, c)
    r[0] = r[0] + (low * q[0] + low_in * dn)
    r[3] = r[3] + (high * q[3] + high_in * up)
    return r


def beside(low, high, halo_dn, halo_up, step):
    upper = bit(low.shape, step)
    dn = jnp.where(upper, roll(high, step, low.ndim - 2), halo_dn)
    up = jnp.where(upper, halo_up, roll(low, -step, low.ndim - 2))
    return dn, up


def pack_high(a, b, step):
    return jnp.where(bit(a.shape, step), b, roll(a, -step, a.ndim - 2))


def pack_low(a, b, step):
    return jnp.where(bit(a.shape, step), roll(a, step, a.ndim - 2), b)


def unpack_dn(m, second, step):
    return roll(m, -step, m.ndim - 2) if second else m


def unpack_up(m, second, step):
    return roll(m, step, m.ndim - 2) if second else m


def tendency(q_ref, acc_ref, p, coef, halo_y, halo_z, finish):
    for k in range(4):
        qx = [q_ref[p, k, :, i] for i in range(4)]
        rx = with_faces(qx, coef[0], roll(qx[3], 1, 2), roll(qx[0], -1, 2))
        for i in range(4):
            acc_ref[p, k, :, i] = rx[i]
        qy = [q_ref[p, k, j] for j in range(4)]
        dn, up = beside(qy[0], qy[3], *halo_y(p, k), 1)
        ry = with_faces(qy, coef[1], dn, up)
        for j in range(4):
            acc_ref[p, k, j] = acc_ref[p, k, j] + ry[j]
    for j in range(4):
        qz = [q_ref[p, k, j] for k in range(4)]
        dn, up = beside(qz[0], qz[3], *halo_z(p, j), 2)
        rz = with_faces(qz, coef[2], dn, up)
        for k in range(4):
            finish(p, k, j, qz[k], acc_ref[p, k, j] + rz[k])


def put_messages(q_ref, p, messages):
    outs = {"dev": messages[:2], "grp": messages[2:]}
    for axis in ("dev", "grp"):
        step = STEP[axis]
        even = even_device(axis)
        first, second = outs[axis]
        for half in range(2):
            m = 2 * half
            if axis == "dev":
                low = [q_ref[p, m, 0], q_ref[p, m + 1, 0]]
                high = [q_ref[p, m, 3], q_ref[p, m + 1, 3]]
            else:
                low = [q_ref[p, 0, m], q_ref[p, 0, m + 1]]
                high = [q_ref[p, 3, m], q_ref[p, 3, m + 1]]
            to_next = pack_high(high[0], high[1], step)
            to_last = pack_low(low[0], low[1], step)
            at = pl.ds(8 * p + 4 * half, 4)
            first[at] = jnp.where(even, to_next, to_last)
            second[at] = jnp.where(even, to_last, to_next)


def halo_reader(first, second, axis):
    step = STEP[axis]
    even = even_device(axis)

    def read(p, plane):
        at = pl.ds(8 * p + 4 * (plane // 2), 4)
        x, y = first[at], second[at]
        dn = unpack_dn(jnp.where(even, y, x), plane % 2, step)
        up = unpack_up(jnp.where(even, x, y), plane % 2, step)
        return dn, up

    return read


def open_kernel(fields_ref, q_ref, ext_ref, *messages):
    low_half = sublane((8, 128)) < 4

    def pair(p, carry):
        tops, bottoms = [], []
        for k in range(4):
            for j in range(4):
                for h in range(2):
                    m = 8 * k + 2 * j + h
                    a = fields_ref[2 * p, m]
                    b = fields_ref[2 * p + 1, m]
                    x = jnp.where(low_half, a, roll(b, 4, 0))
                    y = jnp.where(low_half, roll(a, 4, 0), b)
                    q_ref[p, k, j, 2 * h] = x
                    q_ref[p, k, j, 2 * h + 1] = y
                    tops.append(jnp.maximum(x, y))
                    bottoms.append(jnp.minimum(x, y))
        while len(tops) > 1:
            tops = [jnp.maximum(x, y) for x, y in zip(tops[::2], tops[1::2])]
            bottoms = [jnp.minimum(x, y) for x, y in zip(bottoms[::2], bottoms[1::2])]
        ext_ref[0, p] = tops[0]
        ext_ref[1, p] = bottoms[0]
        put_messages(q_ref, p, messages)
        outs = {"dev": messages[:2], "grp": messages[2:]}
        for axis in ("dev", "grp"):
            even = even_device(axis)
            to_next = pack_high(tops[0], bottoms[0], STEP[axis])
            to_last = pack_low(tops[0], bottoms[0], STEP[axis])
            first, second = outs[axis]
            first[FACE + p] = jnp.where(even, to_next, to_last)
            second[FACE + p] = jnp.where(even, to_last, to_next)
        return carry

    lax.fori_loop(0, 3, pair, 0)


def bounds(ext_ref, messages, p):
    top, bottom = ext_ref[0, p], ext_ref[1, p]
    upper = jnp.maximum(top, jnp.maximum(roll(top, 1, 1), roll(top, -1, 1)))
    lower = jnp.minimum(bottom, jnp.minimum(roll(bottom, 1, 1), roll(bottom, -1, 1)))
    outs = {"dev": messages[:2], "grp": messages[2:]}
    for axis in ("dev", "grp"):
        step = STEP[axis]
        even = even_device(axis)
        first, second = outs[axis]
        x, y = first[FACE + p], second[FACE + p]
        from_last = jnp.where(even, y, x)
        from_next = jnp.where(even, x, y)
        for second_half, combine in ((0, jnp.maximum), (1, jnp.minimum)):
            own = (top, bottom)[second_half]
            dn, up = beside(
                own,
                own,
                unpack_dn(from_last, second_half, step),
                unpack_up(from_next, second_half, step),
                step,
            )
            if second_half == 0:
                upper = jnp.maximum(upper, jnp.maximum(dn, up))
            else:
                lower = jnp.minimum(lower, jnp.minimum(dn, up))
    return upper, lower


def first_kernel(q_ref, speeds_ref, ext_ref, *refs):
    got, (s_ref, limit_ref), messages = refs[:4], refs[4:6], refs[6:]
    coef = coefficients(speeds_ref)
    halo_y = halo_reader(got[0], got[1], "dev")
    halo_z = halo_reader(got[2], got[3], "grp")

    def finish(p, k, j, q, t):
        s_ref[p, k, j] = q + t

    def pair(p, carry):
        tendency(q_ref, s_ref, p, coef, halo_y, halo_z, finish)
        put_messages(s_ref, p, messages)
        upper, lower = bounds(ext_ref, got, p)
        limit_ref[0, p] = upper
        limit_ref[1, p] = lower
        return carry

    lax.fori_loop(0, 3, pair, 0)


def second_kernel(q_ref, s_ref, speeds_ref, *refs):
    got, out_ref, messages = refs[:4], refs[4], refs[5:]
    coef = coefficients(speeds_ref)
    halo_y = halo_reader(got[0], got[1], "dev")
    halo_z = halo_reader(got[2], got[3], "grp")

    def finish(p, k, j, s, t):
        out_ref[p, k, j] = 0.75 * q_ref[p, k, j] + 0.25 * (s + t)

    def pair(p, carry):
        tendency(s_ref, out_ref, p, coef, halo_y, halo_z, finish)
        put_messages(out_ref, p, messages)
        return carry

    lax.fori_loop(0, 3, pair, 0)


def operator_kernel(sharpen_ref, high_ref, low_ref):
    s = sharpen_ref[...]
    high = s.astype(jnp.bfloat16)
    low = (s - high.astype(jnp.float32)).astype(jnp.bfloat16)
    rows = lax.broadcasted_iota(jnp.int32, (256, 64), 0)
    cols = lax.broadcasted_iota(jnp.int32, (256, 64), 1)
    tall = (rows // 4 == cols).astype(jnp.bfloat16)
    rows = lax.broadcasted_iota(jnp.int32, (64, 256), 0)
    cols = lax.broadcasted_iota(jnp.int32, (64, 256), 1)
    wide = (cols // 4 == rows).astype(jnp.bfloat16)
    rows = lax.broadcasted_iota(jnp.int32, (256, 256), 0)
    cols = lax.broadcasted_iota(jnp.int32, (256, 256), 1)
    same = (rows & 3) == (cols & 3)
    for part, ref in ((high, high_ref), (low, low_ref)):
        half = jnp.dot(tall, part, preferred_element_type=jnp.float32).astype(jnp.bfloat16)
        full = jnp.dot(half, wide, preferred_element_type=jnp.float32)
        ref[...] = jnp.where(same, full, 0.0).astype(jnp.bfloat16)


def last_kernel(q_ref, s_ref, speeds_ref, limit_ref, count_ref, high_ref, low_ref, *refs):
    got, out_ref, acc_ref, off_ref = refs[:4], refs[4], refs[5], refs[6]
    coef = coefficients(speeds_ref)
    halo_y = halo_reader(got[0], got[1], "dev")
    halo_z = halo_reader(got[2], got[3], "grp")
    low_half = sublane((8, 128)) < 4

    def finish(p, k, j, s, t):
        acc_ref[p, k, j] = q_ref[p, k, j] * (1.0 / 3.0) + (2.0 / 3.0) * (s + t)

    def pair(p, carry):
        tendency(s_ref, acc_ref, p, coef, halo_y, halo_z, finish)
        return carry

    lax.fori_loop(0, 3, pair, 0)

    counts = count_ref[...].astype(jnp.float32)
    counts = jnp.concatenate([counts, counts], axis=0)
    present = [(counts > float(f)).astype(jnp.float32) for f in range(6)]
    share = 1.0 / counts

    def node_pair(k, carry):
        for j in range(4):
            for h in range(2):
                m = 8 * k + 2 * j + h
                rows = []
                for p in range(3):
                    x = acc_ref[p, k, j, 2 * h]
                    y = acc_ref[p, k, j, 2 * h + 1]
                    rows.append(jnp.where(low_half, x, roll(y, 4, 0)))
                    rows.append(jnp.where(low_half, roll(x, 4, 0), y))
                mean = rows[0] * present[0]
                for f in range(1, 6):
                    mean = mean + rows[f] * present[f]
                mean = mean * share
                for f in range(6):
                    out_ref[f, m] = rows[f]
                    off_ref[f, m] = (rows[f] - mean) * present[f]
        return carry

    lax.fori_loop(0, 4, node_pair, 0)

    high, low = high_ref[...], low_ref[...]
    for p in range(3):
        off = jnp.concatenate(
            [off_ref[2 * p].reshape(256, 128), off_ref[2 * p + 1].reshape(256, 128)], axis=1
        )
        off_high = off.astype(jnp.bfloat16)
        off_low = (off - off_high.astype(jnp.float32)).astype(jnp.bfloat16)
        fix = jnp.dot(high, off_high, preferred_element_type=jnp.float32)
        fix = fix + jnp.dot(high, off_low, preferred_element_type=jnp.float32)
        fix = fix + jnp.dot(low, off_high, preferred_element_type=jnp.float32)
        upper, lower = limit_ref[0, p], limit_ref[1, p]
        for h in range(2):
            u, v = roll(upper, 4, 0), roll(lower, 4, 0)
            if h == 0:
                u, v = jnp.where(low_half, upper, u), jnp.where(low_half, lower, v)
            else:
                u, v = jnp.where(low_half, u, upper), jnp.where(low_half, v, lower)
            f = 2 * p + h
            value = out_ref[f] + fix[:, 128 * h : 128 * h + 128].reshape(32, 8, 128)
            out_ref[f] = jnp.minimum(jnp.maximum(value, v), u)


def call(kernel, outs, args, scratch=(), flops=5_000_000):
    return pl.pallas_call(
        kernel,
        out_shape=[jax.ShapeDtypeStruct(*o) for o in outs],
        in_specs=[pl.BlockSpec(memory_space=pltpu.VMEM)] * len(args),
        out_specs=[pl.BlockSpec(memory_space=pltpu.VMEM)] * len(outs),
        scratch_shapes=[pltpu.VMEM(*s) for s in scratch],
        compiler_params=pltpu.CompilerParams(vmem_limit_bytes=LIMIT),
        cost_estimate=pl.CostEstimate(flops=flops, bytes_accessed=2_000_000, transcendentals=0),
    )(*args)


EVEN_PAIRS = [(i, i ^ 1) for i in range(16)]
ODD_PAIRS = [((i + 1) % 16, ((i ^ 1) + 1) % 16) for i in range(16)]


def exchange(messages):
    ways = (("dev", EVEN_PAIRS), ("dev", ODD_PAIRS), ("grp", EVEN_PAIRS), ("grp", ODD_PAIRS))
    return [lax.ppermute(m, axis, pairs) for m, (axis, pairs) in zip(messages, ways)]


def shards(fields, speeds, sharpen, mat_count):
    f32, bf16 = jnp.float32, jnp.bfloat16
    rows = fields.reshape(ROW)
    speeds = speeds.reshape(24, 128)
    counts = mat_count.reshape(4, 128)
    face = ((FACE, 8, 128), f32)
    face_ext = ((FACE + EXT, 8, 128), f32)
    ext = ((2, 3, 8, 128), f32)
    high, low = call(operator_kernel, [((256, 256), bf16)] * 2, [sharpen])
    q, extremes, *messages = call(open_kernel, [(NODE, f32), ext] + [face_ext] * 4, [rows])
    got = exchange(messages)
    s, limits, *messages = call(
        first_kernel, [(NODE, f32), ext] + [face] * 4, [q, speeds, extremes, *got]
    )
    got = exchange(messages)
    s, *messages = call(second_kernel, [(NODE, f32)] + [face] * 4, [q, s, speeds, *got])
    got = exchange(messages)
    (out,) = call(
        last_kernel,
        [(ROW, f32)],
        [q, s, speeds, limits, counts, high, low, *got],
        scratch=[(NODE, f32), (ROW, f32)],
    )
    return out.reshape(fields.shape)


def solution(mesh):
    in_specs = (
        P(None, None, "grp", "dev", None),
        P(None, None, "grp", "dev", None),
        P(),
        P("grp", "dev", None),
    )
    out_specs = P(None, None, "grp", "dev", None)
    return jax.shard_map(shards, mesh=mesh, in_specs=in_specs, out_specs=out_specs, check_vma=False)
```

profile of v0, /device:TPU:0, one launch (start us, length us, event | category | flops | bytes accessed | tf_op | source)
XLA Modules:
  0.0 38.3 jit_solution(12273752017061926377)
XLA Ops:
  0.0 0.0 copy-start
  0.0 1.1 %copy-done = f32[6,64,2,2,128]{4,3,2,1,0:T(2,128)S(1)} copy-done((f32[6,64,2,2,128]{4,3,2,1,0:T(2,128)S(1)}, f32[6,64,2,2,128]{4,3,2,1,0:T(2,128)}, u32[]{:S(2)}) %copy-start) | copy-done | bytes 786456
  1.1 0.2 shard_map.46
  1.3 0.0 copy-start.1
  1.3 0.1 collective-permute-start
  1.4 4.2 %collective-permute-start.1 = (f32[27,8,128]{2,1,0:T(8,128)S(1)}, f32[27,8,128]{2,1,0:T(8,128)S(1)}, u32[]{:S(2)}, u32[]{:S(2)}) collective-permute-start(f32[27,8,128]{2,1,0:T(8,128)S(1)} %get-tuple-element.27), channel_id=1, source_target_pairs={{1,2},{2,1},{3,4},{4,3},{5,6},{6,5},{7,8},{8,7},{9,10},{10,9},{11,... | collective-permute-start | bytes 331784 | tf_op jit(solution)/shard_map/ppermute | solution.py:381
  5.7 0.0 collective-permute-start.2
  5.7 6.0 %collective-permute-start.3 = (f32[27,8,128]{2,1,0:T(8,128)S(1)}, f32[27,8,128]{2,1,0:T(8,128)S(1)}, u32[]{:S(2)}, u32[]{:S(2)}) collective-permute-start(f32[27,8,128]{2,1,0:T(8,128)S(1)} %get-tuple-element.29), channel_id=1, source_target_pairs={{16,32},{32,16},{48,64},{64,48},{80,96},{96,80},{112,128},{128,112... | collective-permute-start | bytes 331784 | tf_op jit(solution)/shard_map/ppermute | solution.py:381
  11.6 0.0 collective-permute-done.refs_0_
  11.6 0.0 collective-permute-done.1.refs_1_
  11.6 0.0 collective-permute-done.2.refs_2_
  11.6 2.4 %collective-permute-done.3.refs_3_ = f32[27,8,128]{2,1,0:T(8,128)S(1)} collective-permute-done((f32[27,8,128]{2,1,0:T(8,128)S(1)}, f32[27,8,128]{2,1,0:T(8,128)S(1)}, u32[]{:S(2)}, u32[]{:S(2)}) %collective-permute-start.3) | collective-permute-done | bytes 110624 | tf_op jit(solution)/shard_map/ppermute | solution.py:381
  14.1 0.0 copy-done.1
  14.1 0.9 %shard_map.47 = (f32[3,4,4,4,8,128]{5,4,3,2,1,0:T(8,128)S(1)}, f32[2,3,8,128]{3,2,1,0:T(8,128)S(1)}, f32[24,8,128]{2,1,0:T(8,128)S(1)}, f32[24,8,128]{2,1,0:T(8,...) custom-call(f32[3,4,4,4,8,128]{5,4,3,2,1,0:T(8,128)S(1)} %get-tuple-element.24.q_ref, ...), custom_call_target="tpu_custom_call" | custom-call | flops 5000000 | bytes 2000000 | tf_op jit(solution)/shard_map/pallas_call | solution.py:364
  15.0 0.1 collective-permute-start.4
  15.1 1.3 %collective-permute-start.5 = (f32[24,8,128]{2,1,0:T(8,128)S(1)}, f32[24,8,128]{2,1,0:T(8,128)S(1)}, u32[]{:S(2)}, u32[]{:S(2)}) collective-permute-start(f32[24,8,128]{2,1,0:T(8,128)S(1)} %get-tuple-element.32), channel_id=1, source_target_pairs={{1,2},{2,1},{3,4},{4,3},{5,6},{6,5},{7,8},{8,7},{9,10},{10,9},{11,... | collective-permute-start | bytes 294920 | tf_op jit(solution)/shard_map/ppermute | solution.py:381
  16.3 0.0 collective-permute-start.6
  16.3 4.5 %collective-permute-start.7 = (f32[24,8,128]{2,1,0:T(8,128)S(1)}, f32[24,8,128]{2,1,0:T(8,128)S(1)}, u32[]{:S(2)}, u32[]{:S(2)}) collective-permute-start(f32[24,8,128]{2,1,0:T(8,128)S(1)} %get-tuple-element.34), channel_id=1, source_target_pairs={{16,32},{32,16},{48,64},{64,48},{80,96},{96,80},{112,128},{128,112... | collective-permute-start | bytes 294920 | tf_op jit(solution)/shard_map/ppermute | solution.py:381
  20.8 0.0 collective-permute-done.4.refs_0_
  20.8 2.3 %collective-permute-done.5.refs_1_ = f32[24,8,128]{2,1,0:T(8,128)S(1)} collective-permute-done((f32[24,8,128]{2,1,0:T(8,128)S(1)}, f32[24,8,128]{2,1,0:T(8,128)S(1)}, u32[]{:S(2)}, u32[]{:S(2)}) %collective-permute-start.5) | collective-permute-done | bytes 98336 | tf_op jit(solution)/shard_map/ppermute | solution.py:381
  23.1 0.0 collective-permute-done.6.refs_2_
  23.1 0.0 collective-permute-done.7.refs_3_
  23.1 0.0 copy-start.2
  23.1 0.9 %shard_map.48 = (f32[3,4,4,4,8,128]{5,4,3,2,1,0:T(8,128)S(1)}, f32[24,8,128]{2,1,0:T(8,128)S(1)}, f32[24,8,128]{2,1,0:T(8,128)S(1)}, f32[24,8,128]{2,1,0:T(8,128)S(1)}, f32[24,8,128]{2,1,0:T(8,128)S(1)}) custom-call(f32[3,4,4,4,8,128]{5,4,3,2,1,0:T(8,128)S(1)} %get-tuple-element.24.q_ref, f32[3,4,4,4,8,128]{5,4,3,2,1,0:T(8,128)S(1)} %get-tuple-element.30.s_ref, ...), custom_call_target="tpu_custom_call" | custom-call | flops 5000000 | bytes 2000000 | tf_op jit(solution)/shard_map/pallas_call | solution.py:364
  24.0 0.1 collective-permute-start.10
  24.1 3.0 %collective-permute-start.11 = (f32[24,8,128]{2,1,0:T(8,128)S(1)}, f32[24,8,128]{2,1,0:T(8,128)S(1)}, u32[]{:S(2)}, u32[]{:S(2)}) collective-permute-start(f32[24,8,128]{2,1,0:T(8,128)S(1)} %get-tuple-element.42), channel_id=1, source_target_pairs={{16,32},{32,16},{48,64},{64,48},{80,96},{96,80},{112,128},{128,112... | collective-permute-start | bytes 294920 | tf_op jit(solution)/shard_map/ppermute | solution.py:381
  27.2 0.0 collective-permute-start.8
  27.2 2.6 %collective-permute-start.9 = (f32[24,8,128]{2,1,0:T(8,128)S(1)}, f32[24,8,128]{2,1,0:T(8,128)S(1)}, u32[]{:S(2)}, u32[]{:S(2)}) collective-permute-start(f32[24,8,128]{2,1,0:T(8,128)S(1)} %get-tuple-element.40), channel_id=1, source_target_pairs={{1,2},{2,1},{3,4},{4,3},{5,6},{6,5},{7,8},{8,7},{9,10},{10,9},{11,... | collective-permute-start | bytes 294920 | tf_op jit(solution)/shard_map/ppermute | solution.py:381
  29.8 0.0 copy-done.2
  29.8 0.3 shard_map.49
  30.1 0.0 collective-permute-done.10.refs_2_
  30.1 0.0 collective-permute-done.11.refs_3_
  30.1 1.7 %collective-permute-done.8.refs_0_ = f32[24,8,128]{2,1,0:T(8,128)S(1)} collective-permute-done((f32[24,8,128]{2,1,0:T(8,128)S(1)}, f32[24,8,128]{2,1,0:T(8,128)S(1)}, u32[]{:S(2)}, u32[]{:S(2)}) %collective-permute-start.8) | collective-permute-done | bytes 98336 | tf_op jit(solution)/shard_map/ppermute | solution.py:381
  31.8 3.3 %collective-permute-done.9.refs_1_ = f32[24,8,128]{2,1,0:T(8,128)S(1)} collective-permute-done((f32[24,8,128]{2,1,0:T(8,128)S(1)}, f32[24,8,128]{2,1,0:T(8,128)S(1)}, u32[]{:S(2)}, u32[]{:S(2)}) %collective-permute-start.9) | collective-permute-done | bytes 98336 | tf_op jit(solution)/shard_map/ppermute | solution.py:381
  35.1 0.0 copy-start.3
  35.1 0.7 %copy-done.3 = s32[2,2,128]{2,1,0:T(2,128)S(1)} copy-done((s32[2,2,128]{2,1,0:T(2,128)S(1)}, s32[2,2,128]{2,1,0:T(2,128)}, u32[]{:S(2)}) %copy-start.3) | copy-done | bytes 2072
  35.8 2.5 %shard_map.50 = f32[6,32,8,128]{3,2,1,0:T(8,128)} custom-call(f32[3,4,4,4,8,128]{5,4,3,2,1,0:T(8,128)S(1)} %get-tuple-element.24.q_ref, f32[3,4,4,4,8,128]{5,4,3,2,1,0:T(8,128)S(1)} %get-tuple-element.35.s_ref, f32[24,128]{1,0:T(8,128)S(1)} %bitcast.7, f32[2,3,8,128]{3,2,1,0:T(8,128)S(1)} %get-tuple-element.36.limit_ref, s32[4,128]{1,0:T(4,128)S(1)} %bitcast.8, ...), custom_call_target="tpu_custom_call" | custom-call | flops 5000000 | bytes 2000000 | tf_op jit(solution)/shard_map/pallas_call | solution.py:364
Async XLA Ops:
  0.0 1.1 %copy-start = (f32[6,64,2,2,128]{4,3,2,1,0:T(2,128)S(1)}, f32[6,64,2,2,128]{4,3,2,1,0:T(2,128)}, u32[]{:S(2)}) copy-start(f32[6,64,2,2,128]{4,3,2,1,0:T(2,128)} %param.4) | copy-start | bytes 2359300
  1.3 12.7 %copy-start.1 = (f32[3,2,2,2,128]{4,3,2,1,0:T(2,128)S(1)}, f32[3,2,2,2,128]{4,3,2,1,0:T(2,128)}, u32[]{:S(2)}) copy-start(f32[3,2,2,2,128]{4,3,2,1,0:T(2,128)} %param.5) | copy-start | bytes 36868
  1.3 10.3 %collective-permute-start = (f32[27,8,128]{2,1,0:T(8,128)S(1)}, f32[27,8,128]{2,1,0:T(8,128)S(1)}, u32[]{:S(2)}, u32[]{:S(2)}) collective-permute-start(f32[27,8,128]{2,1,0:T(8,128)S(1)} %get-tuple-element.26), channel_id=1, source_target_pairs={{0,1},{1,0},{2,3},{3,2},{4,5},{5,4},{6,7},{7,6},{8,9},{9,8},{10,11... | collective-permute-start | bytes 331784 | tf_op jit(solution)/shard_map/ppermute | solution.py:381
  1.4 10.2 %collective-permute-start.1 = (f32[27,8,128]{2,1,0:T(8,128)S(1)}, f32[27,8,128]{2,1,0:T(8,128)S(1)}, u32[]{:S(2)}, u32[]{:S(2)}) collective-permute-start(f32[27,8,128]{2,1,0:T(8,128)S(1)} %get-tuple-element.27), channel_id=1, source_target_pairs={{1,2},{2,1},{3,4},{4,3},{5,6},{6,5},{7,8},{8,7},{9,10},{10,9},{11,... | collective-permute-start | bytes 331784 | tf_op jit(solution)/shard_map/ppermute | solution.py:381
  5.7 6.0 %collective-permute-start.2 = (f32[27,8,128]{2,1,0:T(8,128)S(1)}, f32[27,8,128]{2,1,0:T(8,128)S(1)}, u32[]{:S(2)}, u32[]{:S(2)}) collective-permute-start(f32[27,8,128]{2,1,0:T(8,128)S(1)} %get-tuple-element.28), channel_id=1, source_target_pairs={{0,16},{16,0},{32,48},{48,32},{64,80},{80,64},{96,112},{112,96},{1... | collective-permute-start | bytes 331784 | tf_op jit(solution)/shard_map/ppermute | solution.py:381
  5.7 8.4 %collective-permute-start.3 = (f32[27,8,128]{2,1,0:T(8,128)S(1)}, f32[27,8,128]{2,1,0:T(8,128)S(1)}, u32[]{:S(2)}, u32[]{:S(2)}) collective-permute-start(f32[27,8,128]{2,1,0:T(8,128)S(1)} %get-tuple-element.29), channel_id=1, source_target_pairs={{16,32},{32,16},{48,64},{64,48},{80,96},{96,80},{112,128},{128,112... | collective-permute-start | bytes 331784 | tf_op jit(solution)/shard_map/ppermute | solution.py:381
  15.0 5.8 %collective-permute-start.4 = (f32[24,8,128]{2,1,0:T(8,128)S(1)}, f32[24,8,128]{2,1,0:T(8,128)S(1)}, u32[]{:S(2)}, u32[]{:S(2)}) collective-permute-start(f32[24,8,128]{2,1,0:T(8,128)S(1)} %get-tuple-element.31), channel_id=1, source_target_pairs={{0,1},{1,0},{2,3},{3,2},{4,5},{5,4},{6,7},{7,6},{8,9},{9,8},{10,11... | collective-permute-start | bytes 294920 | tf_op jit(solution)/shard_map/ppermute | solution.py:381
  15.1 8.0 %collective-permute-start.5 = (f32[24,8,128]{2,1,0:T(8,128)S(1)}, f32[24,8,128]{2,1,0:T(8,128)S(1)}, u32[]{:S(2)}, u32[]{:S(2)}) collective-permute-start(f32[24,8,128]{2,1,0:T(8,128)S(1)} %get-tuple-element.32), channel_id=1, source_target_pairs={{1,2},{2,1},{3,4},{4,3},{5,6},{6,5},{7,8},{8,7},{9,10},{10,9},{11,... | collective-permute-start | bytes 294920 | tf_op jit(solution)/shard_map/ppermute | solution.py:381
  16.3 6.8 %collective-permute-start.6 = (f32[24,8,128]{2,1,0:T(8,128)S(1)}, f32[24,8,128]{2,1,0:T(8,128)S(1)}, u32[]{:S(2)}, u32[]{:S(2)}) collective-permute-start(f32[24,8,128]{2,1,0:T(8,128)S(1)} %get-tuple-element.33), channel_id=1, source_target_pairs={{0,16},{16,0},{32,48},{48,32},{64,80},{80,64},{96,112},{112,96},{1... | collective-permute-start | bytes 294920 | tf_op jit(solution)/shard_map/ppermute | solution.py:381
  16.3 6.8 %collective-permute-start.7 = (f32[24,8,128]{2,1,0:T(8,128)S(1)}, f32[24,8,128]{2,1,0:T(8,128)S(1)}, u32[]{:S(2)}, u32[]{:S(2)}) collective-permute-start(f32[24,8,128]{2,1,0:T(8,128)S(1)} %get-tuple-element.34), channel_id=1, source_target_pairs={{16,32},{32,16},{48,64},{64,48},{80,96},{96,80},{112,128},{128,112... | collective-permute-start | bytes 294920 | tf_op jit(solution)/shard_map/ppermute | solution.py:381
  23.1 6.7 %copy-start.2 = (f32[64,64]{1,0:T(8,128)S(1)}, f32[64,64]{1,0:T(8,128)}, u32[]{:S(2)}) copy-start(f32[64,64]{1,0:T(8,128)} %sharpen_ref.1) | copy-start | bytes 49156
  24.0 6.1 %collective-permute-start.10 = (f32[24,8,128]{2,1,0:T(8,128)S(1)}, f32[24,8,128]{2,1,0:T(8,128)S(1)}, u32[]{:S(2)}, u32[]{:S(2)}) collective-permute-start(f32[24,8,128]{2,1,0:T(8,128)S(1)} %get-tuple-element.41), channel_id=1, source_target_pairs={{0,16},{16,0},{32,48},{48,32},{64,80},{80,64},{96,112},{112,96},{1... | collective-permute-start | bytes 294920 | tf_op jit(solution)/shard_map/ppermute | solution.py:381
  24.1 6.0 %collective-permute-start.11 = (f32[24,8,128]{2,1,0:T(8,128)S(1)}, f32[24,8,128]{2,1,0:T(8,128)S(1)}, u32[]{:S(2)}, u32[]{:S(2)}) collective-permute-start(f32[24,8,128]{2,1,0:T(8,128)S(1)} %get-tuple-element.42), channel_id=1, source_target_pairs={{16,32},{32,16},{48,64},{64,48},{80,96},{96,80},{112,128},{128,112... | collective-permute-start | bytes 294920 | tf_op jit(solution)/shard_map/ppermute | solution.py:381
  27.2 4.6 %collective-permute-start.8 = (f32[24,8,128]{2,1,0:T(8,128)S(1)}, f32[24,8,128]{2,1,0:T(8,128)S(1)}, u32[]{:S(2)}, u32[]{:S(2)}) collective-permute-start(f32[24,8,128]{2,1,0:T(8,128)S(1)} %get-tuple-element.39), channel_id=1, source_target_pairs={{0,1},{1,0},{2,3},{3,2},{4,5},{5,4},{6,7},{7,6},{8,9},{9,8},{10,11... | collective-permute-start | bytes 294920 | tf_op jit(solution)/shard_map/ppermute | solution.py:381
  27.2 7.9 %collective-permute-start.9 = (f32[24,8,128]{2,1,0:T(8,128)S(1)}, f32[24,8,128]{2,1,0:T(8,128)S(1)}, u32[]{:S(2)}, u32[]{:S(2)}) collective-permute-start(f32[24,8,128]{2,1,0:T(8,128)S(1)} %get-tuple-element.40), channel_id=1, source_target_pairs={{1,2},{2,1},{3,4},{4,3},{5,6},{6,5},{7,8},{8,7},{9,10},{10,9},{11,... | collective-permute-start | bytes 294920 | tf_op jit(solution)/shard_map/ppermute | solution.py:381
  35.1 0.7 %copy-start.3 = (s32[2,2,128]{2,1,0:T(2,128)S(1)}, s32[2,2,128]{2,1,0:T(2,128)}, u32[]{:S(2)}) copy-start(s32[2,2,128]{2,1,0:T(2,128)} %param.7) | copy-start | bytes 6148
where the time goes:
time: 38.4 us; the launch traced here: 38.3 us
  starting transfers between devices  21.8 us (57%)
  waiting for transfers between devices  9.71 us (25%)
  Pallas kernels  4.81 us (13%)
  local copies, waits for them, and re-layouts  1.82 us (5%)
    ppermute x12, starting transfers between devices, exchange(): lax.ppermute(m, axis, pairs)  21.8 us
    ppermute x12, waiting for transfers between devices, exchange(): lax.ppermute(m, axis, pairs)  9.71 us
    pallas_call x5, Pallas kernels, call(): pl.pallas_call(kernel, out_shape=[jax.ShapeDtypeStruct(*o) for o in outs]...  4.81 us
    unnamed x8, local copies, waits for them, and re-layouts  1.82 us
  transfers between devices with their start and end apart: 12, of which 4 were waited for; matrix products, arithmetic and copies ran while one was open for 0% of the time, Pallas kernels for 1%

commit v1 on v0

--- a/solution.py
+++ b/solution.py
@@ -13,7 +13,8 @@
 NODE = (3, 4, 4, 4, 8, 128)
 ROW = (6, 32, 8, 128)
 FACE = 24
-EXT = 3
+EXT = 2 * FACE
+COEF = EXT + 3
 STEP = {"dev": 1, "grp": 2}
 LIMIT = 48 * 1024 * 1024
 
@@ -77,9 +78,16 @@
                 (DT * LIFT) * jnp.maximum(a, 0.0),
                 (-DT * LIFT) * (jnp.maximum(b, 0.0) - c),
                 (-DT * LIFT) * jnp.minimum(b, 0.0),
+                (-DT * LIFT) * jnp.minimum(a, 0.0),
+                (DT * LIFT) * jnp.maximum(b, 0.0),
             )
         )
     return out
+
+
+def rim_coefficients(coef, step):
+    upper = bit((8, 128), step)
+    return jnp.where(upper, coef[4], coef[2]), jnp.where(upper, coef[6], coef[5])
 
 
 def line(q, c):
@@ -92,7 +100,7 @@
 
 
 def with_faces(q, coef, dn, up):
-    c, low, low_in, high, high_in = coef
+    c, low, low_in, high, high_in = coef[:5]
     r = line(q, c)
     r[0] = r[0] + (low * q[0] + low_in * dn)
     r[3] = r[3] + (high * q[3] + high_in * up)
@@ -141,45 +149,94 @@
             finish(p, k, j, qz[k], acc_ref[p, k, j] + rz[k])
 
 
-def put_messages(q_ref, p, messages):
-    outs = {"dev": messages[:2], "grp": messages[2:]}
-    for axis in ("dev", "grp"):
+AXES = ("dev", "grp")
+
+
+def put(messages, axis, at, to_next, to_last):
+    even = even_device(axis)
+    second, first = messages[2 * AXES.index(axis) :][:2]
+    first[at] = jnp.where(even, to_next, to_last)
+    second[at] = jnp.where(even, to_last, to_next)
+
+
+def get(messages, axis, at):
+    even = even_device(axis)
+    second, first = messages[2 * AXES.index(axis) :][:2]
+    x, y = first[at], second[at]
+    return jnp.where(even, y, x), jnp.where(even, x, y)
+
+
+def get_single(messages, axis, at, second):
+    last, after = get(messages, axis, at)
+    step = STEP[axis]
+    return unpack_dn(last, second, step), unpack_up(after, second, step)
+
+
+def face(q_ref, p, axis, side, plane):
+    return q_ref[p, plane, side] if axis == "dev" else q_ref[p, side, plane]
+
+
+def put_faces(q_ref, p, messages, base):
+    for axis in AXES:
         step = STEP[axis]
-        even = even_device(axis)
-        first, second = outs[axis]
         for half in range(2):
             m = 2 * half
-            if axis == "dev":
-                low = [q_ref[p, m, 0], q_ref[p, m + 1, 0]]
-                high = [q_ref[p, m, 3], q_ref[p, m + 1, 3]]
-            else:
-                low = [q_ref[p, 0, m], q_ref[p, 0, m + 1]]
-                high = [q_ref[p, 3, m], q_ref[p, 3, m + 1]]
-            to_next = pack_high(high[0], high[1], step)
-            to_last = pack_low(low[0], low[1], step)
-            at = pl.ds(8 * p + 4 * half, 4)
-            first[at] = jnp.where(even, to_next, to_last)
-            second[at] = jnp.where(even, to_last, to_next)
-
-
-def halo_reader(first, second, axis):
-    step = STEP[axis]
-    even = even_device(axis)
-
-    def read(p, plane):
-        at = pl.ds(8 * p + 4 * (plane // 2), 4)
-        x, y = first[at], second[at]
-        dn = unpack_dn(jnp.where(even, y, x), plane % 2, step)
-        up = unpack_up(jnp.where(even, x, y), plane % 2, step)
-        return dn, up
-
-    return read
-
-
-def open_kernel(fields_ref, q_ref, ext_ref, *messages):
+            low = [face(q_ref, p, axis, 0, m + h) for h in range(2)]
+            high = [face(q_ref, p, axis, 3, m + h) for h in range(2)]
+            put(
+                messages,
+                axis,
+                pl.ds(base + 8 * p + 4 * half, 4),
+                pack_high(high[0], high[1], step),
+                pack_low(low[0], low[1], step),
+            )
+
+
+def get_face(messages, axis, p, plane, base):
+    at = pl.ds(base + 8 * p + 4 * (plane // 2), 4)
+    return get_single(messages, axis, at, plane % 2)
+
+
+def no_halo(p, plane):
+    zero = jnp.zeros((4, 8, 128), jnp.float32)
+    return zero, zero
+
+
+def open_kernel(fields_hbm, speeds_hbm, count_hbm, *refs):
+    q_ref, s_ref, ext_ref, wide_count_ref, speeds_ref = refs[:5]
+    messages, (fields_ref, count_ref, sems) = refs[5:9], refs[9:]
+    copies = [
+        pltpu.make_async_copy(speeds_hbm, speeds_ref, sems.at[3]),
+        pltpu.make_async_copy(count_hbm, count_ref, sems.at[4]),
+    ]
+
+    def part(p):
+        at = pl.ds(2 * p, 2)
+        return pltpu.make_async_copy(fields_hbm.at[at], fields_ref.at[at], sems.at[p])
+
+    for copy in copies + [part(p) for p in range(3)]:
+        copy.start()
+    for copy in copies:
+        copy.wait()
     low_half = sublane((8, 128)) < 4
+    coef = coefficients(speeds_ref)
+    counts = count_ref[...].astype(jnp.float32)
+    wide_count_ref[...] = jnp.concatenate([counts, counts], axis=0)
+    for axis, d in (("dev", 2), ("grp", 1)):
+        pair = rim_coefficients(coef[d], STEP[AXES[d - 1]])
+        put(
+            messages,
+            axis,
+            COEF,
+            pack_high(pair[0], pair[1], STEP[axis]),
+            pack_low(pair[0], pair[1], STEP[axis]),
+        )
+
+    def finish(p, k, j, q, t):
+        s_ref[p, k, j] = q + t
 
     def pair(p, carry):
+        part(p).wait()
         tops, bottoms = [], []
         for k in range(4):
             for j in range(4):
@@ -198,15 +255,17 @@
             bottoms = [jnp.minimum(x, y) for x, y in zip(bottoms[::2], bottoms[1::2])]
         ext_ref[0, p] = tops[0]
         ext_ref[1, p] = bottoms[0]
-        put_messages(q_ref, p, messages)
-        outs = {"dev": messages[:2], "grp": messages[2:]}
-        for axis in ("dev", "grp"):
-            even = even_device(axis)
-            to_next = pack_high(tops[0], bottoms[0], STEP[axis])
-            to_last = pack_low(tops[0], bottoms[0], STEP[axis])
-            first, second = outs[axis]
-            first[FACE + p] = jnp.where(even, to_next, to_last)
-            second[FACE + p] = jnp.where(even, to_last, to_next)
+        for axis in AXES:
+            put(
+                messages,
+                axis,
+                EXT + p,
+                pack_high(tops[0], bottoms[0], STEP[axis]),
+                pack_low(tops[0], bottoms[0], STEP[axis]),
+            )
+        put_faces(q_ref, p, messages, 0)
+        tendency(q_ref, s_ref, p, coef, no_halo, no_halo, finish)
+        put_faces(s_ref, p, messages, FACE)
         return carry
 
     lax.fori_loop(0, 3, pair, 0)
@@ -216,62 +275,76 @@
     top, bottom = ext_ref[0, p], ext_ref[1, p]
     upper = jnp.maximum(top, jnp.maximum(roll(top, 1, 1), roll(top, -1, 1)))
     lower = jnp.minimum(bottom, jnp.minimum(roll(bottom, 1, 1), roll(bottom, -1, 1)))
-    outs = {"dev": messages[:2], "grp": messages[2:]}
-    for axis in ("dev", "grp"):
-        step = STEP[axis]
-        even = even_device(axis)
-        first, second = outs[axis]
-        x, y = first[FACE + p], second[FACE + p]
-        from_last = jnp.where(even, y, x)
-        from_next = jnp.where(even, x, y)
-        for second_half, combine in ((0, jnp.maximum), (1, jnp.minimum)):
-            own = (top, bottom)[second_half]
-            dn, up = beside(
-                own,
-                own,
-                unpack_dn(from_last, second_half, step),
-                unpack_up(from_next, second_half, step),
-                step,
-            )
-            if second_half == 0:
-                upper = jnp.maximum(upper, jnp.maximum(dn, up))
-            else:
-                lower = jnp.minimum(lower, jnp.minimum(dn, up))
+    for axis in AXES:
+        dn, up = beside(top, top, *get_single(messages, axis, EXT + p, 0), STEP[axis])
+        upper = jnp.maximum(upper, jnp.maximum(dn, up))
+        dn, up = beside(bottom, bottom, *get_single(messages, axis, EXT + p, 1), STEP[axis])
+        lower = jnp.minimum(lower, jnp.minimum(dn, up))
     return upper, lower
 
 
-def first_kernel(q_ref, speeds_ref, ext_ref, *refs):
-    got, (s_ref, limit_ref), messages = refs[:4], refs[4:6], refs[6:]
+def outer(pair, step):
+    return jnp.where(bit(pair[0].shape, step), pair[1], pair[0])
+
+
+def first_kernel(q_ref, part_ref, speeds_ref, ext_ref, *refs):
+    got, (out_ref, limit_ref, corner_ref, weight_ref) = refs[:4], refs[4:8]
+    messages, s_ref = refs[8:12], refs[12]
     coef = coefficients(speeds_ref)
-    halo_y = halo_reader(got[0], got[1], "dev")
-    halo_z = halo_reader(got[2], got[3], "grp")
-
-    def finish(p, k, j, q, t):
-        s_ref[p, k, j] = q + t
+    in_y, to_y = rim_coefficients(coef[1], 1)
+    in_z, to_z = rim_coefficients(coef[2], 2)
+    in_zn, to_zn = [outer(get_single(got, "dev", COEF, h), 1) for h in range(2)]
+    in_ym, to_ym = [outer(get_single(got, "grp", COEF, h), 2) for h in range(2)]
+    weight_ref[...] = 0.25 * (in_y * in_zn + in_z * in_ym)
+    weight_n = 0.25 * (to_y * in_z + in_zn * to_ym)
+    weight_m = 0.25 * (to_z * in_y + in_ym * to_zn)
+    high_y, high_z = bit((8, 128), 1), bit((8, 128), 2)
+    y_in = [jnp.where(high_y, 0.0, in_y), jnp.where(high_y, in_y, 0.0)]
+    z_in = [jnp.where(high_z, 0.0, in_z), jnp.where(high_z, in_z, 0.0)]
+
+    def halo_y(p, k):
+        dn, up = get_face(got, "dev", p, k, FACE)
+        return dn + to_y * q_ref[p, k, 0], up + to_y * q_ref[p, k, 3]
+
+    def halo_z(p, j):
+        dn, up = get_face(got, "grp", p, j, FACE)
+        return dn + to_z * q_ref[p, 0, j], up + to_z * q_ref[p, 3, j]
+
+    def finish(p, k, j, s, t):
+        out_ref[p, k, j] = 0.75 * q_ref[p, k, j] + 0.25 * (s + t)
 
     def pair(p, carry):
-        tendency(q_ref, s_ref, p, coef, halo_y, halo_z, finish)
-        put_messages(s_ref, p, messages)
+        edges_y, edges_z = {}, {}
+        for k in range(4):
+            dn, up = get_face(got, "dev", p, k, 0)
+            s_ref[p, k, 0] = part_ref[p, k, 0] + y_in[0] * dn
+            s_ref[p, k, 1] = part_ref[p, k, 1]
+            s_ref[p, k, 2] = part_ref[p, k, 2]
+            s_ref[p, k, 3] = part_ref[p, k, 3] + y_in[1] * up
+            if k in (0, 3):
+                edges_y[k] = outer((dn, up), 1)
+        for j in range(4):
+            dn, up = get_face(got, "grp", p, j, 0)
+            s_ref[p, 0, j] = s_ref[p, 0, j] + z_in[0] * dn
+            s_ref[p, 3, j] = s_ref[p, 3, j] + z_in[1] * up
+            if j in (0, 3):
+                edges_z[j] = outer((dn, up), 2)
+        edge_n = jnp.where(high_z, edges_y[3], edges_y[0])
+        edge_m = jnp.where(high_y, edges_z[3], edges_z[0])
+        corner_ref[0, p] = weight_n * edge_m
+        corner_ref[1, p] = weight_m * edge_n
+        put(
+            messages,
+            "dev",
+            pl.ds(FACE + 2 * p, 2),
+            pack_high(edge_m[:2], edge_m[2:], 1),
+            pack_low(edge_m[:2], edge_m[2:], 1),
+        )
+        tendency(s_ref, out_ref, p, coef, halo_y, halo_z, finish)
+        put_faces(out_ref, p, messages, 0)
         upper, lower = bounds(ext_ref, got, p)
         limit_ref[0, p] = upper
         limit_ref[1, p] = lower
-        return carry
-
-    lax.fori_loop(0, 3, pair, 0)
-
-
-def second_kernel(q_ref, s_ref, speeds_ref, *refs):
-    got, out_ref, messages = refs[:4], refs[4], refs[5:]
-    coef = coefficients(speeds_ref)
-    halo_y = halo_reader(got[0], got[1], "dev")
-    halo_z = halo_reader(got[2], got[3], "grp")
-
-    def finish(p, k, j, s, t):
-        out_ref[p, k, j] = 0.75 * q_ref[p, k, j] + 0.25 * (s + t)
-
-    def pair(p, carry):
-        tendency(s_ref, out_ref, p, coef, halo_y, halo_z, finish)
-        put_messages(out_ref, p, messages)
         return carry
 
     lax.fori_loop(0, 3, pair, 0)
@@ -296,24 +369,56 @@
         ref[...] = jnp.where(same, full, 0.0).astype(jnp.bfloat16)
 
 
-def last_kernel(q_ref, s_ref, speeds_ref, limit_ref, count_ref, high_ref, low_ref, *refs):
-    got, out_ref, acc_ref, off_ref = refs[:4], refs[4], refs[5], refs[6]
+def last_kernel(
+    q_ref, part_ref, speeds_ref, limit_ref, corner_ref, weight_ref, count_ref, high_ref, low_ref, *refs
+):
+    got, out_hbm, (s_ref, acc_ref, off_ref, out_ref, sems) = refs[:4], refs[4], refs[5:]
+
+    def part(p):
+        at = pl.ds(2 * p, 2)
+        return pltpu.make_async_copy(out_ref.at[at], out_hbm.at[at], sems.at[p])
+
     coef = coefficients(speeds_ref)
-    halo_y = halo_reader(got[0], got[1], "dev")
-    halo_z = halo_reader(got[2], got[3], "grp")
     low_half = sublane((8, 128)) < 4
+    high_y, high_z = bit((8, 128), 1), bit((8, 128), 2)
+    at_y = {0: jnp.logical_not(high_y), 3: high_y}
+    at_z = {0: jnp.logical_not(high_z), 3: high_z}
+
+    def halo_y(p, k):
+        dn, up = get_face(got, "dev", p, k, 0)
+        if k in at_z:
+            more = jnp.where(at_z[k], corner_ref[0, p], 0.0)
+            dn, up = dn + more, up + more
+        return dn, up
+
+    def halo_z(p, j):
+        dn, up = get_face(got, "grp", p, j, 0)
+        if j in at_y:
+            more = jnp.where(at_y[j], corner_ref[1, p], 0.0)
+            dn, up = dn + more, up + more
+        return dn, up
 
     def finish(p, k, j, s, t):
         acc_ref[p, k, j] = q_ref[p, k, j] * (1.0 / 3.0) + (2.0 / 3.0) * (s + t)
 
     def pair(p, carry):
+        at = pl.ds(FACE + 2 * p, 2)
+        edge = jnp.concatenate(
+            [outer(get_single(got, "dev", at, h), 1) for h in range(2)], axis=0
+        )
+        edge = weight_ref[...] * edge
+        for k in range(4):
+            for j in range(4):
+                value = part_ref[p, k, j]
+                if k in at_z and j in at_y:
+                    value = value + jnp.where(jnp.logical_and(at_z[k], at_y[j]), edge, 0.0)
+                s_ref[p, k, j] = value
         tendency(s_ref, acc_ref, p, coef, halo_y, halo_z, finish)
         return carry
 
     lax.fori_loop(0, 3, pair, 0)
 
-    counts = count_ref[...].astype(jnp.float32)
-    counts = jnp.concatenate([counts, counts], axis=0)
+    counts = count_ref[...]
     present = [(counts > float(f)).astype(jnp.float32) for f in range(6)]
     share = 1.0 / counts
 
@@ -358,15 +463,18 @@
             f = 2 * p + h
             value = out_ref[f] + fix[:, 128 * h : 128 * h + 128].reshape(32, 8, 128)
             out_ref[f] = jnp.minimum(jnp.maximum(value, v), u)
-
-
-def call(kernel, outs, args, scratch=(), flops=5_000_000):
+        part(p).start()
+    for p in range(3):
+        part(p).wait()
+
+
+def call(kernel, outs, args, scratch=(), flops=5_000_000, space=pltpu.VMEM, out_space=pltpu.VMEM):
     return pl.pallas_call(
         kernel,
         out_shape=[jax.ShapeDtypeStruct(*o) for o in outs],
-        in_specs=[pl.BlockSpec(memory_space=pltpu.VMEM)] * len(args),
-        out_specs=[pl.BlockSpec(memory_space=pltpu.VMEM)] * len(outs),
-        scratch_shapes=[pltpu.VMEM(*s) for s in scratch],
+        in_specs=[pl.BlockSpec(memory_space=space)] * len(args),
+        out_specs=[pl.BlockSpec(memory_space=out_space)] * len(outs),
+        scratch_shapes=[pltpu.VMEM(*s) if isinstance(s, tuple) else s for s in scratch],
         compiler_params=pltpu.CompilerParams(vmem_limit_bytes=LIMIT),
         cost_estimate=pl.CostEstimate(flops=flops, bytes_accessed=2_000_000, transcendentals=0),
     )(*args)
@@ -377,7 +485,7 @@
 
 
 def exchange(messages):
-    ways = (("dev", EVEN_PAIRS), ("dev", ODD_PAIRS), ("grp", EVEN_PAIRS), ("grp", ODD_PAIRS))
+    ways = (("dev", ODD_PAIRS), ("dev", EVEN_PAIRS), ("grp", ODD_PAIRS), ("grp", EVEN_PAIRS))
     return [lax.ppermute(m, axis, pairs) for m, (axis, pairs) in zip(messages, ways)]
 
 
@@ -386,23 +494,31 @@
     rows = fields.reshape(ROW)
     speeds = speeds.reshape(24, 128)
     counts = mat_count.reshape(4, 128)
-    face = ((FACE, 8, 128), f32)
-    face_ext = ((FACE + EXT, 8, 128), f32)
-    ext = ((2, 3, 8, 128), f32)
+    node, one, ext = (NODE, f32), ((8, 128), f32), ((2, 3, 8, 128), f32)
+    corner = ((2, 3, 4, 8, 128), f32)
     high, low = call(operator_kernel, [((256, 256), bf16)] * 2, [sharpen])
-    q, extremes, *messages = call(open_kernel, [(NODE, f32), ext] + [face_ext] * 4, [rows])
-    got = exchange(messages)
-    s, limits, *messages = call(
-        first_kernel, [(NODE, f32), ext] + [face] * 4, [q, speeds, extremes, *got]
+    arguments = [pltpu.with_memory_space_constraint(x, pltpu.HBM) for x in (rows, speeds, counts)]
+    q, s, extremes, counts, speeds, *messages = call(
+        open_kernel,
+        [node, node, ext, one, ((24, 128), f32)] + [((COEF + 1, 8, 128), f32)] * 4,
+        arguments,
+        scratch=[(ROW, f32), ((4, 128), jnp.int32), pltpu.SemaphoreType.DMA((5,))],
+        space=pltpu.HBM,
     )
     got = exchange(messages)
-    s, *messages = call(second_kernel, [(NODE, f32)] + [face] * 4, [q, s, speeds, *got])
+    s, limits, corners, weight, *messages = call(
+        first_kernel,
+        [node, ext, corner, one] + [((FACE + 6, 8, 128), f32)] * 2 + [((FACE, 8, 128), f32)] * 2,
+        [q, s, speeds, extremes, *got],
+        scratch=[node],
+    )
     got = exchange(messages)
     (out,) = call(
         last_kernel,
         [(ROW, f32)],
-        [q, s, speeds, limits, counts, high, low, *got],
-        scratch=[(NODE, f32), (ROW, f32)],
+        [q, s, speeds, limits, corners, weight, counts, high, low, *got],
+        scratch=[node, node, (ROW, f32), (ROW, f32), pltpu.SemaphoreType.DMA((3,))],
+        out_space=pltpu.HBM,
     )
     return out.reshape(fields.shape)
 

time: 38.4 us -> 28.1 us (0.73)
  the two profiles are of different devices: /device:TPU:0 before, /device:TPU:1 now
where the time goes in v1:
time: 28.1 us; the launch traced here: 27.9 us
  starting transfers between devices  20.3 us (72%)
  Pallas kernels  5.88 us (21%)
  waiting for transfers between devices  1.69 us (6%)
    ppermute x8, starting transfers between devices, exchange(): lax.ppermute(m, axis, pairs)  20.3 us
    pallas_call x4, Pallas kernels, call(): pl.pallas_call(kernel, out_shape=[jax.ShapeDtypeStruct(*o) for o in outs]...  5.88 us
    ppermute x8, waiting for transfers between devices, exchange(): lax.ppermute(m, axis, pairs)  1.69 us
  transfers between devices with their start and end apart: 8, of which 3 were waited for; matrix products, arithmetic and copies ran while one was open for 0% of the time, Pallas kernels for 1%

profile of v1, /device:TPU:1, one launch (start us, length us, event | category | flops | bytes accessed | tf_op | source)
XLA Modules:
  0.0 27.9 jit_solution(7317185623579702516)
XLA Ops:
  0.0 2.0 %shard_map.46 = (f32[3,4,4,4,8,128]{5,4,3,2,1,0:T(8,128)S(1)}, f32[3,4,4,4,8,128]{5,4,3,2,1,0:T(8,128)S(1)}, f32[2,3,8,128]{3,2,1,0:T(8,128)S(1)}, f32[8,128]{1,...) custom-call(f32[6,32,8,128]{3,2,1,0:T(8,128)} %bitcast.4, ...), custom_call_target="tpu_custom_call" | custom-call | flops 5000000 | bytes 2000000 | tf_op jit(solution)/shard_map/pallas_call | solution.py:472
  2.0 5.8 %collective-permute-start = (f32[52,8,128]{2,1,0:T(8,128)S(1)}, f32[52,8,128]{2,1,0:T(8,128)S(1)}, u32[]{:S(2)}, u32[]{:S(2)}) collective-permute-start(f32[52,8,128]{2,1,0:T(8,128)S(1)} %get-tuple-element.28), channel_id=1, source_target_pairs={{1,2},{2,1},{3,4},{4,3},{5,6},{6,5},{7,8},{8,7},{9,10},{10,9},{11,... | collective-permute-start | bytes 638984 | tf_op jit(solution)/shard_map/ppermute | solution.py:489
  7.8 0.0 collective-permute-start.1
  7.8 2.5 %collective-permute-start.2 = (f32[52,8,128]{2,1,0:T(8,128)S(1)}, f32[52,8,128]{2,1,0:T(8,128)S(1)}, u32[]{:S(2)}, u32[]{:S(2)}) collective-permute-start(f32[52,8,128]{2,1,0:T(8,128)S(1)} %get-tuple-element.30), channel_id=1, source_target_pairs={{16,32},{32,16},{48,64},{64,48},{80,96},{96,80},{112,128},{128,112... | collective-permute-start | bytes 638984 | tf_op jit(solution)/shard_map/ppermute | solution.py:489
  10.3 3.5 %collective-permute-start.3 = (f32[52,8,128]{2,1,0:T(8,128)S(1)}, f32[52,8,128]{2,1,0:T(8,128)S(1)}, u32[]{:S(2)}, u32[]{:S(2)}) collective-permute-start(f32[52,8,128]{2,1,0:T(8,128)S(1)} %get-tuple-element.31), channel_id=1, source_target_pairs={{0,16},{16,0},{32,48},{48,32},{64,80},{80,64},{96,112},{112,96},{1... | collective-permute-start | bytes 638984 | tf_op jit(solution)/shard_map/ppermute | solution.py:489
  13.8 0.0 collective-permute-done.refs_0_
  13.8 0.0 collective-permute-done.1.refs_1_
  13.8 0.3 %collective-permute-done.2.refs_2_ = f32[52,8,128]{2,1,0:T(8,128)S(1)} collective-permute-done((f32[52,8,128]{2,1,0:T(8,128)S(1)}, f32[52,8,128]{2,1,0:T(8,128)S(1)}, u32[]{:S(2)}, u32[]{:S(2)}) %collective-permute-start.2) | collective-permute-done | bytes 213024 | tf_op jit(solution)/shard_map/ppermute | solution.py:489
  14.1 0.8 %collective-permute-done.3.refs_3_ = f32[52,8,128]{2,1,0:T(8,128)S(1)} collective-permute-done((f32[52,8,128]{2,1,0:T(8,128)S(1)}, f32[52,8,128]{2,1,0:T(8,128)S(1)}, u32[]{:S(2)}, u32[]{:S(2)}) %collective-permute-start.3) | collective-permute-done | bytes 213024 | tf_op jit(solution)/shard_map/ppermute | solution.py:489
  14.9 0.0 copy-start
  14.9 1.1 %shard_map.47 = (f32[3,4,4,4,8,128]{5,4,3,2,1,0:T(8,128)S(1)}, f32[2,3,8,128]{3,2,1,0:T(8,128)S(1)}, f32[2,3,4,8,128]{4,3,2,1,0:T(8,128)S(1)}, f32[8,128]{1,0:T(...) custom-call(f32[3,4,4,4,8,128]{5,4,3,2,1,0:T(8,128)S(1)} %get-tuple-, ...), custom_call_target="tpu_custom_call" | custom-call | flops 5000000 | bytes 2000000 | tf_op jit(solution)/shard_map/pallas_call | solution.py:472
  16.0 2.5 %collective-permute-start.4 = (f32[30,8,128]{2,1,0:T(8,128)S(1)}, f32[30,8,128]{2,1,0:T(8,128)S(1)}, u32[]{:S(2)}, u32[]{:S(2)}) collective-permute-start(f32[30,8,128]{2,1,0:T(8,128)S(1)} %get-tuple-element.39), channel_id=1, source_target_pairs={{1,2},{2,1},{3,4},{4,3},{5,6},{6,5},{7,8},{8,7},{9,10},{10,9},{11,... | collective-permute-start | bytes 368648 | tf_op jit(solution)/shard_map/ppermute | solution.py:489
  18.5 0.0 collective-permute-start.5
  18.5 3.4 %collective-permute-start.6 = (f32[24,8,128]{2,1,0:T(8,128)S(1)}, f32[24,8,128]{2,1,0:T(8,128)S(1)}, u32[]{:S(2)}, u32[]{:S(2)}) collective-permute-start(f32[24,8,128]{2,1,0:T(8,128)S(1)} %get-tuple-element.41), channel_id=1, source_target_pairs={{16,32},{32,16},{48,64},{64,48},{80,96},{96,80},{112,128},{128,112... | collective-permute-start | bytes 294920 | tf_op jit(solution)/shard_map/ppermute | solution.py:489
  21.9 2.6 %collective-permute-start.7 = (f32[24,8,128]{2,1,0:T(8,128)S(1)}, f32[24,8,128]{2,1,0:T(8,128)S(1)}, u32[]{:S(2)}, u32[]{:S(2)}) collective-permute-start(f32[24,8,128]{2,1,0:T(8,128)S(1)} %get-tuple-element.42), channel_id=1, source_target_pairs={{0,16},{16,0},{32,48},{48,32},{64,80},{80,64},{96,112},{112,96},{1... | collective-permute-start | bytes 294920 | tf_op jit(solution)/shard_map/ppermute | solution.py:489
  24.5 0.0 copy-done
  24.5 0.3 %shard_map.48 = (bf16[256,256]{1,0:T(8,128)(2,1)S(1)}, bf16[256,256]{1,0:T(8,128)(2,1)S(1)}) custom-call(f32[64,64]{1,0:T(8,128)S(1)} %copy-done), custom_call_target="tpu_custom_call" | custom-call | flops 5000000 | bytes 2000000 | tf_op jit(solution)/shard_map/pallas_call | solution.py:472
  24.8 0.0 collective-permute-done.6.refs_2_
  24.8 0.6 %collective-permute-done.7.refs_3_ = f32[24,8,128]{2,1,0:T(8,128)S(1)} collective-permute-done((f32[24,8,128]{2,1,0:T(8,128)S(1)}, f32[24,8,128]{2,1,0:T(8,128)S(1)}, u32[]{:S(2)}, u32[]{:S(2)}) %collective-permute-start.7) | collective-permute-done | bytes 98336 | tf_op jit(solution)/shard_map/ppermute | solution.py:489
  25.4 0.0 collective-permute-done.4.refs_0_
  25.4 0.0 collective-permute-done.5.refs_1_
  25.4 2.5 %shard_map.49 = f32[6,32,8,128]{3,2,1,0:T(8,128)} custom-call(f32[3,4,4,4,8,128]{5,4,3,2,1,0:T(8,128)S(1)} %get-tuple-element.24.q_ref, f32[3,4,4,4,8,128]{5,4,3,2,1,0:T(8,128)S(1)} %get-tuple-element.32.part_ref, f32[24,128]{1,0:T(8,128)S(1)} %get-tuple-element.26.speeds_ref, f32[2,3,8,128]{3,2,1,0:T(8,128)S(1)} %get-tuple-element.33.limit_ref, ...), custom_call_target="tpu_custom_call" | custom-call | flops 5000000 | bytes 2000000 | tf_op jit(solution)/shard_map/pallas_call | solution.py:472
Async XLA Ops:
  2.0 11.8 %collective-permute-start = (f32[52,8,128]{2,1,0:T(8,128)S(1)}, f32[52,8,128]{2,1,0:T(8,128)S(1)}, u32[]{:S(2)}, u32[]{:S(2)}) collective-permute-start(f32[52,8,128]{2,1,0:T(8,128)S(1)} %get-tuple-element.28), channel_id=1, source_target_pairs={{1,2},{2,1},{3,4},{4,3},{5,6},{6,5},{7,8},{8,7},{9,10},{10,9},{11,... | collective-permute-start | bytes 638984 | tf_op jit(solution)/shard_map/ppermute | solution.py:489
  7.8 6.0 %collective-permute-start.1 = (f32[52,8,128]{2,1,0:T(8,128)S(1)}, f32[52,8,128]{2,1,0:T(8,128)S(1)}, u32[]{:S(2)}, u32[]{:S(2)}) collective-permute-start(f32[52,8,128]{2,1,0:T(8,128)S(1)} %get-tuple-element.29), channel_id=1, source_target_pairs={{0,1},{1,0},{2,3},{3,2},{4,5},{5,4},{6,7},{7,6},{8,9},{9,8},{10,11... | collective-permute-start | bytes 638984 | tf_op jit(solution)/shard_map/ppermute | solution.py:489
  7.8 6.3 %collective-permute-start.2 = (f32[52,8,128]{2,1,0:T(8,128)S(1)}, f32[52,8,128]{2,1,0:T(8,128)S(1)}, u32[]{:S(2)}, u32[]{:S(2)}) collective-permute-start(f32[52,8,128]{2,1,0:T(8,128)S(1)} %get-tuple-element.30), channel_id=1, source_target_pairs={{16,32},{32,16},{48,64},{64,48},{80,96},{96,80},{112,128},{128,112... | collective-permute-start | bytes 638984 | tf_op jit(solution)/shard_map/ppermute | solution.py:489
  10.3 4.6 %collective-permute-start.3 = (f32[52,8,128]{2,1,0:T(8,128)S(1)}, f32[52,8,128]{2,1,0:T(8,128)S(1)}, u32[]{:S(2)}, u32[]{:S(2)}) collective-permute-start(f32[52,8,128]{2,1,0:T(8,128)S(1)} %get-tuple-element.31), channel_id=1, source_target_pairs={{0,16},{16,0},{32,48},{48,32},{64,80},{80,64},{96,112},{112,96},{1... | collective-permute-start | bytes 638984 | tf_op jit(solution)/shard_map/ppermute | solution.py:489
  14.9 9.6 %copy-start = (f32[64,64]{1,0:T(8,128)S(1)}, f32[64,64]{1,0:T(8,128)}, u32[]{:S(2)}) copy-start(f32[64,64]{1,0:T(8,128)} %sharpen_ref.1) | copy-start | bytes 49156
  16.0 9.4 %collective-permute-start.4 = (f32[30,8,128]{2,1,0:T(8,128)S(1)}, f32[30,8,128]{2,1,0:T(8,128)S(1)}, u32[]{:S(2)}, u32[]{:S(2)}) collective-permute-start(f32[30,8,128]{2,1,0:T(8,128)S(1)} %get-tuple-element.39), channel_id=1, source_target_pairs={{1,2},{2,1},{3,4},{4,3},{5,6},{6,5},{7,8},{8,7},{9,10},{10,9},{11,... | collective-permute-start | bytes 368648 | tf_op jit(solution)/shard_map/ppermute | solution.py:489
  18.5 6.9 %collective-permute-start.5 = (f32[30,8,128]{2,1,0:T(8,128)S(1)}, f32[30,8,128]{2,1,0:T(8,128)S(1)}, u32[]{:S(2)}, u32[]{:S(2)}) collective-permute-start(f32[30,8,128]{2,1,0:T(8,128)S(1)} %get-tuple-element.40), channel_id=1, source_target_pairs={{0,1},{1,0},{2,3},{3,2},{4,5},{5,4},{6,7},{7,6},{8,9},{9,8},{10,11... | collective-permute-start | bytes 368648 | tf_op jit(solution)/shard_map/ppermute | solution.py:489
  18.5 6.3 %collective-permute-start.6 = (f32[24,8,128]{2,1,0:T(8,128)S(1)}, f32[24,8,128]{2,1,0:T(8,128)S(1)}, u32[]{:S(2)}, u32[]{:S(2)}) collective-permute-start(f32[24,8,128]{2,1,0:T(8,128)S(1)} %get-tuple-element.41), channel_id=1, source_target_pairs={{16,32},{32,16},{48,64},{64,48},{80,96},{96,80},{112,128},{128,112... | collective-permute-start | bytes 294920 | tf_op jit(solution)/shard_map/ppermute | solution.py:489
  21.9 3.6 %collective-permute-start.7 = (f32[24,8,128]{2,1,0:T(8,128)S(1)}, f32[24,8,128]{2,1,0:T(8,128)S(1)}, u32[]{:S(2)}, u32[]{:S(2)}) collective-permute-start(f32[24,8,128]{2,1,0:T(8,128)S(1)} %get-tuple-element.42), channel_id=1, source_target_pairs={{0,16},{16,0},{32,48},{48,32},{64,80},{80,64},{96,112},{112,96},{1... | collective-permute-start | bytes 294920 | tf_op jit(solution)/shard_map/ppermute | solution.py:489

commit v2 on v1

v2 whole, which is shorter than its diff:
```python
import functools

import jax
import jax.numpy as jnp
import numpy as np
from jax import lax
from jax.experimental import pallas as pl
from jax.experimental.pallas import tpu as pltpu
from jax.sharding import PartitionSpec as P

DT = 0.08
LIFT = 6.0
NODE = (3, 4, 4, 4, 8, 128)
ROW = (6, 32, 8, 128)
FACE = 24
EXT = 2 * FACE
COEF = EXT + 3
STEP = {"dev": 1, "grp": 2}
LIMIT = 48 * 1024 * 1024


def gll_derivative():
    points = np.array([-1.0, -1.0 / np.sqrt(5.0), 1.0 / np.sqrt(5.0), 1.0])
    products = np.array(
        [
            np.prod([points[first] - points[second] for second in range(4) if second != first])
            for first in range(4)
        ]
    )
    matrix = np.zeros((4, 4))
    for first in range(4):
        for second in range(4):
            if first != second:
                matrix[first, second] = (
                    products[first] / products[second] / (points[first] - points[second])
                )
        matrix[first, first] = sum(
            (1.0 / (points[first] - points[other]) for other in range(4) if other != first)
        )
    return matrix


D = gll_derivative()
SCALE = [float(x) / 2 for x in (D[0, 0] + D[0, 3], D[0, 0] - D[0, 3], D[0, 1] - D[0, 2])]
RATIO = [float(x) / 2 / s for x, s in zip((D[1, 0] + D[1, 3], D[1, 0] - D[1, 3], D[1, 1] - D[1, 2]), SCALE)]


def roll(x, shift, axis):
    size = x.shape[axis]
    return pltpu.roll(x, shift % size, axis)


def sublane(shape):
    return lax.broadcasted_iota(jnp.int32, shape, len(shape) - 2)


def bit(shape, step):
    return (sublane(shape) & step) != 0


def even_device(axis):
    return lax.rem(lax.axis_index(axis), 2) == 0


def coefficients(speeds_ref, factor=1.0):
    out = []
    low_half = sublane((8, 128)) < 4
    for d in range(3):
        v = speeds_ref[pl.ds(8 * d, 8), :]
        w = roll(v, 4, 0)
        a = jnp.where(low_half, v, w)
        b = jnp.where(low_half, w, v)
        c = 0.5 * (a + b)
        dt = DT * factor
        out.append(
            (
                -dt * c,
                (-dt * LIFT) * (c - jnp.minimum(a, 0.0)),
                (dt * LIFT) * jnp.maximum(a, 0.0),
                (-dt * LIFT) * (jnp.maximum(b, 0.0) - c),
                (-dt * LIFT) * jnp.minimum(b, 0.0),
                (-dt * LIFT) * jnp.minimum(a, 0.0),
                (dt * LIFT) * jnp.maximum(b, 0.0),
            )
        )
    return out


def rim_coefficients(coef, step):
    upper = bit((8, 128), step)
    return jnp.where(upper, coef[4], coef[2]), jnp.where(upper, coef[6], coef[5])


def local(coef, step):
    c, low, low_in, high, high_in = coef[:5]
    if step:
        upper = bit((8, 128), step)
        low_in, high_in = jnp.where(upper, low_in, 0.0), jnp.where(upper, 0.0, high_in)
    return [c * s for s in SCALE], low, low_in, high, high_in, step


def line(q, c):
    t = c[0] * ((q[0] + q[3]) - (q[1] + q[2]))
    o0 = c[1] * (q[0] - q[3])
    o1 = c[2] * (q[1] - q[2])
    e = RATIO[0] * t
    o = RATIO[1] * o0 + RATIO[2] * o1
    o0 = o0 + o1
    return [o0 + t, o + e, o - e, o0 - t]


def with_faces(q, coef):
    c, low, low_in, high, high_in, step = coef
    axis = q[0].ndim - 2 if step else q[0].ndim - 1
    step = step if step else 1
    r = line(q, c)
    r[0] = r[0] + (low * q[0] + low_in * roll(q[3], step, axis))
    r[3] = r[3] + (high * q[3] + high_in * roll(q[0], -step, axis))
    return r


def beside(low, high, halo_dn, halo_up, step):
    upper = bit(low.shape, step)
    dn = jnp.where(upper, roll(high, step, low.ndim - 2), halo_dn)
    up = jnp.where(upper, halo_up, roll(low, -step, low.ndim - 2))
    return dn, up


def pack_high(a, b, step):
    return jnp.where(bit(a.shape, step), b, roll(a, -step, a.ndim - 2))


def pack_low(a, b, step):
    return jnp.where(bit(a.shape, step), roll(a, step, a.ndim - 2), b)


def unpack_dn(m, second, step):
    return roll(m, -step, m.ndim - 2) if second else m


def unpack_up(m, second, step):
    return roll(m, step, m.ndim - 2) if second else m


def tendency(q_ref, acc_ref, p, coef, finish):
    along_x, along_y, along_z = [local(coef[d], d) for d in range(3)]
    for k in range(4):
        rx = with_faces([q_ref[p, k, :, i] for i in range(4)], along_x)
        for i in range(4):
            acc_ref[p, k, :, i] = rx[i]
        ry = with_faces([q_ref[p, k, j] for j in range(4)], along_y)
        for j in range(4):
            acc_ref[p, k, j] = acc_ref[p, k, j] + ry[j]
    for j in range(4):
        qz = [q_ref[p, k, j] for k in range(4)]
        rz = with_faces(qz, along_z)
        for k in range(4):
            finish(p, k, j, qz[k], acc_ref[p, k, j] + rz[k])


AXES = ("dev", "grp")
WAYS = (("dev", 1), ("dev", 0), ("grp", 1), ("grp", 0))


def put(messages, axis, at, to_next, to_last):
    even = even_device(axis)
    first, second = [messages[WAYS.index((axis, odd))] for odd in (0, 1)]
    first[at] = jnp.where(even, to_next, to_last)
    second[at] = jnp.where(even, to_last, to_next)


def get(messages, axis, at):
    even = even_device(axis)
    first, second = [messages[WAYS.index((axis, odd))] for odd in (0, 1)]
    x, y = first[at], second[at]
    return jnp.where(even, y, x), jnp.where(even, x, y)


def get_single(messages, axis, at, second):
    last, after = get(messages, axis, at)
    step = STEP[axis]
    return unpack_dn(last, second, step), unpack_up(after, second, step)


def face(q_ref, p, axis, side, plane):
    return q_ref[p, plane, side] if axis == "dev" else q_ref[p, side, plane]


def put_faces(q_ref, p, messages, base):
    for axis in AXES:
        step = STEP[axis]
        for half in range(2):
            m = 2 * half
            low = [face(q_ref, p, axis, 0, m + h) for h in range(2)]
            high = [face(q_ref, p, axis, 3, m + h) for h in range(2)]
            put(
                messages,
                axis,
                pl.ds(base + 8 * p + 4 * half, 4),
                pack_high(high[0], high[1], step),
                pack_low(low[0], low[1], step),
            )


def get_face(messages, axis, p, plane, base):
    at = pl.ds(base + 8 * p + 4 * (plane // 2), 4)
    return get_single(messages, axis, at, plane % 2)


def open_kernel(fields_hbm, speeds_hbm, count_hbm, *refs):
    q_ref, s_ref, ext_ref, wide_count_ref, speeds_ref = refs[:5]
    messages, (fields_ref, count_ref, sems) = refs[5:9], refs[9:]
    copies = [
        pltpu.make_async_copy(speeds_hbm, speeds_ref, sems.at[3]),
        pltpu.make_async_copy(count_hbm, count_ref, sems.at[4]),
    ]

    def part(p):
        at = pl.ds(2 * p, 2)
        return pltpu.make_async_copy(fields_hbm.at[at], fields_ref.at[at], sems.at[p])

    for copy in copies + [part(p) for p in range(3)]:
        copy.start()
    for copy in copies:
        copy.wait()
    low_half = sublane((8, 128)) < 4
    coef = coefficients(speeds_ref)
    counts = count_ref[...].astype(jnp.float32)
    wide_count_ref[...] = jnp.concatenate([counts, counts], axis=0)
    for axis, d in (("dev", 2), ("grp", 1)):
        pair = rim_coefficients(coef[d], STEP[AXES[d - 1]])
        put(
            messages,
            axis,
            COEF,
            pack_high(pair[0], pair[1], STEP[axis]),
            pack_low(pair[0], pair[1], STEP[axis]),
        )

    def finish(p, k, j, q, t):
        s_ref[p, k, j] = q + t

    def pair(p, carry):
        part(p).wait()
        tops, bottoms = [], []
        for k in range(4):
            for j in range(4):
                for h in range(2):
                    m = 8 * k + 2 * j + h
                    a = fields_ref[2 * p, m]
                    b = fields_ref[2 * p + 1, m]
                    x = jnp.where(low_half, a, roll(b, 4, 0))
                    y = jnp.where(low_half, roll(a, 4, 0), b)
                    q_ref[p, k, j, 2 * h] = x
                    q_ref[p, k, j, 2 * h + 1] = y
                    tops.append(jnp.maximum(x, y))
                    bottoms.append(jnp.minimum(x, y))
        while len(tops) > 1:
            tops = [jnp.maximum(x, y) for x, y in zip(tops[::2], tops[1::2])]
            bottoms = [jnp.minimum(x, y) for x, y in zip(bottoms[::2], bottoms[1::2])]
        ext_ref[0, p] = tops[0]
        ext_ref[1, p] = bottoms[0]
        for axis in AXES:
            put(
                messages,
                axis,
                EXT + p,
                pack_high(tops[0], bottoms[0], STEP[axis]),
                pack_low(tops[0], bottoms[0], STEP[axis]),
            )
        put_faces(q_ref, p, messages, 0)
        tendency(q_ref, s_ref, p, coef, finish)
        put_faces(s_ref, p, messages, FACE)
        return carry

    lax.fori_loop(0, 3, pair, 0)


def bounds(ext_ref, messages, p):
    top, bottom = ext_ref[0, p], ext_ref[1, p]
    upper = jnp.maximum(top, jnp.maximum(roll(top, 1, 1), roll(top, -1, 1)))
    lower = jnp.minimum(bottom, jnp.minimum(roll(bottom, 1, 1), roll(bottom, -1, 1)))
    for axis in AXES:
        dn, up = beside(top, top, *get_single(messages, axis, EXT + p, 0), STEP[axis])
        upper = jnp.maximum(upper, jnp.maximum(dn, up))
        dn, up = beside(bottom, bottom, *get_single(messages, axis, EXT + p, 1), STEP[axis])
        lower = jnp.minimum(lower, jnp.minimum(dn, up))
    return upper, lower


def outer(pair, step):
    return jnp.where(bit(pair[0].shape, step), pair[1], pair[0])


def spread(coef, step):
    upper = bit((8, 128), step)
    c, low, _, high = coef[:4]
    out = [c * jnp.where(upper, float(D[n, 3]), float(D[n, 0])) for n in range(4)]
    out[0] = out[0] + jnp.where(upper, 0.0, low)
    out[3] = out[3] + jnp.where(upper, high, 0.0)
    return out


def along_plane(h, along_x, along_t):
    out = with_faces(h, along_t)
    for t in range(4):
        out[t] = out[t] + jnp.stack(with_faces([h[t][i] for i in range(4)], along_x))
    return out


def local_kernel(q_ref, part_ref, speeds_ref, sharpen_ref, out_ref, *operators):
    coef = coefficients(speeds_ref, 0.25)
    build_operators(sharpen_ref, *operators)

    def finish(p, k, j, s, t):
        out_ref[p, k, j] = (0.75 * q_ref[p, k, j] + 0.25 * s) + t

    def pair(p, carry):
        tendency(part_ref, out_ref, p, coef, finish)
        return carry

    lax.fori_loop(0, 3, pair, 0)


def first_kernel(q_ref, base_ref, speeds_ref, *refs):
    got, (out_ref, corner_ref, weight_ref), messages = refs[:4], refs[4:7], refs[7:]
    coef = coefficients(speeds_ref)
    in_y, to_y = rim_coefficients(coef[1], 1)
    in_z, to_z = rim_coefficients(coef[2], 2)
    in_zn, to_zn = [outer(get_single(got, "dev", COEF, h), 1) for h in range(2)]
    in_ym, to_ym = [outer(get_single(got, "grp", COEF, h), 2) for h in range(2)]
    weight_ref[...] = 0.25 * (in_y * in_zn + in_z * in_ym)
    weight_n = 0.25 * (to_y * in_z + in_zn * to_ym)
    weight_m = 0.25 * (to_z * in_y + in_ym * to_zn)
    high_y, high_z = bit((8, 128), 1), bit((8, 128), 2)
    some_y, some_z = 0.25 * in_y, 0.25 * in_z
    along = [local(coef[d], d) for d in range(3)]
    spread_y, spread_z = spread(coef[1], 1), spread(coef[2], 2)

    def pair(p, carry):
        from_n = [outer(get_face(got, "dev", p, k, 0), 1) for k in range(4)]
        from_m = [outer(get_face(got, "grp", p, j, 0), 2) for j in range(4)]
        edge_n = jnp.where(high_z, from_n[3], from_n[0])
        edge_m = jnp.where(high_y, from_m[3], from_m[0])
        corner_ref[0, p] = weight_n * edge_m
        corner_ref[1, p] = weight_m * edge_n
        put(
            messages,
            "dev",
            pl.ds(FACE + 2 * p, 2),
            pack_high(edge_m[:2], edge_m[2:], 1),
            pack_low(edge_m[:2], edge_m[2:], 1),
        )
        hy = [some_y * x for x in from_n]
        hz = [some_z * x for x in from_m]
        plane_y = along_plane(hy, along[0], along[2])
        plane_z = along_plane(hz, along[0], along[1])
        for n in range(4):
            own = jnp.where(high_y, q_ref[p, n, 3], q_ref[p, n, 0])
            ghost = outer(get_face(got, "dev", p, n, FACE), 1) + to_y * own
            plane_y[n] = plane_y[n] + (hy[n] + some_y * ghost)
            own = jnp.where(high_z, q_ref[p, 3, n], q_ref[p, 0, n])
            ghost = outer(get_face(got, "grp", p, n, FACE), 2) + to_z * own
            plane_z[n] = plane_z[n] + (hz[n] + some_z * ghost)
        for k in range(4):
            for j in range(4):
                value = base_ref[p, k, j] + (spread_y[j] * hy[k] + spread_z[k] * hz[j])
                if j in (0, 3):
                    value = value + jnp.where(high_y == (j == 3), plane_y[k], 0.0)
                if k in (0, 3):
                    value = value + jnp.where(high_z == (k == 3), plane_z[j], 0.0)
                out_ref[p, k, j] = value
        put_faces(out_ref, p, messages, 0)
        return carry

    lax.fori_loop(0, 3, pair, 0)


def build_operators(sharpen_ref, high_ref, low_ref, rim_ref, rim_low_ref):
    f32, bf16 = jnp.float32, jnp.bfloat16

    def index(shape, axis):
        return lax.broadcasted_iota(jnp.int32, shape, axis)

    tall = (index((256, 64), 0) // 4 == index((256, 64), 1)).astype(bf16)
    wide = (index((64, 256), 1) // 4 == index((64, 256), 0)).astype(f32)
    node, col = index((64, 128), 0), index((64, 128), 1)
    t, i = (col >> 4) & 3, (col >> 2) & 3
    on_y = 16 * t + 12 * (col & 1) + i
    on_z = 48 * ((col >> 1) & 1) + 4 * t + i
    pick = (node == jnp.where(col < 64, on_y, on_z)).astype(f32)
    wide = jnp.concatenate([wide, pick], axis=1).astype(bf16)
    same = (index((256, 128), 0) & 3) == (index((256, 128), 1) & 3)
    for part, ref in zip(split(sharpen_ref[...]), (high_ref, low_ref)):
        half = jnp.dot(tall, part, preferred_element_type=f32).astype(bf16)
        full = jnp.dot(half, wide, preferred_element_type=f32)
        full = [jnp.where(same, full[:, 128 * n : 128 * n + 128], 0.0).astype(bf16) for n in range(3)]
        ref[...] = jnp.concatenate(full[:2], axis=1)
        if ref is high_ref:
            rim_ref[...] = jnp.concatenate([full[2], full[2]], axis=1)
        else:
            rim_low_ref[...] = full[2]


def split(x):
    high = x.astype(jnp.bfloat16)
    return high, (x - high.astype(jnp.float32)).astype(jnp.bfloat16)


def to_rows(pairs):
    low_half = sublane((8, 128)) < 4
    rows = []
    for x, y in pairs:
        rows.append(jnp.where(low_half, x, roll(y, 4, 0)))
        rows.append(jnp.where(low_half, roll(x, 4, 0), y))
    return rows


def presence(count_ref):
    counts = count_ref[...]
    return [(counts > float(f)).astype(jnp.float32) for f in range(6)], 1.0 / counts


def offsets(rows, present, share):
    mean = rows[0] * present[0]
    for f in range(1, 6):
        mean = mean + rows[f] * present[f]
    mean = mean * share
    return [(rows[f] - mean) * present[f] for f in range(6)]


def columns(ref, p, rows):
    return jnp.concatenate([ref[2 * p].reshape(rows, 128), ref[2 * p + 1].reshape(rows, 128)], axis=1)


def inner_kernel(q_ref, part_ref, speeds_ref, ext_ref, count_ref, high_ref, low_ref, *refs):
    got, (out_ref, limit_ref, acc_ref, off_ref) = refs[:4], refs[4:]
    coef = coefficients(speeds_ref, 2.0 / 3.0)
    low_half = sublane((8, 128)) < 4

    def finish(p, k, j, s, t):
        acc_ref[p, k, j] = (q_ref[p, k, j] * (1.0 / 3.0) + (2.0 / 3.0) * s) + t

    def pair(p, carry):
        tendency(part_ref, acc_ref, p, coef, finish)
        for n, x in enumerate(bounds(ext_ref, got, p)):
            y = roll(x, 4, 0)
            limit_ref[n, 2 * p] = jnp.where(low_half, x, y)
            limit_ref[n, 2 * p + 1] = jnp.where(low_half, y, x)
        return carry

    lax.fori_loop(0, 3, pair, 0)
    present, share = presence(count_ref)

    def node_pair(k, carry):
        for j in range(4):
            for h in range(2):
                m = 8 * k + 2 * j + h
                rows = to_rows([(acc_ref[p, k, j, 2 * h], acc_ref[p, k, j, 2 * h + 1]) for p in range(3)])
                off = offsets(rows, present, share)
                for f in range(6):
                    out_ref[f, m] = rows[f]
                    off_ref[f, m] = off[f]
        return carry

    lax.fori_loop(0, 4, node_pair, 0)
    high, low = high_ref[...], low_ref[...]
    for p in range(3):
        off_high, off_low = split(columns(off_ref, p, 256))
        fix = jnp.dot(high, off_high, preferred_element_type=jnp.float32)
        fix = fix + jnp.dot(high, off_low, preferred_element_type=jnp.float32)
        fix = fix + jnp.dot(low, off_high, preferred_element_type=jnp.float32)
        for h in range(2):
            f = 2 * p + h
            out_ref[f] = out_ref[f] + fix[:, 128 * h : 128 * h + 128].reshape(32, 8, 128)


def last_kernel(
    base_ref, speeds_ref, limit_ref, corner_ref, weight_ref, count_ref, rim_ref, rim_low_ref, *refs
):
    got, out_hbm, (plane_ref, off_ref, out_ref, sems) = refs[:4], refs[4], refs[5:]

    def part(p):
        at = pl.ds(2 * p, 2)
        return pltpu.make_async_copy(out_ref.at[at], out_hbm.at[at], sems.at[p])

    coef = coefficients(speeds_ref)
    in_y, _ = rim_coefficients(coef[1], 1)
    in_z, _ = rim_coefficients(coef[2], 2)
    high_y, high_z = bit((8, 128), 1), bit((8, 128), 2)
    some_y, some_z = (2.0 / 3.0) * in_y, (2.0 / 3.0) * in_z
    spread_y, spread_z = spread(coef[1], 1), spread(coef[2], 2)
    weight = (2.0 / 3.0) * weight_ref[...]
    present, share = presence(count_ref)

    planes = []
    for p in range(3):
        at = pl.ds(FACE + 2 * p, 2)
        late = weight * jnp.concatenate(
            [outer(get_single(got, "dev", at, h), 1) for h in range(2)], axis=0
        )
        x = with_faces([late[i] for i in range(4)], local(coef[0], 0))
        at_corner = late + jnp.stack(x) + some_y * corner_ref[0, p]
        to_corner = some_z * corner_ref[1, p]
        both = []
        for k in range(4):
            value = some_y * outer(get_face(got, "dev", p, k, 0), 1) + spread_z[k] * late
            if k in (0, 3):
                value = value + jnp.where(high_z == (k == 3), at_corner, 0.0)
            both.append(value)
        for j in range(4):
            value = some_z * outer(get_face(got, "grp", p, j, 0), 2) + spread_y[j] * late
            if j in (0, 3):
                value = value + jnp.where(high_y == (j == 3), to_corner, 0.0)
            both.append(value)
        planes.append(both)
    for t in range(8):
        for h in range(2):
            rows = to_rows([(planes[p][t][2 * h], planes[p][t][2 * h + 1]) for p in range(3)])
            off = offsets(rows, present, share)
            for f in range(6):
                plane_ref[f, 2 * t + h] = rows[f]
                off_ref[f, 2 * t + h] = off[f]

    rim, rim_low = rim_ref[...], rim_low_ref[...]
    for p in range(3):
        off_high, off_low = split(columns(off_ref, p, 128))
        fix = jnp.dot(rim, jnp.concatenate([off_high, off_low], axis=0), preferred_element_type=jnp.float32)
        fix = fix + jnp.dot(rim_low, off_high, preferred_element_type=jnp.float32)
        for g in range(2):
            f = 2 * p + g
            part_fix = fix[:, 128 * g : 128 * g + 128].reshape(4, 4, 2, 8, 128)
            for k in range(4):
                for j in range(4):
                    at = pl.ds(8 * k + 2 * j, 2)
                    value = base_ref[f, at] + part_fix[k, j]
                    if j in (0, 3):
                        value = value + jnp.where(high_y == (j == 3), plane_ref[f, pl.ds(2 * k, 2)], 0.0)
                    if k in (0, 3):
                        value = value + jnp.where(
                            high_z == (k == 3), plane_ref[f, pl.ds(8 + 2 * j, 2)], 0.0
                        )
                    out_ref[f, at] = jnp.minimum(jnp.maximum(value, limit_ref[1, f]), limit_ref[0, f])
        part(p).start()
    for p in range(3):
        part(p).wait()


def call(kernel, outs, args, scratch=(), flops=5_000_000, space=pltpu.VMEM, out_space=pltpu.VMEM):
    return pl.pallas_call(
        kernel,
        out_shape=[jax.ShapeDtypeStruct(*o) for o in outs],
        in_specs=[pl.BlockSpec(memory_space=space)] * len(args),
        out_specs=[pl.BlockSpec(memory_space=out_space)] * len(outs),
        scratch_shapes=[pltpu.VMEM(*s) if isinstance(s, tuple) else s for s in scratch],
        compiler_params=pltpu.CompilerParams(vmem_limit_bytes=LIMIT),
        cost_estimate=pl.CostEstimate(flops=flops, bytes_accessed=2_000_000, transcendentals=0),
    )(*args)


EVEN_PAIRS = [(i, i ^ 1) for i in range(16)]
ODD_PAIRS = [((i + 1) % 16, ((i ^ 1) + 1) % 16) for i in range(16)]


def exchange(messages):
    pairs = (EVEN_PAIRS, ODD_PAIRS)
    return [lax.ppermute(m, axis, pairs[odd]) for m, (axis, odd) in zip(messages, WAYS)]


def shards(fields, speeds, sharpen, mat_count):
    f32, bf16 = jnp.float32, jnp.bfloat16
    rows = fields.reshape(ROW)
    speeds = speeds.reshape(24, 128)
    counts = mat_count.reshape(4, 128)
    node, one, ext = (NODE, f32), ((8, 128), f32), ((2, 3, 8, 128), f32)
    corner = ((2, 3, 4, 8, 128), f32)
    q, s, extremes, counts, speeds, *messages = call(
        open_kernel,
        [node, node, ext, one, ((24, 128), f32)] + [((COEF + 1, 8, 128), f32)] * 4,
        [pltpu.with_memory_space_constraint(x, pltpu.HBM) for x in (rows, speeds, counts)],
        scratch=[(ROW, f32), ((4, 128), jnp.int32), pltpu.SemaphoreType.DMA((5,))],
        space=pltpu.HBM,
    )
    first = exchange(messages)
    square = ((256, 256), bf16)
    base, high, low, rim, rim_low = call(
        local_kernel, [node, square, square, square, ((256, 128), bf16)], [q, s, speeds, sharpen]
    )
    s, corners, weight, *messages = call(
        first_kernel,
        [node, corner, one] + [((FACE + (6 if axis == "dev" else 0), 8, 128), f32) for axis, _ in WAYS],
        [q, base, speeds, *first],
    )
    second = exchange(messages)
    base, limits = call(
        inner_kernel,
        [(ROW, f32), ((2, 6, 8, 128), f32)],
        [q, s, speeds, extremes, counts, high, low, *first],
        scratch=[node, (ROW, f32)],
    )
    plane = ((6, 16, 8, 128), f32)
    (out,) = call(
        last_kernel,
        [(ROW, f32)],
        [base, speeds, limits, corners, weight, counts, rim, rim_low, *second],
        scratch=[plane, plane, (ROW, f32), pltpu.SemaphoreType.DMA((3,))],
        out_space=pltpu.HBM,
    )
    return out.reshape(fields.shape)


def solution(mesh):
    in_specs = (
        P(None, None, "grp", "dev", None),
        P(None, None, "grp", "dev", None),
        P(),
        P("grp", "dev", None),
    )
    out_specs = P(None, None, "grp", "dev", None)
    return jax.shard_map(shards, mesh=mesh, in_specs=in_specs, out_specs=out_specs, check_vma=False)
```

time: 28.1 us -> 27.1 us (0.964)
  waiting for transfers between devices: 1.69 us -> 0.02 us
  Pallas kernels: 5.88 us -> 6.92 us
  starting transfers between devices: 20.3 us -> 20 us
    ppermute x8, waiting for transfers between devices: 1.69 us -> 0.02 us  [exchange(): lax.ppermute(m, axis, pairs[odd])]
    pallas_call x4 -> x5, Pallas kernels: 5.88 us -> 6.92 us  [call(): pl.pallas_call(kernel, out_shape=[jax.ShapeDtypeStruct(*o) for o in outs]...]
    ppermute x8, starting transfers between devices: 20.3 us -> 20 us  [exchange(): lax.ppermute(m, axis, pairs[odd])]
  transfers between devices with their start and end apart: 8 -> 8, of which waited for: 3 -> 0; matrix products, arithmetic and copies ran while one was open for 0% -> 0% of each run, Pallas kernels for 1% -> 11%
where the time goes in v2:
time: 27.1 us; the launch traced here: 27 us
  starting transfers between devices  20 us (74%)
  Pallas kernels  6.92 us (26%)
    ppermute x8, starting transfers between devices, exchange(): lax.ppermute(m, axis, pairs[odd])  20 us
    pallas_call x5, Pallas kernels, call(): pl.pallas_call(kernel, out_shape=[jax.ShapeDtypeStruct(*o) for o in outs]...  6.92 us
  transfers between devices with their start and end apart: 8, of which 0 were waited for; matrix products, arithmetic and copies ran while one was open for 0% of the time, Pallas kernels for 11%

profile of v2, /device:TPU:1, one launch (start us, length us, event | category | flops | bytes accessed | tf_op | source)
XLA Modules:
  0.0 27.0 jit_solution(5743592978645113192)
XLA Ops:
  0.0 0.0 copy-start
  0.0 1.9 %shard_map.46 = (f32[3,4,4,4,8,128]{5,4,3,2,1,0:T(8,128)S(1)}, f32[3,4,4,4,8,128]{5,4,3,2,1,0:T(8,128)S(1)}, f32[2,3,8,128]{3,2,1,0:T(8,128)S(1)}, f32[8,128]{1,...) custom-call(f32[6,32,8,128]{3,2,1,0:T(8,128)} %bitcast.4, ...), custom_call_target="tpu_custom_call" | custom-call | flops 5000000 | bytes 2000000 | tf_op jit(solution)/shard_map/pallas_call | solution.py:550
  2.0 5.8 %collective-permute-start = (f32[52,8,128]{2,1,0:T(8,128)S(1)}, f32[52,8,128]{2,1,0:T(8,128)S(1)}, u32[]{:S(2)}, u32[]{:S(2)}) collective-permute-start(f32[52,8,128]{2,1,0:T(8,128)S(1)} %get-tuple-element.32), channel_id=1, source_target_pairs={{1,2},{2,1},{3,4},{4,3},{5,6},{6,5},{7,8},{8,7},{9,10},{10,9},{11,... | collective-permute-start | bytes 638984 | tf_op jit(solution)/shard_map/ppermute | solution.py:567
  7.8 0.0 collective-permute-start.1
  7.8 2.5 %collective-permute-start.2 = (f32[52,8,128]{2,1,0:T(8,128)S(1)}, f32[52,8,128]{2,1,0:T(8,128)S(1)}, u32[]{:S(2)}, u32[]{:S(2)}) collective-permute-start(f32[52,8,128]{2,1,0:T(8,128)S(1)} %get-tuple-element.34), channel_id=1, source_target_pairs={{16,32},{32,16},{48,64},{64,48},{80,96},{96,80},{112,128},{128,112... | collective-permute-start | bytes 638984 | tf_op jit(solution)/shard_map/ppermute | solution.py:567
  10.3 3.5 %collective-permute-start.3 = (f32[52,8,128]{2,1,0:T(8,128)S(1)}, f32[52,8,128]{2,1,0:T(8,128)S(1)}, u32[]{:S(2)}, u32[]{:S(2)}) collective-permute-start(f32[52,8,128]{2,1,0:T(8,128)S(1)} %get-tuple-element.35), channel_id=1, source_target_pairs={{0,16},{16,0},{32,48},{48,32},{64,80},{80,64},{96,112},{112,96},{1... | collective-permute-start | bytes 638984 | tf_op jit(solution)/shard_map/ppermute | solution.py:567
  13.8 0.0 copy-done
  13.8 1.3 %shard_map.47 = (f32[3,4,4,4,8,128]{5,4,3,2,1,0:T(8,128)S(1)}, bf16[256,256]{1,0:T(8,128)(2,1)S(1)}, bf16[256,256]{1,0:T(8,128)(2,1)S(1)}, bf16[256,256]{1,0:T(8,128)(2,1)S(1)}, bf16[256,128]{1,0:T(8,128)(2,1)S(1)}) custom-call(f32[3,4,4,4,8,128]{5,4,3,2,1,0:T(8,128)S(1)} %get-tuple-element.28.q_ref, ...), custom_call_target="tpu_custom_call" | custom-call | flops 5000000 | bytes 2000000 | tf_op jit(solution)/shard_map/pallas_call | solution.py:550
  15.1 0.0 collective-permute-done.refs_0_
  15.1 0.0 collective-permute-done.1.refs_1_
  15.1 0.0 collective-permute-done.2.refs_2_
  15.1 0.0 collective-permute-done.3.refs_3_
  15.1 0.7 %shard_map.48 = (f32[3,4,4,4,8,128]{5,4,3,2,1,0:T(8,128)S(1)}, f32[2,3,4,8,128]{4,3,2,1,0:T(8,128)S(1)}, f32[8,128]{1,0:T(8,128)S(1)}, f32[30,8,128]{2,1,0:T(8,1...) custom-call(f32[3,4,4,4,8,128]{5,4,3,2,1,0:T(8,128)S(1)} %get-tuple-element.28.q_ref, ...), custom_call_target="tpu_custom_call" | custom-call | flops 5000000 | bytes 2000000 | tf_op jit(solution)/shard_map/pallas_call | solution.py:550
  15.8 2.2 %collective-permute-start.4 = (f32[30,8,128]{2,1,0:T(8,128)S(1)}, f32[30,8,128]{2,1,0:T(8,128)S(1)}, u32[]{:S(2)}, u32[]{:S(2)}) collective-permute-start(f32[30,8,128]{2,1,0:T(8,128)S(1)} %get-tuple-element.47), channel_id=1, source_target_pairs={{1,2},{2,1},{3,4},{4,3},{5,6},{6,5},{7,8},{8,7},{9,10},{10,9},{11,... | collective-permute-start | bytes 368648 | tf_op jit(solution)/shard_map/ppermute | solution.py:567
  18.0 0.0 collective-permute-start.5
  18.0 3.4 %collective-permute-start.6 = (f32[24,8,128]{2,1,0:T(8,128)S(1)}, f32[24,8,128]{2,1,0:T(8,128)S(1)}, u32[]{:S(2)}, u32[]{:S(2)}) collective-permute-start(f32[24,8,128]{2,1,0:T(8,128)S(1)} %get-tuple-element.49), channel_id=1, source_target_pairs={{16,32},{32,16},{48,64},{64,48},{80,96},{96,80},{112,128},{128,112... | collective-permute-start | bytes 294920 | tf_op jit(solution)/shard_map/ppermute | solution.py:567
  21.4 2.6 %collective-permute-start.7 = (f32[24,8,128]{2,1,0:T(8,128)S(1)}, f32[24,8,128]{2,1,0:T(8,128)S(1)}, u32[]{:S(2)}, u32[]{:S(2)}) collective-permute-start(f32[24,8,128]{2,1,0:T(8,128)S(1)} %get-tuple-element.50), channel_id=1, source_target_pairs={{0,16},{16,0},{32,48},{48,32},{64,80},{80,64},{96,112},{112,96},{1... | collective-permute-start | bytes 294920 | tf_op jit(solution)/shard_map/ppermute | solution.py:567
  24.0 1.6 %shard_map.49 = (f32[6,32,8,128]{3,2,1,0:T(8,128)S(1)}, f32[2,6,8,128]{3,2,1,0:T(8,128)S(1)}) custom-call(f32[3,4,4,4,8,128]{5,4,3,2,1,0:T(8,128)S(1)} %get-tuple-element.28.q_ref, f32[3,4,4,4,8,128]{5,4,3,2,1,0:T(8,128)S(1)} %get-tuple-element.36.part_ref, f32[24,128]{1,0:T(8,128)S(1)} %get-tuple-element.30.speeds_ref, ...), custom_call_target="tpu_custom_call" | custom-call | flops 5000000 | bytes 2000000 | tf_op jit(solution)/shard_map/pallas_call | solution.py:550
  25.6 0.0 collective-permute-done.6.refs_2_
  25.6 0.0 collective-permute-done.7.refs_3_
  25.6 0.0 collective-permute-done.4.refs_0_
  25.6 0.0 collective-permute-done.5.refs_1_
  25.6 1.4 %shard_map.50 = f32[6,32,8,128]{3,2,1,0:T(8,128)} custom-call(f32[6,32,8,128]{3,2,1,0:T(8,128)S(1)} %get-tuple-element.41.base_ref, f32[24,128]{1,0:T(8,128)S(1)} %get-tuple-element.30.speeds_ref, f32[2,6,8,128]{3,2,1,0:T(8,128)S(1)} %get-tuple-element.42.limit_ref, f32[2,3,4,8,128]{4,3,2,1,0:T(8,128)S(1)} %get-tuple-element.43.corner_ref, ...), custom_call_target="tpu_custom_call" | custom-call | flops 5000000 | bytes 2000000 | tf_op jit(solution)/shard_map/pallas_call | solution.py:550
Async XLA Ops:
  0.0 13.8 %copy-start = (f32[64,64]{1,0:T(8,128)S(1)}, f32[64,64]{1,0:T(8,128)}, u32[]{:S(2)}) copy-start(f32[64,64]{1,0:T(8,128)} %sharpen_ref.1) | copy-start | bytes 49156
  2.0 13.1 %collective-permute-start = (f32[52,8,128]{2,1,0:T(8,128)S(1)}, f32[52,8,128]{2,1,0:T(8,128)S(1)}, u32[]{:S(2)}, u32[]{:S(2)}) collective-permute-start(f32[52,8,128]{2,1,0:T(8,128)S(1)} %get-tuple-element.32), channel_id=1, source_target_pairs={{1,2},{2,1},{3,4},{4,3},{5,6},{6,5},{7,8},{8,7},{9,10},{10,9},{11,... | collective-permute-start | bytes 638984 | tf_op jit(solution)/shard_map/ppermute | solution.py:567
  7.8 7.3 %collective-permute-start.1 = (f32[52,8,128]{2,1,0:T(8,128)S(1)}, f32[52,8,128]{2,1,0:T(8,128)S(1)}, u32[]{:S(2)}, u32[]{:S(2)}) collective-permute-start(f32[52,8,128]{2,1,0:T(8,128)S(1)} %get-tuple-element.33), channel_id=1, source_target_pairs={{0,1},{1,0},{2,3},{3,2},{4,5},{5,4},{6,7},{7,6},{8,9},{9,8},{10,11... | collective-permute-start | bytes 638984 | tf_op jit(solution)/shard_map/ppermute | solution.py:567
  7.8 7.3 %collective-permute-start.2 = (f32[52,8,128]{2,1,0:T(8,128)S(1)}, f32[52,8,128]{2,1,0:T(8,128)S(1)}, u32[]{:S(2)}, u32[]{:S(2)}) collective-permute-start(f32[52,8,128]{2,1,0:T(8,128)S(1)} %get-tuple-element.34), channel_id=1, source_target_pairs={{16,32},{32,16},{48,64},{64,48},{80,96},{96,80},{112,128},{128,112... | collective-permute-start | bytes 638984 | tf_op jit(solution)/shard_map/ppermute | solution.py:567
  10.3 4.8 %collective-permute-start.3 = (f32[52,8,128]{2,1,0:T(8,128)S(1)}, f32[52,8,128]{2,1,0:T(8,128)S(1)}, u32[]{:S(2)}, u32[]{:S(2)}) collective-permute-start(f32[52,8,128]{2,1,0:T(8,128)S(1)} %get-tuple-element.35), channel_id=1, source_target_pairs={{0,16},{16,0},{32,48},{48,32},{64,80},{80,64},{96,112},{112,96},{1... | collective-permute-start | bytes 638984 | tf_op jit(solution)/shard_map/ppermute | solution.py:567
  15.8 9.8 %collective-permute-start.4 = (f32[30,8,128]{2,1,0:T(8,128)S(1)}, f32[30,8,128]{2,1,0:T(8,128)S(1)}, u32[]{:S(2)}, u32[]{:S(2)}) collective-permute-start(f32[30,8,128]{2,1,0:T(8,128)S(1)} %get-tuple-element.47), channel_id=1, source_target_pairs={{1,2},{2,1},{3,4},{4,3},{5,6},{6,5},{7,8},{8,7},{9,10},{10,9},{11,... | collective-permute-start | bytes 368648 | tf_op jit(solution)/shard_map/ppermute | solution.py:567
  18.0 7.6 %collective-permute-start.5 = (f32[30,8,128]{2,1,0:T(8,128)S(1)}, f32[30,8,128]{2,1,0:T(8,128)S(1)}, u32[]{:S(2)}, u32[]{:S(2)}) collective-permute-start(f32[30,8,128]{2,1,0:T(8,128)S(1)} %get-tuple-element.48), channel_id=1, source_target_pairs={{0,1},{1,0},{2,3},{3,2},{4,5},{5,4},{6,7},{7,6},{8,9},{9,8},{10,11... | collective-permute-start | bytes 368648 | tf_op jit(solution)/shard_map/ppermute | solution.py:567
  18.0 7.6 %collective-permute-start.6 = (f32[24,8,128]{2,1,0:T(8,128)S(1)}, f32[24,8,128]{2,1,0:T(8,128)S(1)}, u32[]{:S(2)}, u32[]{:S(2)}) collective-permute-start(f32[24,8,128]{2,1,0:T(8,128)S(1)} %get-tuple-element.49), channel_id=1, source_target_pairs={{16,32},{32,16},{48,64},{64,48},{80,96},{96,80},{112,128},{128,112... | collective-permute-start | bytes 294920 | tf_op jit(solution)/shard_map/ppermute | solution.py:567
  21.4 4.2 %collective-permute-start.7 = (f32[24,8,128]{2,1,0:T(8,128)S(1)}, f32[24,8,128]{2,1,0:T(8,128)S(1)}, u32[]{:S(2)}, u32[]{:S(2)}) collective-permute-start(f32[24,8,128]{2,1,0:T(8,128)S(1)} %get-tuple-element.50), channel_id=1, source_target_pairs={{0,16},{16,0},{32,48},{48,32},{64,80},{80,64},{96,112},{112,96},{1... | collective-permute-start | bytes 294920 | tf_op jit(solution)/shard_map/ppermute | solution.py:567

commit v3 on v2

--- a/solution.py
+++ b/solution.py
@@ -109,14 +109,27 @@
     return [o0 + t, o + e, o - e, o0 - t]
 
 
-def with_faces(q, coef):
+def beside_faces(q, coef):
     c, low, low_in, high, high_in, step = coef
     axis = q[0].ndim - 2 if step else q[0].ndim - 1
     step = step if step else 1
     r = line(q, c)
-    r[0] = r[0] + (low * q[0] + low_in * roll(q[3], step, axis))
-    r[3] = r[3] + (high * q[3] + high_in * roll(q[0], -step, axis))
+    r[0] = r[0] + low_in * roll(q[3], step, axis)
+    r[3] = r[3] + high_in * roll(q[0], -step, axis)
     return r
+
+
+def with_faces(q, coef):
+    r = beside_faces(q, coef)
+    r[0] = r[0] + coef[1] * q[0]
+    r[3] = r[3] + coef[3] * q[3]
+    return r
+
+
+def own_terms(coef, keep):
+    x, y, z = [[c[1], 0.0, 0.0, c[3]] for c in coef]
+    x = jnp.stack([jnp.broadcast_to(keep + v, (8, 128)) for v in x])
+    return [[x + (y[j] + z[k]) for j in range(4)] for k in range(4)]
 
 
 def beside(low, high, halo_dn, halo_up, step):
@@ -142,36 +155,41 @@
     return roll(m, step, m.ndim - 2) if second else m
 
 
-def tendency(q_ref, acc_ref, p, coef, finish):
-    along_x, along_y, along_z = [local(coef[d], d) for d in range(3)]
+def tendency(q_ref, acc_ref, p, along, own, finish, between=lambda step: None):
     for k in range(4):
-        rx = with_faces([q_ref[p, k, :, i] for i in range(4)], along_x)
+        between(k)
+        rx = beside_faces([q_ref[p, k, :, i] for i in range(4)], along[0])
         for i in range(4):
             acc_ref[p, k, :, i] = rx[i]
-        ry = with_faces([q_ref[p, k, j] for j in range(4)], along_y)
+        ry = beside_faces([q_ref[p, k, j] for j in range(4)], along[1])
         for j in range(4):
             acc_ref[p, k, j] = acc_ref[p, k, j] + ry[j]
     for j in range(4):
         qz = [q_ref[p, k, j] for k in range(4)]
-        rz = with_faces(qz, along_z)
+        rz = beside_faces(qz, along[2])
         for k in range(4):
-            finish(p, k, j, qz[k], acc_ref[p, k, j] + rz[k])
+            finish(p, k, j, acc_ref[p, k, j] + (rz[k] + own[k][j] * qz[k]))
+
+
+def locals_of(coef):
+    return [local(coef[d], d) for d in range(3)]
 
 
 AXES = ("dev", "grp")
-WAYS = (("dev", 1), ("dev", 0), ("grp", 1), ("grp", 0))
+FIRST = (("dev", 1), ("dev", 0), ("grp", 1), ("grp", 0))
+SECOND = (("dev", 1), ("dev", 0), ("grp", 1), ("grp", 0))
 
 
 def put(messages, axis, at, to_next, to_last):
     even = even_device(axis)
-    first, second = [messages[WAYS.index((axis, odd))] for odd in (0, 1)]
+    first, second = messages[axis, 0], messages[axis, 1]
     first[at] = jnp.where(even, to_next, to_last)
     second[at] = jnp.where(even, to_last, to_next)
 
 
 def get(messages, axis, at):
     even = even_device(axis)
-    first, second = [messages[WAYS.index((axis, odd))] for odd in (0, 1)]
+    first, second = messages[axis, 0], messages[axis, 1]
     x, y = first[at], second[at]
     return jnp.where(even, y, x), jnp.where(even, x, y)
 
@@ -207,9 +225,33 @@
     return get_single(messages, axis, at, plane % 2)
 
 
+def along_plane(h, along_x, along_t):
+    out = with_faces(h, along_t)
+    for t in range(4):
+        out[t] = out[t] + jnp.stack(with_faces([h[t][i] for i in range(4)], along_x))
+    return out
+
+
+def across(coef, step):
+    upper = bit((8, 128), step)
+    c = jnp.where(upper, -coef[0], coef[0])
+    out = [c * float(D[0, n]) for n in range(4)]
+    out[0] = out[0] + jnp.where(upper, coef[3], coef[1])
+    return out
+
+
+def put_planes(planes, p, messages, base):
+    for axis in AXES:
+        step = STEP[axis]
+        for half in range(2):
+            a, b = planes[axis][2 * half : 2 * half + 2]
+            at = pl.ds(base + 8 * p + 4 * half, 4)
+            put(messages, axis, at, pack_high(a, b, step), pack_low(a, b, step))
+
+
 def open_kernel(fields_hbm, speeds_hbm, count_hbm, *refs):
-    q_ref, s_ref, ext_ref, wide_count_ref, speeds_ref = refs[:5]
-    messages, (fields_ref, count_ref, sems) = refs[5:9], refs[9:]
+    q_ref, ext_ref, wide_count_ref, speeds_ref = refs[:4]
+    messages, (fields_ref, count_ref, sems) = dict(zip(FIRST, refs[4:8])), refs[8:]
     copies = [
         pltpu.make_async_copy(speeds_hbm, speeds_ref, sems.at[3]),
         pltpu.make_async_copy(count_hbm, count_ref, sems.at[4]),
@@ -237,8 +279,9 @@
             pack_low(pair[0], pair[1], STEP[axis]),
         )
 
-    def finish(p, k, j, q, t):
-        s_ref[p, k, j] = q + t
+    along = locals_of(coef)
+    across_y, across_z = across(coef[1], 1), across(coef[2], 2)
+    high_y, high_z = bit((8, 128), 1), bit((8, 128), 2)
 
     def pair(p, carry):
         part(p).wait()
@@ -268,9 +311,22 @@
                 pack_high(tops[0], bottoms[0], STEP[axis]),
                 pack_low(tops[0], bottoms[0], STEP[axis]),
             )
-        put_faces(q_ref, p, messages, 0)
-        tendency(q_ref, s_ref, p, coef, finish)
-        put_faces(s_ref, p, messages, FACE)
+        ys, zs = [], []
+        for t in range(4):
+            qy, qz = [q_ref[p, t, j] for j in range(4)], [q_ref[p, k, t] for k in range(4)]
+            ys.append([jnp.where(high_y, qy[3 - n], qy[n]) for n in range(4)])
+            zs.append([jnp.where(high_z, qz[3 - n], qz[n]) for n in range(4)])
+        planes = {"dev": [y[0] for y in ys], "grp": [z[0] for z in zs]}
+        put_planes(planes, p, messages, 0)
+        later = {}
+        for axis, lines, ways, other in (("dev", ys, across_y, along[2]), ("grp", zs, across_z, along[1])):
+            tangent = along_plane(planes[axis], along[0], other)
+            later[axis] = []
+            for t in range(4):
+                x = ways[0] * lines[t][0] + ways[1] * lines[t][1]
+                x = x + (ways[2] * lines[t][2] + ways[3] * lines[t][3])
+                later[axis].append(lines[t][0] + (tangent[t] + x))
+        put_planes(later, p, messages, FACE)
         return carry
 
     lax.fori_loop(0, 3, pair, 0)
@@ -301,29 +357,31 @@
     return out
 
 
-def along_plane(h, along_x, along_t):
-    out = with_faces(h, along_t)
-    for t in range(4):
-        out[t] = out[t] + jnp.stack(with_faces([h[t][i] for i in range(4)], along_x))
-    return out
-
-
-def local_kernel(q_ref, part_ref, speeds_ref, sharpen_ref, out_ref, *operators):
-    coef = coefficients(speeds_ref, 0.25)
-    build_operators(sharpen_ref, *operators)
-
-    def finish(p, k, j, s, t):
-        out_ref[p, k, j] = (0.75 * q_ref[p, k, j] + 0.25 * s) + t
+def local_kernel(q_ref, speeds_ref, sharpen_ref, out_ref, both_ref, rim_ref, part_ref):
+    coef = coefficients(speeds_ref)
+    some = coefficients(speeds_ref, 0.25)
+    build_operators(sharpen_ref, both_ref, rim_ref)
+
+    own, own_some = own_terms(coef, 1.0), own_terms(some, 0.25)
+    along, along_some = locals_of(coef), locals_of(some)
+
+    def middle(p, k, j, t):
+        part_ref[p, k, j] = t
+
+    def finish(p, k, j, t):
+        out_ref[p, k, j] = 0.75 * q_ref[p, k, j] + t
 
     def pair(p, carry):
-        tendency(part_ref, out_ref, p, coef, finish)
+        tendency(q_ref, part_ref, p, along, own, middle)
+        tendency(part_ref, out_ref, p, along_some, own_some, finish)
         return carry
 
     lax.fori_loop(0, 3, pair, 0)
 
 
 def first_kernel(q_ref, base_ref, speeds_ref, *refs):
-    got, (out_ref, corner_ref, weight_ref), messages = refs[:4], refs[4:7], refs[7:]
+    got, messages = dict(zip(FIRST, refs[:4])), dict(zip(SECOND, refs[7:]))
+    out_ref, corner_ref, weight_ref = refs[4:7]
     coef = coefficients(speeds_ref)
     in_y, to_y = rim_coefficients(coef[1], 1)
     in_z, to_z = rim_coefficients(coef[2], 2)
@@ -334,7 +392,7 @@
     weight_m = 0.25 * (to_z * in_y + in_ym * to_zn)
     high_y, high_z = bit((8, 128), 1), bit((8, 128), 2)
     some_y, some_z = 0.25 * in_y, 0.25 * in_z
-    along = [local(coef[d], d) for d in range(3)]
+    along = locals_of(coef)
     spread_y, spread_z = spread(coef[1], 1), spread(coef[2], 2)
 
     def pair(p, carry):
@@ -376,7 +434,7 @@
     lax.fori_loop(0, 3, pair, 0)
 
 
-def build_operators(sharpen_ref, high_ref, low_ref, rim_ref, rim_low_ref):
+def build_operators(sharpen_ref, both_ref, rim_ref):
     f32, bf16 = jnp.float32, jnp.bfloat16
 
     def index(shape, axis):
@@ -391,15 +449,13 @@
     pick = (node == jnp.where(col < 64, on_y, on_z)).astype(f32)
     wide = jnp.concatenate([wide, pick], axis=1).astype(bf16)
     same = (index((256, 128), 0) & 3) == (index((256, 128), 1) & 3)
-    for part, ref in zip(split(sharpen_ref[...]), (high_ref, low_ref)):
+    for n, part in enumerate(split(sharpen_ref[...])):
         half = jnp.dot(tall, part, preferred_element_type=f32).astype(bf16)
         full = jnp.dot(half, wide, preferred_element_type=f32)
-        full = [jnp.where(same, full[:, 128 * n : 128 * n + 128], 0.0).astype(bf16) for n in range(3)]
-        ref[...] = jnp.concatenate(full[:2], axis=1)
-        if ref is high_ref:
-            rim_ref[...] = jnp.concatenate([full[2], full[2]], axis=1)
-        else:
-            rim_low_ref[...] = full[2]
+        full = [jnp.where(same, full[:, 128 * m : 128 * m + 128], 0.0).astype(bf16) for m in range(3)]
+        at = pl.ds(256 * n, 256)
+        both_ref[at, :] = jnp.concatenate(full[:2], axis=1)
+        rim_ref[at, :] = jnp.concatenate([full[2], full[2]], axis=1)
 
 
 def split(x):
@@ -433,52 +489,51 @@
     return jnp.concatenate([ref[2 * p].reshape(rows, 128), ref[2 * p + 1].reshape(rows, 128)], axis=1)
 
 
-def inner_kernel(q_ref, part_ref, speeds_ref, ext_ref, count_ref, high_ref, low_ref, *refs):
-    got, (out_ref, limit_ref, acc_ref, off_ref) = refs[:4], refs[4:]
+def inner_kernel(q_ref, part_ref, speeds_ref, ext_ref, count_ref, both_ref, *refs):
+    got, (out_ref, limit_ref, acc_ref, fix_ref) = dict(zip(FIRST, refs[:4])), refs[4:]
     coef = coefficients(speeds_ref, 2.0 / 3.0)
     low_half = sublane((8, 128)) < 4
 
-    def finish(p, k, j, s, t):
-        acc_ref[p, k, j] = (q_ref[p, k, j] * (1.0 / 3.0) + (2.0 / 3.0) * s) + t
-
-    def pair(p, carry):
-        tendency(part_ref, acc_ref, p, coef, finish)
+    own, along = own_terms(coef, 2.0 / 3.0), locals_of(coef)
+
+    def finish(p, k, j, t):
+        acc_ref[p, k, j] = (1.0 / 3.0) * q_ref[p, k, j] + t
+
+    def product(p, step=2):
+        if p < 0 or step != 2:
+            return
+        both = both_ref[...]
+        x_high, x_low = parts[p]
+        fix = jnp.dot(both, x_high, preferred_element_type=jnp.float32)
+        fix = fix[:256] + fix[256:] + jnp.dot(both[:256], x_low, preferred_element_type=jnp.float32)
+        for h in range(2):
+            fix_ref[2 * p + h] = fix[:, 128 * h : 128 * h + 128].reshape(32, 8, 128)
+
+    parts = []
+    for p in range(3):
+        tendency(part_ref, acc_ref, p, along, own, finish, functools.partial(product, p - 1))
+        for n in range(32):
+            k, j, h = n // 8, n // 2 % 4, n % 2
+            rows = to_rows([(acc_ref[p, k, j, 2 * h], acc_ref[p, k, j, 2 * h + 1])])
+            out_ref[2 * p, n], out_ref[2 * p + 1, n] = rows
+        parts.append(split(columns(out_ref, p, 256)))
         for n, x in enumerate(bounds(ext_ref, got, p)):
             y = roll(x, 4, 0)
             limit_ref[n, 2 * p] = jnp.where(low_half, x, y)
             limit_ref[n, 2 * p + 1] = jnp.where(low_half, y, x)
-        return carry
-
-    lax.fori_loop(0, 3, pair, 0)
+    product(2)
     present, share = presence(count_ref)
-
-    def node_pair(k, carry):
-        for j in range(4):
-            for h in range(2):
-                m = 8 * k + 2 * j + h
-                rows = to_rows([(acc_ref[p, k, j, 2 * h], acc_ref[p, k, j, 2 * h + 1]) for p in range(3)])
-                off = offsets(rows, present, share)
-                for f in range(6):
-                    out_ref[f, m] = rows[f]
-                    off_ref[f, m] = off[f]
-        return carry
-
-    lax.fori_loop(0, 4, node_pair, 0)
-    high, low = high_ref[...], low_ref[...]
-    for p in range(3):
-        off_high, off_low = split(columns(off_ref, p, 256))
-        fix = jnp.dot(high, off_high, preferred_element_type=jnp.float32)
-        fix = fix + jnp.dot(high, off_low, preferred_element_type=jnp.float32)
-        fix = fix + jnp.dot(low, off_high, preferred_element_type=jnp.float32)
-        for h in range(2):
-            f = 2 * p + h
-            out_ref[f] = out_ref[f] + fix[:, 128 * h : 128 * h + 128].reshape(32, 8, 128)
+    for n in range(32):
+        off = offsets([fix_ref[f, n] for f in range(6)], present, share)
+        for f in range(6):
+            out_ref[f, n] = out_ref[f, n] + off[f]
 
 
 def last_kernel(
-    base_ref, speeds_ref, limit_ref, corner_ref, weight_ref, count_ref, rim_ref, rim_low_ref, *refs
+    base_ref, speeds_ref, limit_ref, corner_ref, weight_ref, count_ref, rim_ref, *refs
 ):
-    got, out_hbm, (plane_ref, off_ref, out_ref, sems) = refs[:4], refs[4], refs[5:]
+    got, out_hbm = dict(zip(SECOND, refs[:4])), refs[4]
+    plane_ref, off_ref, out_ref, sems = refs[5:]
 
     def part(p):
         at = pl.ds(2 * p, 2)
@@ -522,11 +577,11 @@
                 plane_ref[f, 2 * t + h] = rows[f]
                 off_ref[f, 2 * t + h] = off[f]
 
-    rim, rim_low = rim_ref[...], rim_low_ref[...]
+    rim = rim_ref[...]
     for p in range(3):
         off_high, off_low = split(columns(off_ref, p, 128))
         fix = jnp.dot(rim, jnp.concatenate([off_high, off_low], axis=0), preferred_element_type=jnp.float32)
-        fix = fix + jnp.dot(rim_low, off_high, preferred_element_type=jnp.float32)
+        fix = fix[:256] + fix[256:]
         for g in range(2):
             f = 2 * p + g
             part_fix = fix[:, 128 * g : 128 * g + 128].reshape(4, 4, 2, 8, 128)
@@ -562,9 +617,9 @@
 ODD_PAIRS = [((i + 1) % 16, ((i ^ 1) + 1) % 16) for i in range(16)]
 
 
-def exchange(messages):
+def exchange(messages, ways):
     pairs = (EVEN_PAIRS, ODD_PAIRS)
-    return [lax.ppermute(m, axis, pairs[odd]) for m, (axis, odd) in zip(messages, WAYS)]
+    return [lax.ppermute(m, axis, pairs[odd]) for m, (axis, odd) in zip(messages, ways)]
 
 
 def shards(fields, speeds, sharpen, mat_count):
@@ -574,35 +629,33 @@
     counts = mat_count.reshape(4, 128)
     node, one, ext = (NODE, f32), ((8, 128), f32), ((2, 3, 8, 128), f32)
     corner = ((2, 3, 4, 8, 128), f32)
-    q, s, extremes, counts, speeds, *messages = call(
+    q, extremes, counts, speeds, *messages = call(
         open_kernel,
-        [node, node, ext, one, ((24, 128), f32)] + [((COEF + 1, 8, 128), f32)] * 4,
+        [node, ext, one, ((24, 128), f32)] + [((COEF + 1, 8, 128), f32)] * 4,
         [pltpu.with_memory_space_constraint(x, pltpu.HBM) for x in (rows, speeds, counts)],
         scratch=[(ROW, f32), ((4, 128), jnp.int32), pltpu.SemaphoreType.DMA((5,))],
         space=pltpu.HBM,
     )
-    first = exchange(messages)
-    square = ((256, 256), bf16)
-    base, high, low, rim, rim_low = call(
-        local_kernel, [node, square, square, square, ((256, 128), bf16)], [q, s, speeds, sharpen]
-    )
+    first = exchange(messages, FIRST)
+    tall = ((512, 256), bf16)
+    base, both, rim = call(local_kernel, [node, tall, tall], [q, speeds, sharpen], scratch=[node])
     s, corners, weight, *messages = call(
         first_kernel,
-        [node, corner, one] + [((FACE + (6 if axis == "dev" else 0), 8, 128), f32) for axis, _ in WAYS],
+        [node, corner, one] + [((FACE + (6 if axis == "dev" else 0), 8, 128), f32) for axis, _ in SECOND],
         [q, base, speeds, *first],
     )
-    second = exchange(messages)
+    second = exchange(messages, SECOND)
     base, limits = call(
         inner_kernel,
         [(ROW, f32), ((2, 6, 8, 128), f32)],
-        [q, s, speeds, extremes, counts, high, low, *first],
+        [q, s, speeds, extremes, counts, both, *first],
         scratch=[node, (ROW, f32)],
     )
     plane = ((6, 16, 8, 128), f32)
     (out,) = call(
         last_kernel,
         [(ROW, f32)],
-        [base, speeds, limits, corners, weight, counts, rim, rim_low, *second],
+        [base, speeds, limits, corners, weight, counts, rim, *second],
         scratch=[plane, plane, (ROW, f32), pltpu.SemaphoreType.DMA((3,))],
         out_space=pltpu.HBM,
     )

time: 27.1 us -> 26.6 us (0.982)
  starting transfers between devices: 20 us -> 19.5 us
    ppermute x8, starting transfers between devices: 20 us -> 19.5 us  [exchange(): lax.ppermute(m, axis, pairs[odd])]
  transfers between devices with their start and end apart: 8 -> 8, of which waited for: 0 -> 0; matrix products, arithmetic and copies ran while one was open for 0% -> 0% of each run, Pallas kernels for 11% -> 12%
where the time goes in v3:
time: 26.6 us; the launch traced here: 26.5 us
  starting transfers between devices  19.5 us (73%)
  Pallas kernels  6.87 us (26%)
    ppermute x8, starting transfers between devices, exchange(): lax.ppermute(m, axis, pairs[odd])  19.5 us
    pallas_call x5, Pallas kernels, call(): pl.pallas_call(kernel, out_shape=[jax.ShapeDtypeStruct(*o) for o in outs]...  6.87 us
  transfers between devices with their start and end apart: 8, of which 0 were waited for; matrix products, arithmetic and copies ran while one was open for 0% of the time, Pallas kernels for 12%

profile of v3, /device:TPU:1, one launch (start us, length us, event | category | flops | bytes accessed | tf_op | source)
XLA Modules:
  0.0 26.5 jit_solution(8911047859251578691)
XLA Ops:
  0.0 0.0 copy-start
  0.0 1.7 %shard_map.46 = (f32[3,4,4,4,8,128]{5,4,3,2,1,0:T(8,128)S(1)}, f32[2,3,8,128]{3,2,1,0:T(8,128)S(1)}, f32[8,128]{1,0:T(8,128)S(1)}, f32[24,128]{1,0:T(8,128)S(1)}...) custom-call(f32[6,32,8,128]{3,2,1,0:T(8,128)} %bitcast.4, ...), custom_call_target="tpu_custom_call" | custom-call | flops 5000000 | bytes 2000000 | tf_op jit(solution)/shard_map/pallas_call | solution.py:605
  1.7 5.8 %collective-permute-start = (f32[52,8,128]{2,1,0:T(8,128)S(1)}, f32[52,8,128]{2,1,0:T(8,128)S(1)}, u32[]{:S(2)}, u32[]{:S(2)}) collective-permute-start(f32[52,8,128]{2,1,0:T(8,128)S(1)} %get-tuple-element.28), channel_id=1, source_target_pairs={{1,2},{2,1},{3,4},{4,3},{5,6},{6,5},{7,8},{8,7},{9,10},{10,9},{11,... | collective-permute-start | bytes 638984 | tf_op jit(solution)/shard_map/ppermute | solution.py:622
  7.5 0.0 collective-permute-start.1
  7.5 2.5 %collective-permute-start.2 = (f32[52,8,128]{2,1,0:T(8,128)S(1)}, f32[52,8,128]{2,1,0:T(8,128)S(1)}, u32[]{:S(2)}, u32[]{:S(2)}) collective-permute-start(f32[52,8,128]{2,1,0:T(8,128)S(1)} %get-tuple-element.30), channel_id=1, source_target_pairs={{16,32},{32,16},{48,64},{64,48},{80,96},{96,80},{112,128},{128,112... | collective-permute-start | bytes 638984 | tf_op jit(solution)/shard_map/ppermute | solution.py:622
  10.0 3.5 %collective-permute-start.3 = (f32[52,8,128]{2,1,0:T(8,128)S(1)}, f32[52,8,128]{2,1,0:T(8,128)S(1)}, u32[]{:S(2)}, u32[]{:S(2)}) collective-permute-start(f32[52,8,128]{2,1,0:T(8,128)S(1)} %get-tuple-element.31), channel_id=1, source_target_pairs={{0,16},{16,0},{32,48},{48,32},{64,80},{80,64},{96,112},{112,96},{1... | collective-permute-start | bytes 638984 | tf_op jit(solution)/shard_map/ppermute | solution.py:622
  13.5 0.0 copy-done
  13.5 1.8 %shard_map.47 = (f32[3,4,4,4,8,128]{5,4,3,2,1,0:T(8,128)S(1)}, bf16[512,256]{1,0:T(8,128)(2,1)S(1)}, bf16[512,256]{1,0:T(8,128)(2,1)S(1)}) custom-call(f32[3,4,4,4,8,128]{5,4,3,2,1,0:T(8,128)S(1)} %get-tuple-element.25.q_ref, f32[24,128]{1,0:T(8,128)S(1)} %get-tuple-element.26.speeds_ref, f32[64,64]{1,0:T(8,128)S(1)} %copy-done), custom_call_target="tpu_custom_call" | custom-call | flops 5000000 | bytes 2000000 | tf_op jit(solution)/shard_map/pallas_call | solution.py:605
  15.3 0.0 collective-permute-done.refs_0_
  15.3 0.0 collective-permute-done.1.refs_1_
  15.3 0.0 collective-permute-done.2.refs_2_
  15.3 0.0 collective-permute-done.3.refs_3_
  15.3 0.7 %shard_map.48 = (f32[3,4,4,4,8,128]{5,4,3,2,1,0:T(8,128)S(1)}, f32[2,3,4,8,128]{4,3,2,1,0:T(8,128)S(1)}, f32[8,128]{1,0:T(8,128)S(1)}, f32[30,8,128]{2,1,0:T(8,1...) custom-call(f32[3,4,4,4,8,128]{5,4,3,2,1,0:T(8,128)S(1)} %get-tuple-element.25.q_ref, ...), custom_call_target="tpu_custom_call" | custom-call | flops 5000000 | bytes 2000000 | tf_op jit(solution)/shard_map/pallas_call | solution.py:605
  16.0 1.8 %collective-permute-start.4 = (f32[30,8,128]{2,1,0:T(8,128)S(1)}, f32[30,8,128]{2,1,0:T(8,128)S(1)}, u32[]{:S(2)}, u32[]{:S(2)}) collective-permute-start(f32[30,8,128]{2,1,0:T(8,128)S(1)} %get-tuple-element.41), channel_id=1, source_target_pairs={{1,2},{2,1},{3,4},{4,3},{5,6},{6,5},{7,8},{8,7},{9,10},{10,9},{11,... | collective-permute-start | bytes 368648 | tf_op jit(solution)/shard_map/ppermute | solution.py:622
  17.8 0.0 collective-permute-start.5
  17.8 3.4 %collective-permute-start.6 = (f32[24,8,128]{2,1,0:T(8,128)S(1)}, f32[24,8,128]{2,1,0:T(8,128)S(1)}, u32[]{:S(2)}, u32[]{:S(2)}) collective-permute-start(f32[24,8,128]{2,1,0:T(8,128)S(1)} %get-tuple-element.43), channel_id=1, source_target_pairs={{16,32},{32,16},{48,64},{64,48},{80,96},{96,80},{112,128},{128,112... | collective-permute-start | bytes 294920 | tf_op jit(solution)/shard_map/ppermute | solution.py:622
  21.1 2.6 %collective-permute-start.7 = (f32[24,8,128]{2,1,0:T(8,128)S(1)}, f32[24,8,128]{2,1,0:T(8,128)S(1)}, u32[]{:S(2)}, u32[]{:S(2)}) collective-permute-start(f32[24,8,128]{2,1,0:T(8,128)S(1)} %get-tuple-element.44), channel_id=1, source_target_pairs={{0,16},{16,0},{32,48},{48,32},{64,80},{80,64},{96,112},{112,96},{1... | collective-permute-start | bytes 294920 | tf_op jit(solution)/shard_map/ppermute | solution.py:622
  23.7 1.3 %shard_map.49 = (f32[6,32,8,128]{3,2,1,0:T(8,128)S(1)}, f32[2,6,8,128]{3,2,1,0:T(8,128)S(1)}) custom-call(f32[3,4,4,4,8,128]{5,4,3,2,1,0:T(8,128)S(1)} %get-tuple-element.25.q_ref, f32[3,4,4,4,8,128]{5,4,3,2,1,0:T(8,128)S(1)} %get-tuple-element.32.part_ref, f32[24,128]{1,0:T(8,128)S(1)} %get-tuple-element.26.speeds_ref, ...), custom_call_target="tpu_custom_call" | custom-call | flops 5000000 | bytes 2000000 | tf_op jit(solution)/shard_map/pallas_call | solution.py:605
  25.1 0.0 collective-permute-done.6.refs_2_
  25.1 0.0 collective-permute-done.7.refs_3_
  25.1 0.0 collective-permute-done.4.refs_0_
  25.1 0.0 collective-permute-done.5.refs_1_
  25.1 1.4 %shard_map.50 = f32[6,32,8,128]{3,2,1,0:T(8,128)} custom-call(f32[6,32,8,128]{3,2,1,0:T(8,128)S(1)} %get-tuple-element.36.base_ref, f32[24,128]{1,0:T(8,128)S(1)} %get-tuple-element.26.speeds_ref, f32[2,6,8,128]{3,2,1,0:T(8,128)S(1)} %get-tuple-element.37.limit_ref, f32[2,3,4,8,128]{4,3,2,1,0:T(8,128)S(1)} %get-tuple-element.38.corner_ref, ...), custom_call_target="tpu_custom_call" | custom-call | flops 5000000 | bytes 2000000 | tf_op jit(solution)/shard_map/pallas_call | solution.py:605
Async XLA Ops:
  0.0 13.5 %copy-start = (f32[64,64]{1,0:T(8,128)S(1)}, f32[64,64]{1,0:T(8,128)}, u32[]{:S(2)}) copy-start(f32[64,64]{1,0:T(8,128)} %sharpen_ref.1) | copy-start | bytes 49156
  1.7 13.6 %collective-permute-start = (f32[52,8,128]{2,1,0:T(8,128)S(1)}, f32[52,8,128]{2,1,0:T(8,128)S(1)}, u32[]{:S(2)}, u32[]{:S(2)}) collective-permute-start(f32[52,8,128]{2,1,0:T(8,128)S(1)} %get-tuple-element.28), channel_id=1, source_target_pairs={{1,2},{2,1},{3,4},{4,3},{5,6},{6,5},{7,8},{8,7},{9,10},{10,9},{11,... | collective-permute-start | bytes 638984 | tf_op jit(solution)/shard_map/ppermute | solution.py:622
  7.5 7.8 %collective-permute-start.1 = (f32[52,8,128]{2,1,0:T(8,128)S(1)}, f32[52,8,128]{2,1,0:T(8,128)S(1)}, u32[]{:S(2)}, u32[]{:S(2)}) collective-permute-start(f32[52,8,128]{2,1,0:T(8,128)S(1)} %get-tuple-element.29), channel_id=1, source_target_pairs={{0,1},{1,0},{2,3},{3,2},{4,5},{5,4},{6,7},{7,6},{8,9},{9,8},{10,11... | collective-permute-start | bytes 638984 | tf_op jit(solution)/shard_map/ppermute | solution.py:622
  7.5 7.8 %collective-permute-start.2 = (f32[52,8,128]{2,1,0:T(8,128)S(1)}, f32[52,8,128]{2,1,0:T(8,128)S(1)}, u32[]{:S(2)}, u32[]{:S(2)}) collective-permute-start(f32[52,8,128]{2,1,0:T(8,128)S(1)} %get-tuple-element.30), channel_id=1, source_target_pairs={{16,32},{32,16},{48,64},{64,48},{80,96},{96,80},{112,128},{128,112... | collective-permute-start | bytes 638984 | tf_op jit(solution)/shard_map/ppermute | solution.py:622
  10.0 5.3 %collective-permute-start.3 = (f32[52,8,128]{2,1,0:T(8,128)S(1)}, f32[52,8,128]{2,1,0:T(8,128)S(1)}, u32[]{:S(2)}, u32[]{:S(2)}) collective-permute-start(f32[52,8,128]{2,1,0:T(8,128)S(1)} %get-tuple-element.31), channel_id=1, source_target_pairs={{0,16},{16,0},{32,48},{48,32},{64,80},{80,64},{96,112},{112,96},{1... | collective-permute-start | bytes 638984 | tf_op jit(solution)/shard_map/ppermute | solution.py:622
  16.0 9.1 %collective-permute-start.4 = (f32[30,8,128]{2,1,0:T(8,128)S(1)}, f32[30,8,128]{2,1,0:T(8,128)S(1)}, u32[]{:S(2)}, u32[]{:S(2)}) collective-permute-start(f32[30,8,128]{2,1,0:T(8,128)S(1)} %get-tuple-element.41), channel_id=1, source_target_pairs={{1,2},{2,1},{3,4},{4,3},{5,6},{6,5},{7,8},{8,7},{9,10},{10,9},{11,... | collective-permute-start | bytes 368648 | tf_op jit(solution)/shard_map/ppermute | solution.py:622
  17.8 7.3 %collective-permute-start.5 = (f32[30,8,128]{2,1,0:T(8,128)S(1)}, f32[30,8,128]{2,1,0:T(8,128)S(1)}, u32[]{:S(2)}, u32[]{:S(2)}) collective-permute-start(f32[30,8,128]{2,1,0:T(8,128)S(1)} %get-tuple-element.42), channel_id=1, source_target_pairs={{0,1},{1,0},{2,3},{3,2},{4,5},{5,4},{6,7},{7,6},{8,9},{9,8},{10,11... | collective-permute-start | bytes 368648 | tf_op jit(solution)/shard_map/ppermute | solution.py:622
  17.8 7.3 %collective-permute-start.6 = (f32[24,8,128]{2,1,0:T(8,128)S(1)}, f32[24,8,128]{2,1,0:T(8,128)S(1)}, u32[]{:S(2)}, u32[]{:S(2)}) collective-permute-start(f32[24,8,128]{2,1,0:T(8,128)S(1)} %get-tuple-element.43), channel_id=1, source_target_pairs={{16,32},{32,16},{48,64},{64,48},{80,96},{96,80},{112,128},{128,112... | collective-permute-start | bytes 294920 | tf_op jit(solution)/shard_map/ppermute | solution.py:622
  21.1 4.0 %collective-permute-start.7 = (f32[24,8,128]{2,1,0:T(8,128)S(1)}, f32[24,8,128]{2,1,0:T(8,128)S(1)}, u32[]{:S(2)}, u32[]{:S(2)}) collective-permute-start(f32[24,8,128]{2,1,0:T(8,128)S(1)} %get-tuple-element.44), channel_id=1, source_target_pairs={{0,16},{16,0},{32,48},{48,32},{64,80},{80,64},{96,112},{112,96},{1... | collective-permute-start | bytes 294920 | tf_op jit(solution)/shard_map/ppermute | solution.py:622

commit v4 on v3

--- a/solution.py
+++ b/solution.py
@@ -13,8 +13,8 @@
 NODE = (3, 4, 4, 4, 8, 128)
 ROW = (6, 32, 8, 128)
 FACE = 24
-EXT = 2 * FACE
-COEF = EXT + 3
+COEF = 2 * FACE
+EXT = {"dev": FACE + 6, "grp": FACE}
 STEP = {"dev": 1, "grp": 2}
 LIMIT = 48 * 1024 * 1024
 
@@ -187,17 +187,16 @@
     second[at] = jnp.where(even, to_last, to_next)
 
 
-def get(messages, axis, at):
-    even = even_device(axis)
-    first, second = messages[axis, 0], messages[axis, 1]
-    x, y = first[at], second[at]
-    return jnp.where(even, y, x), jnp.where(even, x, y)
-
-
-def get_single(messages, axis, at, second):
-    last, after = get(messages, axis, at)
-    step = STEP[axis]
-    return unpack_dn(last, second, step), unpack_up(after, second, step)
+def get_outer(messages, axis, at, second):
+    step, even = STEP[axis], even_device(axis)
+    first, other = messages[axis, 0][at], messages[axis, 1][at]
+    upper = bit(first.shape, step)
+    here = upper == even
+    if not second:
+        return jnp.where(here, first, other)
+    there = jnp.where(here, other, first)
+    dim = first.ndim - 2
+    return jnp.where(upper, roll(there, step, dim), roll(there, -step, dim))
 
 
 def face(q_ref, p, axis, side, plane):
@@ -222,7 +221,7 @@
 
 def get_face(messages, axis, p, plane, base):
     at = pl.ds(base + 8 * p + 4 * (plane // 2), 4)
-    return get_single(messages, axis, at, plane % 2)
+    return get_outer(messages, axis, at, plane % 2)
 
 
 def along_plane(h, along_x, along_t):
@@ -250,8 +249,8 @@
 
 
 def open_kernel(fields_hbm, speeds_hbm, count_hbm, *refs):
-    q_ref, ext_ref, wide_count_ref, speeds_ref = refs[:4]
-    messages, (fields_ref, count_ref, sems) = dict(zip(FIRST, refs[4:8])), refs[8:]
+    q_ref, wide_count_ref, speeds_ref = refs[:3]
+    messages, (fields_ref, count_ref, sems) = dict(zip(FIRST, refs[3:7])), refs[7:]
     copies = [
         pltpu.make_async_copy(speeds_hbm, speeds_ref, sems.at[3]),
         pltpu.make_async_copy(count_hbm, count_ref, sems.at[4]),
@@ -285,7 +284,6 @@
 
     def pair(p, carry):
         part(p).wait()
-        tops, bottoms = [], []
         for k in range(4):
             for j in range(4):
                 for h in range(2):
@@ -296,21 +294,6 @@
                     y = jnp.where(low_half, roll(a, 4, 0), b)
                     q_ref[p, k, j, 2 * h] = x
                     q_ref[p, k, j, 2 * h + 1] = y
-                    tops.append(jnp.maximum(x, y))
-                    bottoms.append(jnp.minimum(x, y))
-        while len(tops) > 1:
-            tops = [jnp.maximum(x, y) for x, y in zip(tops[::2], tops[1::2])]
-            bottoms = [jnp.minimum(x, y) for x, y in zip(bottoms[::2], bottoms[1::2])]
-        ext_ref[0, p] = tops[0]
-        ext_ref[1, p] = bottoms[0]
-        for axis in AXES:
-            put(
-                messages,
-                axis,
-                EXT + p,
-                pack_high(tops[0], bottoms[0], STEP[axis]),
-                pack_low(tops[0], bottoms[0], STEP[axis]),
-            )
         ys, zs = [], []
         for t in range(4):
             qy, qz = [q_ref[p, t, j] for j in range(4)], [q_ref[p, k, t] for k in range(4)]
@@ -332,20 +315,14 @@
     lax.fori_loop(0, 3, pair, 0)
 
 
-def bounds(ext_ref, messages, p):
-    top, bottom = ext_ref[0, p], ext_ref[1, p]
-    upper = jnp.maximum(top, jnp.maximum(roll(top, 1, 1), roll(top, -1, 1)))
-    lower = jnp.minimum(bottom, jnp.minimum(roll(bottom, 1, 1), roll(bottom, -1, 1)))
-    for axis in AXES:
-        dn, up = beside(top, top, *get_single(messages, axis, EXT + p, 0), STEP[axis])
-        upper = jnp.maximum(upper, jnp.maximum(dn, up))
-        dn, up = beside(bottom, bottom, *get_single(messages, axis, EXT + p, 1), STEP[axis])
-        lower = jnp.minimum(lower, jnp.minimum(dn, up))
-    return upper, lower
-
-
-def outer(pair, step):
-    return jnp.where(bit(pair[0].shape, step), pair[1], pair[0])
+def bounds(ext_ref, p):
+    out = []
+    for x, most in ((ext_ref[0, p], jnp.maximum), (ext_ref[1, p], jnp.minimum)):
+        y = most(x, most(roll(x, 1, 1), roll(x, -1, 1)))
+        for step in (1, 2):
+            y = most(y, jnp.where(bit(x.shape, step), roll(x, step, 0), roll(x, -step, 0)))
+        out.append(y)
+    return out
 
 
 def spread(coef, step):
@@ -357,7 +334,7 @@
     return out
 
 
-def local_kernel(q_ref, speeds_ref, sharpen_ref, out_ref, both_ref, rim_ref, part_ref):
+def local_kernel(q_ref, speeds_ref, sharpen_ref, out_ref, ext_ref, both_ref, rim_ref, part_ref):
     coef = coefficients(speeds_ref)
     some = coefficients(speeds_ref, 0.25)
     build_operators(sharpen_ref, both_ref, rim_ref)
@@ -372,6 +349,13 @@
         out_ref[p, k, j] = 0.75 * q_ref[p, k, j] + t
 
     def pair(p, carry):
+        tops = [q_ref[p, k] for k in range(4)]
+        bottoms = tops
+        for _ in range(2):
+            tops = [jnp.maximum(x, y) for x, y in zip(tops[::2], tops[1::2])]
+            bottoms = [jnp.minimum(x, y) for x, y in zip(bottoms[::2], bottoms[1::2])]
+        ext_ref[0, p] = jnp.max(tops[0].reshape(16, 8, 128), axis=0)
+        ext_ref[1, p] = jnp.min(bottoms[0].reshape(16, 8, 128), axis=0)
         tendency(q_ref, part_ref, p, along, own, middle)
         tendency(part_ref, out_ref, p, along_some, own_some, finish)
         return carry
@@ -379,14 +363,14 @@
     lax.fori_loop(0, 3, pair, 0)
 
 
-def first_kernel(q_ref, base_ref, speeds_ref, *refs):
+def first_kernel(q_ref, base_ref, speeds_ref, ext_ref, *refs):
     got, messages = dict(zip(FIRST, refs[:4])), dict(zip(SECOND, refs[7:]))
     out_ref, corner_ref, weight_ref = refs[4:7]
     coef = coefficients(speeds_ref)
     in_y, to_y = rim_coefficients(coef[1], 1)
     in_z, to_z = rim_coefficients(coef[2], 2)
-    in_zn, to_zn = [outer(get_single(got, "dev", COEF, h), 1) for h in range(2)]
-    in_ym, to_ym = [outer(get_single(got, "grp", COEF, h), 2) for h in range(2)]
+    in_zn, to_zn = [get_outer(got, "dev", COEF, h) for h in range(2)]
+    in_ym, to_ym = [get_outer(got, "grp", COEF, h) for h in range(2)]
     weight_ref[...] = 0.25 * (in_y * in_zn + in_z * in_ym)
     weight_n = 0.25 * (to_y * in_z + in_zn * to_ym)
     weight_m = 0.25 * (to_z * in_y + in_ym * to_zn)
@@ -396,8 +380,8 @@
     spread_y, spread_z = spread(coef[1], 1), spread(coef[2], 2)
 
     def pair(p, carry):
-        from_n = [outer(get_face(got, "dev", p, k, 0), 1) for k in range(4)]
-        from_m = [outer(get_face(got, "grp", p, j, 0), 2) for j in range(4)]
+        from_n = [get_face(got, "dev", p, k, 0) for k in range(4)]
+        from_m = [get_face(got, "grp", p, j, 0) for j in range(4)]
         edge_n = jnp.where(high_z, from_n[3], from_n[0])
         edge_m = jnp.where(high_y, from_m[3], from_m[0])
         corner_ref[0, p] = weight_n * edge_m
@@ -415,10 +399,10 @@
         plane_z = along_plane(hz, along[0], along[1])
         for n in range(4):
             own = jnp.where(high_y, q_ref[p, n, 3], q_ref[p, n, 0])
-            ghost = outer(get_face(got, "dev", p, n, FACE), 1) + to_y * own
+            ghost = get_face(got, "dev", p, n, FACE) + to_y * own
             plane_y[n] = plane_y[n] + (hy[n] + some_y * ghost)
             own = jnp.where(high_z, q_ref[p, 3, n], q_ref[p, 0, n])
-            ghost = outer(get_face(got, "grp", p, n, FACE), 2) + to_z * own
+            ghost = get_face(got, "grp", p, n, FACE) + to_z * own
             plane_z[n] = plane_z[n] + (hz[n] + some_z * ghost)
         for k in range(4):
             for j in range(4):
@@ -429,6 +413,9 @@
                     value = value + jnp.where(high_z == (k == 3), plane_z[j], 0.0)
                 out_ref[p, k, j] = value
         put_faces(out_ref, p, messages, 0)
+        for axis in AXES:
+            step, pair = STEP[axis], (ext_ref[0, p], ext_ref[1, p])
+            put(messages, axis, EXT[axis] + p, pack_high(*pair, step), pack_low(*pair, step))
         return carry
 
     lax.fori_loop(0, 3, pair, 0)
@@ -489,8 +476,9 @@
     return jnp.concatenate([ref[2 * p].reshape(rows, 128), ref[2 * p + 1].reshape(rows, 128)], axis=1)
 
 
-def inner_kernel(q_ref, part_ref, speeds_ref, ext_ref, count_ref, both_ref, *refs):
-    got, (out_ref, limit_ref, acc_ref, fix_ref) = dict(zip(FIRST, refs[:4])), refs[4:]
+def inner_kernel(
+    q_ref, part_ref, speeds_ref, ext_ref, count_ref, both_ref, out_ref, limit_ref, acc_ref, fix_ref
+):
     coef = coefficients(speeds_ref, 2.0 / 3.0)
     low_half = sublane((8, 128)) < 4
 
@@ -517,10 +505,7 @@
             rows = to_rows([(acc_ref[p, k, j, 2 * h], acc_ref[p, k, j, 2 * h + 1])])
             out_ref[2 * p, n], out_ref[2 * p + 1, n] = rows
         parts.append(split(columns(out_ref, p, 256)))
-        for n, x in enumerate(bounds(ext_ref, got, p)):
-            y = roll(x, 4, 0)
-            limit_ref[n, 2 * p] = jnp.where(low_half, x, y)
-            limit_ref[n, 2 * p + 1] = jnp.where(low_half, y, x)
+        limit_ref[0, p], limit_ref[1, p] = bounds(ext_ref, p)
     product(2)
     present, share = presence(count_ref)
     for n in range(32):
@@ -548,23 +533,29 @@
     weight = (2.0 / 3.0) * weight_ref[...]
     present, share = presence(count_ref)
 
-    planes = []
+    planes, limits = [], []
     for p in range(3):
+        ends = []
+        for n, most in ((0, jnp.maximum), (1, jnp.minimum)):
+            y, z = [get_outer(got, axis, EXT[axis] + p, n) for axis in AXES]
+            x = most(limit_ref[n, p], most(y, z))
+            ends.append(to_rows([(x, x)]))
+        limits += list(zip(*ends))
         at = pl.ds(FACE + 2 * p, 2)
         late = weight * jnp.concatenate(
-            [outer(get_single(got, "dev", at, h), 1) for h in range(2)], axis=0
+            [get_outer(got, "dev", at, h) for h in range(2)], axis=0
         )
         x = with_faces([late[i] for i in range(4)], local(coef[0], 0))
         at_corner = late + jnp.stack(x) + some_y * corner_ref[0, p]
         to_corner = some_z * corner_ref[1, p]
         both = []
         for k in range(4):
-            value = some_y * outer(get_face(got, "dev", p, k, 0), 1) + spread_z[k] * late
+            value = some_y * get_face(got, "dev", p, k, 0) + spread_z[k] * late
             if k in (0, 3):
                 value = value + jnp.where(high_z == (k == 3), at_corner, 0.0)
             both.append(value)
         for j in range(4):
-            value = some_z * outer(get_face(got, "grp", p, j, 0), 2) + spread_y[j] * late
+            value = some_z * get_face(got, "grp", p, j, 0) + spread_y[j] * late
             if j in (0, 3):
                 value = value + jnp.where(high_y == (j == 3), to_corner, 0.0)
             both.append(value)
@@ -595,7 +586,7 @@
                         value = value + jnp.where(
                             high_z == (k == 3), plane_ref[f, pl.ds(8 + 2 * j, 2)], 0.0
                         )
-                    out_ref[f, at] = jnp.minimum(jnp.maximum(value, limit_ref[1, f]), limit_ref[0, f])
+                    out_ref[f, at] = jnp.minimum(jnp.maximum(value, limits[f][1]), limits[f][0])
         part(p).start()
     for p in range(3):
         part(p).wait()
@@ -629,26 +620,28 @@
     counts = mat_count.reshape(4, 128)
     node, one, ext = (NODE, f32), ((8, 128), f32), ((2, 3, 8, 128), f32)
     corner = ((2, 3, 4, 8, 128), f32)
-    q, extremes, counts, speeds, *messages = call(
+    q, counts, speeds, *messages = call(
         open_kernel,
-        [node, ext, one, ((24, 128), f32)] + [((COEF + 1, 8, 128), f32)] * 4,
+        [node, one, ((24, 128), f32)] + [((COEF + 1, 8, 128), f32)] * 4,
         [pltpu.with_memory_space_constraint(x, pltpu.HBM) for x in (rows, speeds, counts)],
         scratch=[(ROW, f32), ((4, 128), jnp.int32), pltpu.SemaphoreType.DMA((5,))],
         space=pltpu.HBM,
     )
     first = exchange(messages, FIRST)
     tall = ((512, 256), bf16)
-    base, both, rim = call(local_kernel, [node, tall, tall], [q, speeds, sharpen], scratch=[node])
+    base, extremes, both, rim = call(
+        local_kernel, [node, ext, tall, tall], [q, speeds, sharpen], scratch=[node]
+    )
     s, corners, weight, *messages = call(
         first_kernel,
-        [node, corner, one] + [((FACE + (6 if axis == "dev" else 0), 8, 128), f32) for axis, _ in SECOND],
-        [q, base, speeds, *first],
+        [node, corner, one] + [((EXT[axis] + 3, 8, 128), f32) for axis, _ in SECOND],
+        [q, base, speeds, extremes, *first],
     )
     second = exchange(messages, SECOND)
     base, limits = call(
         inner_kernel,
-        [(ROW, f32), ((2, 6, 8, 128), f32)],
-        [q, s, speeds, extremes, counts, both, *first],
+        [(ROW, f32), ext],
+        [q, s, speeds, extremes, counts, both],
         scratch=[node, (ROW, f32)],
     )
     plane = ((6, 16, 8, 128), f32)

time: 26.6 us -> 26.3 us (0.989)
  starting transfers between devices: 19.5 us -> 19.1 us
    ppermute x8, starting transfers between devices: 19.5 us -> 19.1 us  [exchange(): lax.ppermute(m, axis, pairs[odd])]
where the time goes in v4:
time: 26.3 us; the launch traced here: 26.2 us
  starting transfers between devices  19.1 us (73%)
  Pallas kernels  6.95 us (26%)
    ppermute x8, starting transfers between devices, exchange(): lax.ppermute(m, axis, pairs[odd])  19.1 us
    pallas_call x5, Pallas kernels, call(): pl.pallas_call(kernel, out_shape=[jax.ShapeDtypeStruct(*o) for o in outs]...  6.95 us
  transfers between devices with their start and end apart: 8, of which 0 were waited for; matrix products, arithmetic and copies ran while one was open for 0% of the time, Pallas kernels for 12%

profile of v4, /device:TPU:1, one launch (start us, length us, event | category | flops | bytes accessed | tf_op | source)
XLA Modules:
  0.0 26.2 jit_solution(6484406375565089825)
XLA Ops:
  0.0 0.0 copy-start
  0.0 1.7 %shard_map.46 = (f32[3,4,4,4,8,128]{5,4,3,2,1,0:T(8,128)S(1)}, f32[8,128]{1,0:T(8,128)S(1)}, f32[24,128]{1,0:T(8,128)S(1)}, f32[49,8,128]{2,1,0:T(8,128)S(1)}, f...) custom-call(f32[6,32,8,128]{3,2,1,0:T(8,128)} %bitcast.4, f32[24,128]{1,0:T(8,128)} %bitcast.5, ...), custom_call_target="tpu_custom_call" | custom-call | flops 5000000 | bytes 2000000 | tf_op jit(solution)/shard_map/pallas_call | solution.py:596
  1.7 5.8 %collective-permute-start = (f32[49,8,128]{2,1,0:T(8,128)S(1)}, f32[49,8,128]{2,1,0:T(8,128)S(1)}, u32[]{:S(2)}, u32[]{:S(2)}) collective-permute-start(f32[49,8,128]{2,1,0:T(8,128)S(1)} %get-tuple-element.29), channel_id=1, source_target_pairs={{1,2},{2,1},{3,4},{4,3},{5,6},{6,5},{7,8},{8,7},{9,10},{10,9},{11,... | collective-permute-start | bytes 602120 | tf_op jit(solution)/shard_map/ppermute | solution.py:613
  7.5 0.0 collective-permute-start.1
  7.5 2.5 %collective-permute-start.2 = (f32[49,8,128]{2,1,0:T(8,128)S(1)}, f32[49,8,128]{2,1,0:T(8,128)S(1)}, u32[]{:S(2)}, u32[]{:S(2)}) collective-permute-start(f32[49,8,128]{2,1,0:T(8,128)S(1)} %get-tuple-element.31), channel_id=1, source_target_pairs={{16,32},{32,16},{48,64},{64,48},{80,96},{96,80},{112,128},{128,112... | collective-permute-start | bytes 602120 | tf_op jit(solution)/shard_map/ppermute | solution.py:613
  10.0 3.5 %collective-permute-start.3 = (f32[49,8,128]{2,1,0:T(8,128)S(1)}, f32[49,8,128]{2,1,0:T(8,128)S(1)}, u32[]{:S(2)}, u32[]{:S(2)}) collective-permute-start(f32[49,8,128]{2,1,0:T(8,128)S(1)} %get-tuple-element.32), channel_id=1, source_target_pairs={{0,16},{16,0},{32,48},{48,32},{64,80},{80,64},{96,112},{112,96},{1... | collective-permute-start | bytes 602120 | tf_op jit(solution)/shard_map/ppermute | solution.py:613
  13.5 0.0 copy-done
  13.5 1.9 %shard_map.47 = (f32[3,4,4,4,8,128]{5,4,3,2,1,0:T(8,128)S(1)}, f32[2,3,8,128]{3,2,1,0:T(8,128)S(1)}, bf16[512,256]{1,0:T(8,128)(2,1)S(1)}, bf16[512,256]{1,0:T(8,128)(2,1)S(1)}) custom-call(f32[3,4,4,4,8,128]{5,4,3,2,1,0:T(8,128)S(1)} %get-tuple-element.25.q_ref, f32[24,128]{1,0:T(8,128)S(1)} %get-tuple-element.26.speeds_ref, f32[64,64]{1,0:T(8,128)S(1)} %copy-done), custom_call_target="tpu_custom_call" | custom-call | flops 5000000 | bytes 2000000 | tf_op jit(solution)/shard_map/pallas_call | solution.py:596
  15.4 0.0 collective-permute-done.refs_0_
  15.4 0.0 collective-permute-done.1.refs_1_
  15.4 0.0 collective-permute-done.2.refs_2_
  15.4 0.0 collective-permute-done.3.refs_3_
  15.4 0.7 %shard_map.48 = (f32[3,4,4,4,8,128]{5,4,3,2,1,0:T(8,128)S(1)}, f32[2,3,4,8,128]{4,3,2,1,0:T(8,128)S(1)}, f32[8,128]{1,0:T(8,128)S(1)}, f32[33,8,128]{2,1,0:T(8,1...) custom-call(f32[3,4,4,4,8,128]{5,4,3,2,1,0:T(8,128)S(1)} %get-tuple-element.25.q_ref, ...), custom_call_target="tpu_custom_call" | custom-call | flops 5000000 | bytes 2000000 | tf_op jit(solution)/shard_map/pallas_call | solution.py:596
  16.1 1.4 %collective-permute-start.4 = (f32[33,8,128]{2,1,0:T(8,128)S(1)}, f32[33,8,128]{2,1,0:T(8,128)S(1)}, u32[]{:S(2)}, u32[]{:S(2)}) collective-permute-start(f32[33,8,128]{2,1,0:T(8,128)S(1)} %get-tuple-element.41), channel_id=1, source_target_pairs={{1,2},{2,1},{3,4},{4,3},{5,6},{6,5},{7,8},{8,7},{9,10},{10,9},{11,... | collective-permute-start | bytes 405512 | tf_op jit(solution)/shard_map/ppermute | solution.py:613
  17.5 0.3 %collective-permute-start.5 = (f32[33,8,128]{2,1,0:T(8,128)S(1)}, f32[33,8,128]{2,1,0:T(8,128)S(1)}, u32[]{:S(2)}, u32[]{:S(2)}) collective-permute-start(f32[33,8,128]{2,1,0:T(8,128)S(1)} %get-tuple-element.42), channel_id=1, source_target_pairs={{0,1},{1,0},{2,3},{3,2},{4,5},{5,4},{6,7},{7,6},{8,9},{9,8},{10,11... | collective-permute-start | bytes 405512 | tf_op jit(solution)/shard_map/ppermute | solution.py:613
  17.8 3.1 %collective-permute-start.6 = (f32[27,8,128]{2,1,0:T(8,128)S(1)}, f32[27,8,128]{2,1,0:T(8,128)S(1)}, u32[]{:S(2)}, u32[]{:S(2)}) collective-permute-start(f32[27,8,128]{2,1,0:T(8,128)S(1)} %get-tuple-element.43), channel_id=1, source_target_pairs={{16,32},{32,16},{48,64},{64,48},{80,96},{96,80},{112,128},{128,112... | collective-permute-start | bytes 331784 | tf_op jit(solution)/shard_map/ppermute | solution.py:613
  20.8 2.6 %collective-permute-start.7 = (f32[27,8,128]{2,1,0:T(8,128)S(1)}, f32[27,8,128]{2,1,0:T(8,128)S(1)}, u32[]{:S(2)}, u32[]{:S(2)}) collective-permute-start(f32[27,8,128]{2,1,0:T(8,128)S(1)} %get-tuple-element.44), channel_id=1, source_target_pairs={{0,16},{16,0},{32,48},{48,32},{64,80},{80,64},{96,112},{112,96},{1... | collective-permute-start | bytes 331784 | tf_op jit(solution)/shard_map/ppermute | solution.py:613
  23.5 1.3 %shard_map.49 = (f32[6,32,8,128]{3,2,1,0:T(8,128)S(1)}, f32[2,3,8,128]{3,2,1,0:T(8,128)S(1)}) custom-call(f32[3,4,4,4,8,128]{5,4,3,2,1,0:T(8,128)S(1)} %get-tuple-element.25.q_ref, f32[3,4,4,4,8,128]{5,4,3,2,1,0:T(8,128)S(1)} %get-tuple-element.33.part_ref, f32[24,128]{1,0:T(8,128)S(1)} %get-tuple-element.26.speeds_ref, ...), custom_call_target="tpu_custom_call" | custom-call | flops 5000000 | bytes 2000000 | tf_op jit(solution)/shard_map/pallas_call | solution.py:596
  24.8 0.0 collective-permute-done.6.refs_2_
  24.8 0.0 collective-permute-done.7.refs_3_
  24.8 0.0 collective-permute-done.4.refs_0_
  24.8 0.0 collective-permute-done.5.refs_1_
  24.8 1.4 %shard_map.50 = f32[6,32,8,128]{3,2,1,0:T(8,128)} custom-call(f32[6,32,8,128]{3,2,1,0:T(8,128)S(1)} %get-tuple-element.36.base_ref, f32[24,128]{1,0:T(8,128)S(1)} %get-tuple-element.26.speeds_ref, f32[2,3,8,128]{3,2,1,0:T(8,128)S(1)} %get-tuple-element.37.limit_ref, f32[2,3,4,8,128]{4,3,2,1,0:T(8,128)S(1)} %get-tuple-element.38.corner_ref, ...), custom_call_target="tpu_custom_call" | custom-call | flops 5000000 | bytes 2000000 | tf_op jit(solution)/shard_map/pallas_call | solution.py:596
Async XLA Ops:
  0.0 13.5 %copy-start = (f32[64,64]{1,0:T(8,128)S(1)}, f32[64,64]{1,0:T(8,128)}, u32[]{:S(2)}) copy-start(f32[64,64]{1,0:T(8,128)} %sharpen_ref.1) | copy-start | bytes 49156
  1.7 13.7 %collective-permute-start = (f32[49,8,128]{2,1,0:T(8,128)S(1)}, f32[49,8,128]{2,1,0:T(8,128)S(1)}, u32[]{:S(2)}, u32[]{:S(2)}) collective-permute-start(f32[49,8,128]{2,1,0:T(8,128)S(1)} %get-tuple-element.29), channel_id=1, source_target_pairs={{1,2},{2,1},{3,4},{4,3},{5,6},{6,5},{7,8},{8,7},{9,10},{10,9},{11,... | collective-permute-start | bytes 602120 | tf_op jit(solution)/shard_map/ppermute | solution.py:613
  7.5 7.9 %collective-permute-start.1 = (f32[49,8,128]{2,1,0:T(8,128)S(1)}, f32[49,8,128]{2,1,0:T(8,128)S(1)}, u32[]{:S(2)}, u32[]{:S(2)}) collective-permute-start(f32[49,8,128]{2,1,0:T(8,128)S(1)} %get-tuple-element.30), channel_id=1, source_target_pairs={{0,1},{1,0},{2,3},{3,2},{4,5},{5,4},{6,7},{7,6},{8,9},{9,8},{10,11... | collective-permute-start | bytes 602120 | tf_op jit(solution)/shard_map/ppermute | solution.py:613
  7.5 7.9 %collective-permute-start.2 = (f32[49,8,128]{2,1,0:T(8,128)S(1)}, f32[49,8,128]{2,1,0:T(8,128)S(1)}, u32[]{:S(2)}, u32[]{:S(2)}) collective-permute-start(f32[49,8,128]{2,1,0:T(8,128)S(1)} %get-tuple-element.31), channel_id=1, source_target_pairs={{16,32},{32,16},{48,64},{64,48},{80,96},{96,80},{112,128},{128,112... | collective-permute-start | bytes 602120 | tf_op jit(solution)/shard_map/ppermute | solution.py:613
  10.0 5.4 %collective-permute-start.3 = (f32[49,8,128]{2,1,0:T(8,128)S(1)}, f32[49,8,128]{2,1,0:T(8,128)S(1)}, u32[]{:S(2)}, u32[]{:S(2)}) collective-permute-start(f32[49,8,128]{2,1,0:T(8,128)S(1)} %get-tuple-element.32), channel_id=1, source_target_pairs={{0,16},{16,0},{32,48},{48,32},{64,80},{80,64},{96,112},{112,96},{1... | collective-permute-start | bytes 602120 | tf_op jit(solution)/shard_map/ppermute | solution.py:613
  16.1 8.7 %collective-permute-start.4 = (f32[33,8,128]{2,1,0:T(8,128)S(1)}, f32[33,8,128]{2,1,0:T(8,128)S(1)}, u32[]{:S(2)}, u32[]{:S(2)}) collective-permute-start(f32[33,8,128]{2,1,0:T(8,128)S(1)} %get-tuple-element.41), channel_id=1, source_target_pairs={{1,2},{2,1},{3,4},{4,3},{5,6},{6,5},{7,8},{8,7},{9,10},{10,9},{11,... | collective-permute-start | bytes 405512 | tf_op jit(solution)/shard_map/ppermute | solution.py:613
  17.5 7.3 %collective-permute-start.5 = (f32[33,8,128]{2,1,0:T(8,128)S(1)}, f32[33,8,128]{2,1,0:T(8,128)S(1)}, u32[]{:S(2)}, u32[]{:S(2)}) collective-permute-start(f32[33,8,128]{2,1,0:T(8,128)S(1)} %get-tuple-element.42), channel_id=1, source_target_pairs={{0,1},{1,0},{2,3},{3,2},{4,5},{5,4},{6,7},{7,6},{8,9},{9,8},{10,11... | collective-permute-start | bytes 405512 | tf_op jit(solution)/shard_map/ppermute | solution.py:613
  17.8 7.0 %collective-permute-start.6 = (f32[27,8,128]{2,1,0:T(8,128)S(1)}, f32[27,8,128]{2,1,0:T(8,128)S(1)}, u32[]{:S(2)}, u32[]{:S(2)}) collective-permute-start(f32[27,8,128]{2,1,0:T(8,128)S(1)} %get-tuple-element.43), channel_id=1, source_target_pairs={{16,32},{32,16},{48,64},{64,48},{80,96},{96,80},{112,128},{128,112... | collective-permute-start | bytes 331784 | tf_op jit(solution)/shard_map/ppermute | solution.py:613
  20.8 3.9 %collective-permute-start.7 = (f32[27,8,128]{2,1,0:T(8,128)S(1)}, f32[27,8,128]{2,1,0:T(8,128)S(1)}, u32[]{:S(2)}, u32[]{:S(2)}) collective-permute-start(f32[27,8,128]{2,1,0:T(8,128)S(1)} %get-tuple-element.44), channel_id=1, source_target_pairs={{0,16},{16,0},{32,48},{48,32},{64,80},{80,64},{96,112},{112,96},{1... | collective-permute-start | bytes 331784 | tf_op jit(solution)/shard_map/ppermute | solution.py:613

commit v5 on v4

--- a/solution.py
+++ b/solution.py
@@ -334,7 +334,7 @@
     return out
 
 
-def local_kernel(q_ref, speeds_ref, sharpen_ref, out_ref, ext_ref, both_ref, rim_ref, part_ref):
+def local_kernel(q_ref, speeds_ref, sharpen_ref, out_ref, ext_ref, limit_ref, both_ref, rim_ref, part_ref):
     coef = coefficients(speeds_ref)
     some = coefficients(speeds_ref, 0.25)
     build_operators(sharpen_ref, both_ref, rim_ref)
@@ -356,6 +356,7 @@
             bottoms = [jnp.minimum(x, y) for x, y in zip(bottoms[::2], bottoms[1::2])]
         ext_ref[0, p] = jnp.max(tops[0].reshape(16, 8, 128), axis=0)
         ext_ref[1, p] = jnp.min(bottoms[0].reshape(16, 8, 128), axis=0)
+        limit_ref[0, p], limit_ref[1, p] = bounds(ext_ref, p)
         tendency(q_ref, part_ref, p, along, own, middle)
         tendency(part_ref, out_ref, p, along_some, own_some, finish)
         return carry
@@ -477,7 +478,7 @@
 
 
 def inner_kernel(
-    q_ref, part_ref, speeds_ref, ext_ref, count_ref, both_ref, out_ref, limit_ref, acc_ref, fix_ref
+    q_ref, part_ref, speeds_ref, count_ref, both_ref, out_ref, acc_ref, fix_ref
 ):
     coef = coefficients(speeds_ref, 2.0 / 3.0)
     low_half = sublane((8, 128)) < 4
@@ -505,7 +506,6 @@
             rows = to_rows([(acc_ref[p, k, j, 2 * h], acc_ref[p, k, j, 2 * h + 1])])
             out_ref[2 * p, n], out_ref[2 * p + 1, n] = rows
         parts.append(split(columns(out_ref, p, 256)))
-        limit_ref[0, p], limit_ref[1, p] = bounds(ext_ref, p)
     product(2)
     present, share = presence(count_ref)
     for n in range(32):
@@ -629,8 +629,8 @@
     )
     first = exchange(messages, FIRST)
     tall = ((512, 256), bf16)
-    base, extremes, both, rim = call(
-        local_kernel, [node, ext, tall, tall], [q, speeds, sharpen], scratch=[node]
+    base, extremes, limits, both, rim = call(
+        local_kernel, [node, ext, ext, tall, tall], [q, speeds, sharpen], scratch=[node]
     )
     s, corners, weight, *messages = call(
         first_kernel,
@@ -638,10 +638,10 @@
         [q, base, speeds, extremes, *first],
     )
     second = exchange(messages, SECOND)
-    base, limits = call(
+    (base,) = call(
         inner_kernel,
-        [(ROW, f32), ext],
-        [q, s, speeds, extremes, counts, both],
+        [(ROW, f32)],
+        [q, s, speeds, counts, both],
         scratch=[node, (ROW, f32)],
     )
     plane = ((6, 16, 8, 128), f32)

time: 26.3 us -> 26.3 us (level)
  no operation moved by 1% of the time
where the time goes in v5:
time: 26.3 us; the launch traced here: 26.2 us
  starting transfers between devices  19.2 us (73%)
  Pallas kernels  6.88 us (26%)
    ppermute x8, starting transfers between devices, exchange(): lax.ppermute(m, axis, pairs[odd])  19.2 us
    pallas_call x5, Pallas kernels, call(): pl.pallas_call(kernel, out_shape=[jax.ShapeDtypeStruct(*o) for o in outs]...  6.88 us
  transfers between devices with their start and end apart: 8, of which 0 were waited for; matrix products, arithmetic and copies ran while one was open for 0% of the time, Pallas kernels for 12%

profile of v5, /device:TPU:1, one launch (start us, length us, event | category | flops | bytes accessed | tf_op | source)
XLA Modules:
  0.0 26.2 jit_solution(12203222820905826793)
XLA Ops:
  0.0 0.0 copy-start
  0.0 1.7 %shard_map.46 = (f32[3,4,4,4,8,128]{5,4,3,2,1,0:T(8,128)S(1)}, f32[8,128]{1,0:T(8,128)S(1)}, f32[24,128]{1,0:T(8,128)S(1)}, f32[49,8,128]{2,1,0:T(8,128)S(1)}, f...) custom-call(f32[6,32,8,128]{3,2,1,0:T(8,128)} %bitcast.4, f32[24,128]{1,0:T(8,128)} %bitcast.5, ...), custom_call_target="tpu_custom_call" | custom-call | flops 5000000 | bytes 2000000 | tf_op jit(solution)/shard_map/pallas_call | solution.py:596
  1.7 5.8 %collective-permute-start = (f32[49,8,128]{2,1,0:T(8,128)S(1)}, f32[49,8,128]{2,1,0:T(8,128)S(1)}, u32[]{:S(2)}, u32[]{:S(2)}) collective-permute-start(f32[49,8,128]{2,1,0:T(8,128)S(1)} %get-tuple-element.28), channel_id=1, source_target_pairs={{1,2},{2,1},{3,4},{4,3},{5,6},{6,5},{7,8},{8,7},{9,10},{10,9},{11,... | collective-permute-start | bytes 602120 | tf_op jit(solution)/shard_map/ppermute | solution.py:613
  7.5 0.0 collective-permute-start.1
  7.5 2.5 %collective-permute-start.2 = (f32[49,8,128]{2,1,0:T(8,128)S(1)}, f32[49,8,128]{2,1,0:T(8,128)S(1)}, u32[]{:S(2)}, u32[]{:S(2)}) collective-permute-start(f32[49,8,128]{2,1,0:T(8,128)S(1)} %get-tuple-element.30), channel_id=1, source_target_pairs={{16,32},{32,16},{48,64},{64,48},{80,96},{96,80},{112,128},{128,112... | collective-permute-start | bytes 602120 | tf_op jit(solution)/shard_map/ppermute | solution.py:613
  10.0 3.5 %collective-permute-start.3 = (f32[49,8,128]{2,1,0:T(8,128)S(1)}, f32[49,8,128]{2,1,0:T(8,128)S(1)}, u32[]{:S(2)}, u32[]{:S(2)}) collective-permute-start(f32[49,8,128]{2,1,0:T(8,128)S(1)} %get-tuple-element.31), channel_id=1, source_target_pairs={{0,16},{16,0},{32,48},{48,32},{64,80},{80,64},{96,112},{112,96},{1... | collective-permute-start | bytes 602120 | tf_op jit(solution)/shard_map/ppermute | solution.py:613
  13.5 0.0 copy-done
  13.5 1.9 %shard_map.47 = (f32[3,4,4,4,8,128]{5,4,3,2,1,0:T(8,128)S(1)}, f32[2,3,8,128]{3,2,1,0:T(8,128)S(1)}, f32[2,3,8,128]{3,2,1,0:T(8,128)S(1)}, bf16[512,256]{1,0:T(8,128)(2,1)S(1)}, bf16[512,256]{1,0:T(8,128)(2,1)S(1)}) custom-call(f32[3,4,4,4,8,128]{5,4,3,2,1,0:T(8,128)S(1)} %get-tuple-element.24.q_ref, f32[24,128]{1,0:T(8,128)S(1)} %get-tuple-element.25.speeds_ref, ...), custom_call_target="tpu_custom_call" | custom-call | flops 5000000 | bytes 2000000 | tf_op jit(solution)/shard_map/pallas_call | solution.py:596
  15.4 0.0 collective-permute-done.refs_0_
  15.4 0.0 collective-permute-done.1.refs_1_
  15.4 0.0 collective-permute-done.2.refs_2_
  15.4 0.0 collective-permute-done.3.refs_3_
  15.4 0.7 %shard_map.48 = (f32[3,4,4,4,8,128]{5,4,3,2,1,0:T(8,128)S(1)}, f32[2,3,4,8,128]{4,3,2,1,0:T(8,128)S(1)}, f32[8,128]{1,0:T(8,128)S(1)}, f32[33,8,128]{2,1,0:T(8,1...) custom-call(f32[3,4,4,4,8,128]{5,4,3,2,1,0:T(8,128)S(1)} %get-tuple-element.24.q_ref, ...), custom_call_target="tpu_custom_call" | custom-call | flops 5000000 | bytes 2000000 | tf_op jit(solution)/shard_map/pallas_call | solution.py:596
  16.1 1.4 %collective-permute-start.4 = (f32[33,8,128]{2,1,0:T(8,128)S(1)}, f32[33,8,128]{2,1,0:T(8,128)S(1)}, u32[]{:S(2)}, u32[]{:S(2)}) collective-permute-start(f32[33,8,128]{2,1,0:T(8,128)S(1)} %get-tuple-element.39), channel_id=1, source_target_pairs={{1,2},{2,1},{3,4},{4,3},{5,6},{6,5},{7,8},{8,7},{9,10},{10,9},{11,... | collective-permute-start | bytes 405512 | tf_op jit(solution)/shard_map/ppermute | solution.py:613
  17.5 0.3 %collective-permute-start.5 = (f32[33,8,128]{2,1,0:T(8,128)S(1)}, f32[33,8,128]{2,1,0:T(8,128)S(1)}, u32[]{:S(2)}, u32[]{:S(2)}) collective-permute-start(f32[33,8,128]{2,1,0:T(8,128)S(1)} %get-tuple-element.40), channel_id=1, source_target_pairs={{0,1},{1,0},{2,3},{3,2},{4,5},{5,4},{6,7},{7,6},{8,9},{9,8},{10,11... | collective-permute-start | bytes 405512 | tf_op jit(solution)/shard_map/ppermute | solution.py:613
  17.7 3.1 %collective-permute-start.6 = (f32[27,8,128]{2,1,0:T(8,128)S(1)}, f32[27,8,128]{2,1,0:T(8,128)S(1)}, u32[]{:S(2)}, u32[]{:S(2)}) collective-permute-start(f32[27,8,128]{2,1,0:T(8,128)S(1)} %get-tuple-element.41), channel_id=1, source_target_pairs={{16,32},{32,16},{48,64},{64,48},{80,96},{96,80},{112,128},{128,112... | collective-permute-start | bytes 331784 | tf_op jit(solution)/shard_map/ppermute | solution.py:613
  20.8 2.6 %collective-permute-start.7 = (f32[27,8,128]{2,1,0:T(8,128)S(1)}, f32[27,8,128]{2,1,0:T(8,128)S(1)}, u32[]{:S(2)}, u32[]{:S(2)}) collective-permute-start(f32[27,8,128]{2,1,0:T(8,128)S(1)} %get-tuple-element.42), channel_id=1, source_target_pairs={{0,16},{16,0},{32,48},{48,32},{64,80},{80,64},{96,112},{112,96},{1... | collective-permute-start | bytes 331784 | tf_op jit(solution)/shard_map/ppermute | solution.py:613
  23.4 1.3 %shard_map.49.base_ref = f32[6,32,8,128]{3,2,1,0:T(8,128)S(1)} custom-call(f32[3,4,4,4,8,128]{5,4,3,2,1,0:T(8,128)S(1)} %get-tuple-element.24.q_ref, f32[3,4,4,4,8,128]{5,4,3,2,1,0:T(8,128)S(1)} %get-tuple-element.32.part_ref, f32[24,128]{1,0:T(8,128)S(1)} %get-tuple-element.25.speeds_ref, f32[8,128]{1,0:T(8,128)S(1)} %get-tuple-element.33.count_ref, ...), custom_call_target="tpu_custom_call" | custom-call | flops 5000000 | bytes 2000000 | tf_op jit(solution)/shard_map/pallas_call | solution.py:596
  24.7 0.0 collective-permute-done.6.refs_2_
  24.7 0.0 collective-permute-done.7.refs_3_
  24.8 0.0 collective-permute-done.4.refs_0_
  24.8 0.0 collective-permute-done.5.refs_1_
  24.8 1.4 %shard_map.50 = f32[6,32,8,128]{3,2,1,0:T(8,128)} custom-call(f32[6,32,8,128]{3,2,1,0:T(8,128)S(1)} %shard_map.49.base_ref, f32[24,128]{1,0:T(8,128)S(1)} %get-tuple-element.25.speeds_ref, f32[2,3,8,128]{3,2,1,0:T(8,128)S(1)} %get-tuple-element.35.limit_ref, f32[2,3,4,8,128]{4,3,2,1,0:T(8,128)S(1)} %get-tuple-element.36.corner_ref, ...), custom_call_target="tpu_custom_call" | custom-call | flops 5000000 | bytes 2000000 | tf_op jit(solution)/shard_map/pallas_call | solution.py:596
Async XLA Ops:
  0.0 13.5 %copy-start = (f32[64,64]{1,0:T(8,128)S(1)}, f32[64,64]{1,0:T(8,128)}, u32[]{:S(2)}) copy-start(f32[64,64]{1,0:T(8,128)} %sharpen_ref.1) | copy-start | bytes 49156
  1.7 13.7 %collective-permute-start = (f32[49,8,128]{2,1,0:T(8,128)S(1)}, f32[49,8,128]{2,1,0:T(8,128)S(1)}, u32[]{:S(2)}, u32[]{:S(2)}) collective-permute-start(f32[49,8,128]{2,1,0:T(8,128)S(1)} %get-tuple-element.28), channel_id=1, source_target_pairs={{1,2},{2,1},{3,4},{4,3},{5,6},{6,5},{7,8},{8,7},{9,10},{10,9},{11,... | collective-permute-start | bytes 602120 | tf_op jit(solution)/shard_map/ppermute | solution.py:613
  7.5 7.9 %collective-permute-start.1 = (f32[49,8,128]{2,1,0:T(8,128)S(1)}, f32[49,8,128]{2,1,0:T(8,128)S(1)}, u32[]{:S(2)}, u32[]{:S(2)}) collective-permute-start(f32[49,8,128]{2,1,0:T(8,128)S(1)} %get-tuple-element.29), channel_id=1, source_target_pairs={{0,1},{1,0},{2,3},{3,2},{4,5},{5,4},{6,7},{7,6},{8,9},{9,8},{10,11... | collective-permute-start | bytes 602120 | tf_op jit(solution)/shard_map/ppermute | solution.py:613
  7.5 7.9 %collective-permute-start.2 = (f32[49,8,128]{2,1,0:T(8,128)S(1)}, f32[49,8,128]{2,1,0:T(8,128)S(1)}, u32[]{:S(2)}, u32[]{:S(2)}) collective-permute-start(f32[49,8,128]{2,1,0:T(8,128)S(1)} %get-tuple-element.30), channel_id=1, source_target_pairs={{16,32},{32,16},{48,64},{64,48},{80,96},{96,80},{112,128},{128,112... | collective-permute-start | bytes 602120 | tf_op jit(solution)/shard_map/ppermute | solution.py:613
  10.0 5.4 %collective-permute-start.3 = (f32[49,8,128]{2,1,0:T(8,128)S(1)}, f32[49,8,128]{2,1,0:T(8,128)S(1)}, u32[]{:S(2)}, u32[]{:S(2)}) collective-permute-start(f32[49,8,128]{2,1,0:T(8,128)S(1)} %get-tuple-element.31), channel_id=1, source_target_pairs={{0,16},{16,0},{32,48},{48,32},{64,80},{80,64},{96,112},{112,96},{1... | collective-permute-start | bytes 602120 | tf_op jit(solution)/shard_map/ppermute | solution.py:613
  16.1 8.7 %collective-permute-start.4 = (f32[33,8,128]{2,1,0:T(8,128)S(1)}, f32[33,8,128]{2,1,0:T(8,128)S(1)}, u32[]{:S(2)}, u32[]{:S(2)}) collective-permute-start(f32[33,8,128]{2,1,0:T(8,128)S(1)} %get-tuple-element.39), channel_id=1, source_target_pairs={{1,2},{2,1},{3,4},{4,3},{5,6},{6,5},{7,8},{8,7},{9,10},{10,9},{11,... | collective-permute-start | bytes 405512 | tf_op jit(solution)/shard_map/ppermute | solution.py:613
  17.5 7.3 %collective-permute-start.5 = (f32[33,8,128]{2,1,0:T(8,128)S(1)}, f32[33,8,128]{2,1,0:T(8,128)S(1)}, u32[]{:S(2)}, u32[]{:S(2)}) collective-permute-start(f32[33,8,128]{2,1,0:T(8,128)S(1)} %get-tuple-element.40), channel_id=1, source_target_pairs={{0,1},{1,0},{2,3},{3,2},{4,5},{5,4},{6,7},{7,6},{8,9},{9,8},{10,11... | collective-permute-start | bytes 405512 | tf_op jit(solution)/shard_map/ppermute | solution.py:613
  17.7 7.0 %collective-permute-start.6 = (f32[27,8,128]{2,1,0:T(8,128)S(1)}, f32[27,8,128]{2,1,0:T(8,128)S(1)}, u32[]{:S(2)}, u32[]{:S(2)}) collective-permute-start(f32[27,8,128]{2,1,0:T(8,128)S(1)} %get-tuple-element.41), channel_id=1, source_target_pairs={{16,32},{32,16},{48,64},{64,48},{80,96},{96,80},{112,128},{128,112... | collective-permute-start | bytes 331784 | tf_op jit(solution)/shard_map/ppermute | solution.py:613
  20.8 3.9 %collective-permute-start.7 = (f32[27,8,128]{2,1,0:T(8,128)S(1)}, f32[27,8,128]{2,1,0:T(8,128)S(1)}, u32[]{:S(2)}, u32[]{:S(2)}) collective-permute-start(f32[27,8,128]{2,1,0:T(8,128)S(1)} %get-tuple-element.42), channel_id=1, source_target_pairs={{0,16},{16,0},{32,48},{48,32},{64,80},{80,64},{96,112},{112,96},{1... | collective-permute-start | bytes 331784 | tf_op jit(solution)/shard_map/ppermute | solution.py:613

commit v6 on v5

--- a/solution.py
+++ b/solution.py
@@ -312,7 +312,8 @@
         put_planes(later, p, messages, FACE)
         return carry
 
-    lax.fori_loop(0, 3, pair, 0)
+    for p in range(3):
+        pair(p, 0)
 
 
 def bounds(ext_ref, p):
@@ -419,7 +420,8 @@
             put(messages, axis, EXT[axis] + p, pack_high(*pair, step), pack_low(*pair, step))
         return carry
 
-    lax.fori_loop(0, 3, pair, 0)
+    for p in range(3):
+        pair(p, 0)
 
 
 def build_operators(sharpen_ref, both_ref, rim_ref):

time: 26.3 us -> 26.3 us (level)
  no operation moved by 1% of the time
where the time goes in v6:
time: 26.3 us; the launch traced here: 26.2 us
  starting transfers between devices  19.2 us (73%)
  Pallas kernels  6.87 us (26%)
    ppermute x8, starting transfers between devices, exchange(): lax.ppermute(m, axis, pairs[odd])  19.2 us
    pallas_call x5, Pallas kernels, call(): pl.pallas_call(kernel, out_shape=[jax.ShapeDtypeStruct(*o) for o in outs]...  6.87 us
  transfers between devices with their start and end apart: 8, of which 0 were waited for; matrix products, arithmetic and copies ran while one was open for 0% of the time, Pallas kernels for 12%

profile of v6, /device:TPU:1, one launch (start us, length us, event | category | flops | bytes accessed | tf_op | source)
XLA Modules:
  0.0 26.2 jit_solution(15204920415379087808)
XLA Ops:
  0.0 0.0 copy-start
  0.0 1.6 %shard_map.46 = (f32[3,4,4,4,8,128]{5,4,3,2,1,0:T(8,128)S(1)}, f32[8,128]{1,0:T(8,128)S(1)}, f32[24,128]{1,0:T(8,128)S(1)}, f32[49,8,128]{2,1,0:T(8,128)S(1)}, f...) custom-call(f32[6,32,8,128]{3,2,1,0:T(8,128)} %bitcast.4, f32[24,128]{1,0:T(8,128)} %bitcast.5, ...), custom_call_target="tpu_custom_call" | custom-call | flops 5000000 | bytes 2000000 | tf_op jit(solution)/shard_map/pallas_call | solution.py:598
  1.7 5.8 %collective-permute-start = (f32[49,8,128]{2,1,0:T(8,128)S(1)}, f32[49,8,128]{2,1,0:T(8,128)S(1)}, u32[]{:S(2)}, u32[]{:S(2)}) collective-permute-start(f32[49,8,128]{2,1,0:T(8,128)S(1)} %get-tuple-element.28), channel_id=1, source_target_pairs={{1,2},{2,1},{3,4},{4,3},{5,6},{6,5},{7,8},{8,7},{9,10},{10,9},{11,... | collective-permute-start | bytes 602120 | tf_op jit(solution)/shard_map/ppermute | solution.py:615
  7.5 0.0 collective-permute-start.1
  7.5 2.5 %collective-permute-start.2 = (f32[49,8,128]{2,1,0:T(8,128)S(1)}, f32[49,8,128]{2,1,0:T(8,128)S(1)}, u32[]{:S(2)}, u32[]{:S(2)}) collective-permute-start(f32[49,8,128]{2,1,0:T(8,128)S(1)} %get-tuple-element.30), channel_id=1, source_target_pairs={{16,32},{32,16},{48,64},{64,48},{80,96},{96,80},{112,128},{128,112... | collective-permute-start | bytes 602120 | tf_op jit(solution)/shard_map/ppermute | solution.py:615
  10.0 3.5 %collective-permute-start.3 = (f32[49,8,128]{2,1,0:T(8,128)S(1)}, f32[49,8,128]{2,1,0:T(8,128)S(1)}, u32[]{:S(2)}, u32[]{:S(2)}) collective-permute-start(f32[49,8,128]{2,1,0:T(8,128)S(1)} %get-tuple-element.31), channel_id=1, source_target_pairs={{0,16},{16,0},{32,48},{48,32},{64,80},{80,64},{96,112},{112,96},{1... | collective-permute-start | bytes 602120 | tf_op jit(solution)/shard_map/ppermute | solution.py:615
  13.5 0.0 copy-done
  13.5 1.9 %shard_map.47 = (f32[3,4,4,4,8,128]{5,4,3,2,1,0:T(8,128)S(1)}, f32[2,3,8,128]{3,2,1,0:T(8,128)S(1)}, f32[2,3,8,128]{3,2,1,0:T(8,128)S(1)}, bf16[512,256]{1,0:T(8,128)(2,1)S(1)}, bf16[512,256]{1,0:T(8,128)(2,1)S(1)}) custom-call(f32[3,4,4,4,8,128]{5,4,3,2,1,0:T(8,128)S(1)} %get-tuple-element.24.q_ref, f32[24,128]{1,0:T(8,128)S(1)} %get-tuple-element.25.speeds_ref, ...), custom_call_target="tpu_custom_call" | custom-call | flops 5000000 | bytes 2000000 | tf_op jit(solution)/shard_map/pallas_call | solution.py:598
  15.4 0.0 collective-permute-done.refs_0_
  15.4 0.0 collective-permute-done.1.refs_1_
  15.4 0.0 collective-permute-done.2.refs_2_
  15.4 0.0 collective-permute-done.3.refs_3_
  15.4 0.7 %shard_map.48 = (f32[3,4,4,4,8,128]{5,4,3,2,1,0:T(8,128)S(1)}, f32[2,3,4,8,128]{4,3,2,1,0:T(8,128)S(1)}, f32[8,128]{1,0:T(8,128)S(1)}, f32[33,8,128]{2,1,0:T(8,1...) custom-call(f32[3,4,4,4,8,128]{5,4,3,2,1,0:T(8,128)S(1)} %get-tuple-element.24.q_ref, ...), custom_call_target="tpu_custom_call" | custom-call | flops 5000000 | bytes 2000000 | tf_op jit(solution)/shard_map/pallas_call | solution.py:598
  16.1 1.4 %collective-permute-start.4 = (f32[33,8,128]{2,1,0:T(8,128)S(1)}, f32[33,8,128]{2,1,0:T(8,128)S(1)}, u32[]{:S(2)}, u32[]{:S(2)}) collective-permute-start(f32[33,8,128]{2,1,0:T(8,128)S(1)} %get-tuple-element.39), channel_id=1, source_target_pairs={{1,2},{2,1},{3,4},{4,3},{5,6},{6,5},{7,8},{8,7},{9,10},{10,9},{11,... | collective-permute-start | bytes 405512 | tf_op jit(solution)/shard_map/ppermute | solution.py:615
  17.5 0.3 %collective-permute-start.5 = (f32[33,8,128]{2,1,0:T(8,128)S(1)}, f32[33,8,128]{2,1,0:T(8,128)S(1)}, u32[]{:S(2)}, u32[]{:S(2)}) collective-permute-start(f32[33,8,128]{2,1,0:T(8,128)S(1)} %get-tuple-element.40), channel_id=1, source_target_pairs={{0,1},{1,0},{2,3},{3,2},{4,5},{5,4},{6,7},{7,6},{8,9},{9,8},{10,11... | collective-permute-start | bytes 405512 | tf_op jit(solution)/shard_map/ppermute | solution.py:615
  17.7 3.1 %collective-permute-start.6 = (f32[27,8,128]{2,1,0:T(8,128)S(1)}, f32[27,8,128]{2,1,0:T(8,128)S(1)}, u32[]{:S(2)}, u32[]{:S(2)}) collective-permute-start(f32[27,8,128]{2,1,0:T(8,128)S(1)} %get-tuple-element.41), channel_id=1, source_target_pairs={{16,32},{32,16},{48,64},{64,48},{80,96},{96,80},{112,128},{128,112... | collective-permute-start | bytes 331784 | tf_op jit(solution)/shard_map/ppermute | solution.py:615
  20.8 2.6 %collective-permute-start.7 = (f32[27,8,128]{2,1,0:T(8,128)S(1)}, f32[27,8,128]{2,1,0:T(8,128)S(1)}, u32[]{:S(2)}, u32[]{:S(2)}) collective-permute-start(f32[27,8,128]{2,1,0:T(8,128)S(1)} %get-tuple-element.42), channel_id=1, source_target_pairs={{0,16},{16,0},{32,48},{48,32},{64,80},{80,64},{96,112},{112,96},{1... | collective-permute-start | bytes 331784 | tf_op jit(solution)/shard_map/ppermute | solution.py:615
  23.4 1.3 %shard_map.49.base_ref = f32[6,32,8,128]{3,2,1,0:T(8,128)S(1)} custom-call(f32[3,4,4,4,8,128]{5,4,3,2,1,0:T(8,128)S(1)} %get-tuple-element.24.q_ref, f32[3,4,4,4,8,128]{5,4,3,2,1,0:T(8,128)S(1)} %get-tuple-element.32.part_ref, f32[24,128]{1,0:T(8,128)S(1)} %get-tuple-element.25.speeds_ref, f32[8,128]{1,0:T(8,128)S(1)} %get-tuple-element.33.count_ref, ...), custom_call_target="tpu_custom_call" | custom-call | flops 5000000 | bytes 2000000 | tf_op jit(solution)/shard_map/pallas_call | solution.py:598
  24.7 0.0 collective-permute-done.6.refs_2_
  24.7 0.0 collective-permute-done.7.refs_3_
  24.7 0.0 collective-permute-done.4.refs_0_
  24.7 0.0 collective-permute-done.5.refs_1_
  24.8 1.4 %shard_map.50 = f32[6,32,8,128]{3,2,1,0:T(8,128)} custom-call(f32[6,32,8,128]{3,2,1,0:T(8,128)S(1)} %shard_map.49.base_ref, f32[24,128]{1,0:T(8,128)S(1)} %get-tuple-element.25.speeds_ref, f32[2,3,8,128]{3,2,1,0:T(8,128)S(1)} %get-tuple-element.35.limit_ref, f32[2,3,4,8,128]{4,3,2,1,0:T(8,128)S(1)} %get-tuple-element.36.corner_ref, ...), custom_call_target="tpu_custom_call" | custom-call | flops 5000000 | bytes 2000000 | tf_op jit(solution)/shard_map/pallas_call | solution.py:598
Async XLA Ops:
  0.0 13.5 %copy-start = (f32[64,64]{1,0:T(8,128)S(1)}, f32[64,64]{1,0:T(8,128)}, u32[]{:S(2)}) copy-start(f32[64,64]{1,0:T(8,128)} %sharpen_ref.1) | copy-start | bytes 49156
  1.7 13.7 %collective-permute-start = (f32[49,8,128]{2,1,0:T(8,128)S(1)}, f32[49,8,128]{2,1,0:T(8,128)S(1)}, u32[]{:S(2)}, u32[]{:S(2)}) collective-permute-start(f32[49,8,128]{2,1,0:T(8,128)S(1)} %get-tuple-element.28), channel_id=1, source_target_pairs={{1,2},{2,1},{3,4},{4,3},{5,6},{6,5},{7,8},{8,7},{9,10},{10,9},{11,... | collective-permute-start | bytes 602120 | tf_op jit(solution)/shard_map/ppermute | solution.py:615
  7.5 7.9 %collective-permute-start.1 = (f32[49,8,128]{2,1,0:T(8,128)S(1)}, f32[49,8,128]{2,1,0:T(8,128)S(1)}, u32[]{:S(2)}, u32[]{:S(2)}) collective-permute-start(f32[49,8,128]{2,1,0:T(8,128)S(1)} %get-tuple-element.29), channel_id=1, source_target_pairs={{0,1},{1,0},{2,3},{3,2},{4,5},{5,4},{6,7},{7,6},{8,9},{9,8},{10,11... | collective-permute-start | bytes 602120 | tf_op jit(solution)/shard_map/ppermute | solution.py:615
  7.5 7.9 %collective-permute-start.2 = (f32[49,8,128]{2,1,0:T(8,128)S(1)}, f32[49,8,128]{2,1,0:T(8,128)S(1)}, u32[]{:S(2)}, u32[]{:S(2)}) collective-permute-start(f32[49,8,128]{2,1,0:T(8,128)S(1)} %get-tuple-element.30), channel_id=1, source_target_pairs={{16,32},{32,16},{48,64},{64,48},{80,96},{96,80},{112,128},{128,112... | collective-permute-start | bytes 602120 | tf_op jit(solution)/shard_map/ppermute | solution.py:615
  10.0 5.4 %collective-permute-start.3 = (f32[49,8,128]{2,1,0:T(8,128)S(1)}, f32[49,8,128]{2,1,0:T(8,128)S(1)}, u32[]{:S(2)}, u32[]{:S(2)}) collective-permute-start(f32[49,8,128]{2,1,0:T(8,128)S(1)} %get-tuple-element.31), channel_id=1, source_target_pairs={{0,16},{16,0},{32,48},{48,32},{64,80},{80,64},{96,112},{112,96},{1... | collective-permute-start | bytes 602120 | tf_op jit(solution)/shard_map/ppermute | solution.py:615
  16.1 8.7 %collective-permute-start.4 = (f32[33,8,128]{2,1,0:T(8,128)S(1)}, f32[33,8,128]{2,1,0:T(8,128)S(1)}, u32[]{:S(2)}, u32[]{:S(2)}) collective-permute-start(f32[33,8,128]{2,1,0:T(8,128)S(1)} %get-tuple-element.39), channel_id=1, source_target_pairs={{1,2},{2,1},{3,4},{4,3},{5,6},{6,5},{7,8},{8,7},{9,10},{10,9},{11,... | collective-permute-start | bytes 405512 | tf_op jit(solution)/shard_map/ppermute | solution.py:615
  17.5 7.3 %collective-permute-start.5 = (f32[33,8,128]{2,1,0:T(8,128)S(1)}, f32[33,8,128]{2,1,0:T(8,128)S(1)}, u32[]{:S(2)}, u32[]{:S(2)}) collective-permute-start(f32[33,8,128]{2,1,0:T(8,128)S(1)} %get-tuple-element.40), channel_id=1, source_target_pairs={{0,1},{1,0},{2,3},{3,2},{4,5},{5,4},{6,7},{7,6},{8,9},{9,8},{10,11... | collective-permute-start | bytes 405512 | tf_op jit(solution)/shard_map/ppermute | solution.py:615
  17.7 7.0 %collective-permute-start.6 = (f32[27,8,128]{2,1,0:T(8,128)S(1)}, f32[27,8,128]{2,1,0:T(8,128)S(1)}, u32[]{:S(2)}, u32[]{:S(2)}) collective-permute-start(f32[27,8,128]{2,1,0:T(8,128)S(1)} %get-tuple-element.41), channel_id=1, source_target_pairs={{16,32},{32,16},{48,64},{64,48},{80,96},{96,80},{112,128},{128,112... | collective-permute-start | bytes 331784 | tf_op jit(solution)/shard_map/ppermute | solution.py:615
  20.8 3.9 %collective-permute-start.7 = (f32[27,8,128]{2,1,0:T(8,128)S(1)}, f32[27,8,128]{2,1,0:T(8,128)S(1)}, u32[]{:S(2)}, u32[]{:S(2)}) collective-permute-start(f32[27,8,128]{2,1,0:T(8,128)S(1)} %get-tuple-element.42), channel_id=1, source_target_pairs={{0,16},{16,0},{32,48},{48,32},{64,80},{80,64},{96,112},{112,96},{1... | collective-permute-start | bytes 331784 | tf_op jit(solution)/shard_map/ppermute | solution.py:615
